TPU v7x, 128 devices: a whole 4x4x4 slice. The times are simulated.
128 devices in a mesh: seq: 16 (over x, z), head: 8 (over y, core).
Axes of the slice: x: 4, y: 4, z: 4, core: 2. Of those that a mesh axis runs over, the one named last changes fastest.
Arguments:
- hidden_states: bfloat16 [65536, 2048], P('seq'), may hold values from -40 to 40
- w_query: bfloat16 [2048, 2048], P('seq', 'head'), may hold values from -1 to 1
- w_key: bfloat16 [2048, 2048], P('seq', 'head'), may hold values from -1 to 1
- w_value: bfloat16 [2048, 2048], P('seq', 'head'), may hold values from -1 to 1
- norm_gain: float32 [2048], P('head'), may hold values from 0.1 to 1.9
Outputs:
- normed_out: bfloat16 [65536, 2048], P('seq', 'head')
All inputs are finite; a program needn't handle non-finite values.
Results may differ from a plain program's by a relative error of at most 0.007.
Values may be sent and summed in bfloat16 or wider, within the bound.
No kernel may reach another device: no remote copies, remote signals or barrier semaphores. Data moves between devices by JAX's collectives and lax.ppermute only.
A program may use at most 128 MiB of HBM per device.

v0:
```python
import jax
import jax.numpy as jnp
import numpy as np
from jax import lax
from jax.experimental import pallas as pl
from jax.experimental.pallas import tpu as pltpu
from jax.sharding import PartitionSpec as P

H = 16
DH = 128
B = 128
D = 2048
HEADS = 2
SIDE = 4
TOKENS = 4096
SCALE = float(DH**-0.5 * np.log2(np.e))
GONE = -1e30
SHIFTS = (1, 3, 2)
BF = jnp.bfloat16
F32 = jnp.float32
TM = 1024
SUB = 256


def line_perm(first, shift):
    pairs = []
    for x in range(SIDE):
        for z in range(SIDE):
            for head in range(8):
                if (head % 2 == 0) == first:
                    target = x * SIDE + (z + shift) % SIDE
                else:
                    target = (x + shift) % SIDE * SIDE + z
                pairs.append(((x * SIDE + z) * 8 + head, target * 8 + head))
    return pairs


def along_line(value, first, shift):
    return lax.ppermute(value, ("seq", "head"), line_perm(first, shift))


def flipped(value, bits):
    return lax.ppermute(value, "seq", [(i, i ^ bits) for i in range(16)])


def other_side(value):
    pairs = [(i, i + 1) for i in range(1, 15, 2)] + [(i + 1, i) for i in range(1, 15, 2)]
    return lax.ppermute(value, "seq", pairs)


def over_heads(value, step):
    return lax.ppermute(value, "head", [(i, step(i)) for i in range(8)])


def dot(a, b):
    return lax.dot_general(a, b, (((1,), (0,)), ((), ())), preferred_element_type=F32)


def dot_t(a, b):
    return lax.dot_general(a, b, (((1,), (1,)), ((), ())), preferred_element_type=F32)


def iota(shape, dim):
    return lax.broadcasted_iota(jnp.int32, shape, dim)


def level_matches(rows, first, levels, row_dim):
    shape = (128, rows) if row_dim == 1 else (rows, rows)
    token, slot = iota(shape, 0), iota(shape, 1)
    found = jnp.zeros(shape, jnp.bool_)
    start = 0
    for level in levels:
        count = 128 >> (level - first + 1)
        found = found | ((slot - start) == (token >> (level - first + 1)))  & (slot >= start) & (
            slot < start + count
        )
        start += count
    return found


def pool_matrix(rows, tokens, levels):
    row, token = iota((rows, tokens), 0), iota((rows, tokens), 1)
    total = jnp.zeros((rows, tokens), F32)
    start = 0
    for level in levels:
        count = tokens >> level
        inside = (row >= start) & (row < start + count) & ((row - start) == (token >> level))
        total = jnp.where(inside, 2.0**-level, total)
        start += count
    return total.astype(BF)


def project_kernel(
    place, h_ref, w0, w1, w2, w3, qkv, l1, l2, l3, l4, q5, q6, q7, send_a, send_b, w_all, p_fine, p_coarse
):
    step = pl.program_id(0)

    @pl.when(step == 0)
    def _():
        for outer, piece in enumerate((w0, w1, w2, w3)):
            for inner in range(SIDE):
                at = pl.multiple_of(place[outer * SIDE + inner] * 128, 128)
                w_all[pl.ds(at, 128), :] = piece[inner]
        p_fine[...] = pool_matrix(112, 128, (1, 2, 3))
        p_coarse[...] = pool_matrix(128, TM, (4, 5, 6, 7))

    @pl.loop(0, TM // SUB)
    def _(part):
        at = pl.multiple_of(part * SUB, SUB)
        rows = dot(h_ref[pl.ds(at, SUB), :], w_all[...]).astype(BF)
        qkv[pl.ds(at, SUB), :] = rows
        for half in range(SUB // 128):
            pooled = dot(p_fine[...], rows[half * 128 : half * 128 + 128]).astype(BF)
            block = part * (SUB // 128) + half
            l1[pl.ds(pl.multiple_of(block * 64, 64), 64), :] = pooled[:64]
            l2[pl.ds(pl.multiple_of(block * 32, 32), 32), :] = pooled[64:96]
            l3[pl.ds(pl.multiple_of(block * 16, 16), 16), :] = pooled[96:112]

    pooled = dot(p_coarse[...], qkv[...])
    mine = pooled.astype(BF)
    l4[...] = mine[:64]
    q5[pl.ds(pl.multiple_of(step * 32, 32), 32), :] = mine[64:96, :256]
    q6[pl.ds(pl.multiple_of(step * 16, 16), 16), :] = mine[96:112, :256]
    q7[pl.ds(pl.multiple_of(step * 8, 8), 8), :] = pooled[112:120, :256]
    send_a[pl.ds(pl.multiple_of(128 + step * 32, 32), 32), :] = mine[64:96, 256:]
    send_a[pl.ds(pl.multiple_of(256 + step * 16, 16), 16), :] = mine[96:112, 256:]
    keep = pooled[112:120, 256:]
    for run in range(TOKENS // TM):

        @pl.when(step == run)
        def _(run=run):
            if run % 2 == 0:
                send_a[320 + run * 8 : 336 + run * 8, :] = jnp.concatenate([keep, keep], 0).astype(BF)
            else:
                before = send_a[312 + run * 8 : 328 + run * 8, :].astype(F32)
                send_a[312 + run * 8 : 328 + run * 8, :] = jnp.concatenate(
                    [before[:8], keep], 0
                ).astype(BF)

    odd = place[16] == 1
    low = (step == 0) & odd
    high = (step == TOKENS // TM - 1) & jnp.logical_not(odd)

    @pl.when(step == 0)
    def _():
        edge = qkv[:128, 256:]

        @pl.when(odd)
        def _():
            send_a[:128, :] = edge

        @pl.when(jnp.logical_not(odd))
        def _():
            send_b[...] = edge

    @pl.when(step == TOKENS // TM - 1)
    def _():
        edge = qkv[TM - 128 :, 256:]

        @pl.when(odd)
        def _():
            send_b[...] = edge

        @pl.when(jnp.logical_not(odd))
        def _():
            send_a[:128, :] = edge


def project(place, hidden, pieces):
    whole = lambda shape: pl.BlockSpec(shape, lambda i, p: (0,) * len(shape))
    tiles = lambda rows, cols: pl.BlockSpec((rows, cols), lambda i, p: (i, 0))
    shape = jax.ShapeDtypeStruct
    return pl.pallas_call(
        project_kernel,
        grid_spec=pltpu.PrefetchScalarGridSpec(
            num_scalar_prefetch=1,
            grid=(TOKENS // TM,),
            in_specs=[tiles(TM, D)] + [whole((SIDE, 128, 768))] * 4,
            out_specs=[
                tiles(TM, 768),
                tiles(TM // 2, 768),
                tiles(TM // 4, 768),
                tiles(TM // 8, 768),
                tiles(TM // 16, 768),
                whole((128, 256)),
                whole((64, 256)),
                whole((32, 256)),
                whole((352, 512)),
                whole((128, 512)),
            ],
            scratch_shapes=[
                pltpu.VMEM((D, 768), BF),
                pltpu.VMEM((112, 128), BF),
                pltpu.VMEM((128, TM), BF),
            ],
        ),
        out_shape=[
            shape((TOKENS, 768), BF),
            shape((TOKENS // 2, 768), BF),
            shape((TOKENS // 4, 768), BF),
            shape((TOKENS // 8, 768), BF),
            shape((TOKENS // 16, 768), BF),
            shape((128, 256), BF),
            shape((64, 256), BF),
            shape((32, 256), F32),
            shape((352, 512), BF),
            shape((128, 512), BF),
        ],
        compiler_params=pltpu.CompilerParams(
            dimension_semantics=("arbitrary",), vmem_limit_bytes=56 * 2**20
        ),
        name="project_and_pool",
        cost_estimate=pl.CostEstimate(
            flops=2 * TOKENS * D * 768, bytes_accessed=26 * 2**20, transcendentals=0
        ),
    )(place, hidden, *pieces)


def with_ones(values):
    return jnp.concatenate([values, jnp.ones_like(values)], axis=1)


def attend(queries, key_rows, values):
    scores = dot_t(queries, key_rows) * SCALE
    highest = jnp.max(scores, axis=1, keepdims=True)
    weights = jnp.exp2(scores - highest).astype(BF)
    both = dot(weights, with_ones(values))
    total = both[:, DH:]
    return (both[:, :DH] / total).astype(BF), highest + jnp.log2(total)


def pairs_kernel(l1, l2, o1, e1, o2, e2):
    for head in range(HEADS):
        q, k, v = (slice(i * 256 + head * 128, i * 256 + head * 128 + 128) for i in range(3))
        c = slice(head * 128, head * 128 + 128)

        for block in range(4):
            mine = slice(block * 128, block * 128 + 128)
            its = slice((block ^ 1) * 128, (block ^ 1) * 128 + 128)
            o1[mine, c], e1[mine, c] = attend(l1[mine, q], l1[its, k], l1[its, v])
        for block in range(2):
            mine = slice(block * 128, block * 128 + 128)
            its = slice((block ^ 1) * 128, (block ^ 1) * 128 + 128)
            o2[mine, c], e2[mine, c] = attend(l2[mine, q], l2[its, k], l2[its, v])


def pairs(l1, l2):
    tiles = lambda rows, cols: pl.BlockSpec((rows, cols), lambda i: (i, 0))
    shape = jax.ShapeDtypeStruct
    return pl.pallas_call(
        pairs_kernel,
        grid=(4,),
        in_specs=[tiles(512, 768), tiles(256, 768)],
        out_specs=[tiles(512, 256), tiles(512, 256), tiles(256, 256), tiles(256, 256)],
        out_shape=[
            shape((2048, 256), BF),
            shape((2048, 256), F32),
            shape((1024, 256), BF),
            shape((1024, 256), F32),
        ],
        compiler_params=pltpu.CompilerParams(vmem_limit_bytes=56 * 2**20),
        name="levels_1_2",
        cost_estimate=pl.CostEstimate(
            flops=2 * 3072 * 128 * 512, bytes_accessed=9 * 2**20, transcendentals=3072 * 256
        ),
    )(l1, l2)


def merged(scores, virtual, found, values, virtual_values):
    ends = jnp.where(iota((128, 128), 0) == iota((128, 128), 1), virtual, 0.0)
    ends = jnp.sum(ends, axis=0, keepdims=True)
    coarse = jnp.where(found, ends, GONE)
    highest = jnp.maximum(
        jnp.max(scores, axis=1, keepdims=True), jnp.max(coarse, axis=1, keepdims=True)
    )
    weights = jnp.exp2(scores - highest).astype(BF)
    coarse_weights = jnp.exp2(coarse - highest).astype(BF)
    both = dot(
        jnp.concatenate([weights, coarse_weights], 1),
        with_ones(jnp.concatenate([values, virtual_values], 0)),
    )
    return both[:, :DH], both[:, DH:], highest


def fine_kernel(
    edge, qkv, l3, l4, q5, q6, q7, got_a, got_b, got_c, got_d, got_e, o1, e1, o2, e2,
    out, squares, o3, e3, kv,
):
    step = pl.program_id(0)
    zero_tail = jnp.zeros((8, DH), BF)
    odd = edge[0] == 1

    @pl.when(step == 0)
    def _():
        kv[128 : 128 + TOKENS, :] = qkv[:, 256:]

        @pl.when(odd)
        def _():
            kv[:128, :] = got_a[:128, :]
            kv[128 + TOKENS :, :] = got_b[...]

        @pl.when(jnp.logical_not(odd))
        def _():
            kv[:128, :] = got_b[...]
            kv[128 + TOKENS :, :] = got_a[:128, :]

        found = level_matches(128, 4, (4, 5, 6, 7), 1)
        for head in range(HEADS):
            q, k, v = (slice(i * 256 + head * 128, i * 256 + head * 128 + 128) for i in range(3))
            c = slice(head * 128, head * 128 + 128)
            gk, gv = c, slice(256 + head * 128, 256 + head * 128 + 128)
            o4, e4 = [], []
            for block in range(2):
                mine = slice(block * 128, block * 128 + 128)
                its = slice((block ^ 1) * 128, (block ^ 1) * 128 + 128)
                o, e = attend(l4[mine, q], l4[its, k], l4[its, v])
                o4 += [o[:64], o[64:]]
                e4 += [e[:64], e[64:]]
            o5, e5 = attend(q5[:, c], got_a[128:256, gk], got_a[128:256, gv])
            o6, e6 = attend(q6[:, c], got_c[:, gk], got_c[:, gv])
            far = jnp.concatenate([got_d[...], got_e[...]], 0)
            o7, e7 = attend(q7[:, c].astype(BF), far[:, gk], far[:, gv])
            for run in range(4):
                its = slice((run ^ 1) * 128, (run ^ 1) * 128 + 128)
                mine = slice(run * 128, run * 128 + 128)
                virtual_values = jnp.concatenate(
                    [
                        o4[run].astype(F32),
                        o5[run * 32 : run * 32 + 32].astype(F32),
                        o6[run * 16 : run * 16 + 16].astype(F32),
                        o7.astype(F32)[run * 8 : run * 8 + 8],
                        jnp.zeros((8, DH), F32),
                    ],
                    0,
                ).astype(BF)
                virtual = jnp.concatenate(
                    [
                        e4[run],
                        e5[run * 32 : run * 32 + 32],
                        e6[run * 16 : run * 16 + 16],
                        e7[run * 8 : run * 8 + 8],
                        jnp.zeros((8, DH), F32),
                    ],
                    0,
                )
                scores = dot_t(l3[mine, q], l3[its, k]) * SCALE
                weighted, total, highest = merged(scores, virtual, found, l3[its, v], virtual_values)
                o3[mine, c] = (weighted / total).astype(BF)
                e3[mine, c] = highest + jnp.log2(total)

    found = level_matches(128, 1, (1, 2, 3), 1)
    first = jnp.where((step == 0) & (edge[1] == 1), GONE, 0.0)
    last = jnp.where((step == TOKENS // TM - 1) & (edge[2] == 1), GONE, 0.0)
    row = iota((8, 128), 0)
    gathered = jnp.zeros((8, 128), F32)
    for block in range(8):
        at = pl.multiple_of(step * TM + block * 128, 128)
        sums = jnp.zeros((128, DH), F32)
        for head in range(HEADS):
            c = slice(head * 128, head * 128 + 128)
            gk, gv = c, slice(256 + head * 128, 256 + head * 128 + 128)
            scores = dot_t(qkv[pl.ds(at, 128), c], kv[pl.ds(at, 384), gk]) * SCALE
            if block == 0:
                scores = scores + jnp.where(iota((1, 384), 1) < 128, first, 0.0)
            if block == 7:
                scores = scores + jnp.where(iota((1, 384), 1) >= 256, last, 0.0)
            b = step * 8 + block
            at1 = pl.ds(pl.multiple_of(b * 64, 64), 64)
            at2 = pl.ds(pl.multiple_of(b * 32, 32), 32)
            at3 = pl.ds(pl.multiple_of(b * 16, 16), 16)
            virtual_values = jnp.concatenate(
                [o1[at1, c], o2[at2, c], o3[at3, c], jnp.zeros((16, DH), BF)], 0
            )
            virtual = jnp.concatenate(
                [e1[at1, c], e2[at2, c], e3[at3, c], jnp.zeros((16, DH), F32)], 0
            )
            weighted, total, _ = merged(scores, virtual, found, kv[pl.ds(at, 384), gv], virtual_values)
            attention = weighted / total
            out[block * 128 : block * 128 + 128, c] = attention
            sums = sums + attention * attention
        token_sums = dot_t(jnp.ones((8, DH), F32), sums)
        gathered = jnp.where(row == block, token_sums, gathered)
    squares[...] = gathered


def fine(edge, *arrays):
    whole = lambda a: pl.BlockSpec(a.shape, lambda i, p: (0,) * a.ndim)
    tiles = lambda rows, cols: pl.BlockSpec((rows, cols), lambda i, p: (i, 0))
    shape = jax.ShapeDtypeStruct
    return pl.pallas_call(
        fine_kernel,
        grid_spec=pltpu.PrefetchScalarGridSpec(
            num_scalar_prefetch=1,
            grid=(TOKENS // TM,),
            in_specs=[whole(a) for a in arrays],
            out_specs=[tiles(TM, 256), tiles(8, 128)],
            scratch_shapes=[
                pltpu.VMEM((512, 256), BF),
                pltpu.VMEM((512, 256), F32),
                pltpu.VMEM((TOKENS + 256, 512), BF),
            ],
        ),
        out_shape=[shape((TOKENS, 256), F32), shape((32, 128), F32)],
        compiler_params=pltpu.CompilerParams(vmem_limit_bytes=56 * 2**20),
        name="merge_levels",
        cost_estimate=pl.CostEstimate(
            flops=4 * TOKENS * 512 * 256, bytes_accessed=18 * 2**20, transcendentals=TOKENS * 1024
        ),
    )(edge, *arrays)


def norm_kernel(attention, s0, s1, s2, s3, gain, out):
    total = s0[...] + s1[...] + s2[...] + s3[...]
    factor = lax.rsqrt(total / D + 1e-6)
    eye = iota((128, 128), 0) == iota((128, 128), 1)
    for block in range(8):
        mine = slice(block * 128, block * 128 + 128)
        column = jnp.sum(jnp.where(eye, factor[block : block + 1], 0.0), axis=1, keepdims=True)
        out[mine, :] = (attention[mine, :] * column * gain[...]).astype(BF)


def norm(attention, sums, gain):
    tiles = lambda rows, cols: pl.BlockSpec((rows, cols), lambda i: (i, 0))
    return pl.pallas_call(
        norm_kernel,
        grid=(TOKENS // TM,),
        in_specs=[tiles(TM, 256)] + [tiles(8, 128)] * 4 + [pl.BlockSpec((1, 256), lambda i: (0, 0))],
        out_specs=tiles(TM, 256),
        out_shape=jax.ShapeDtypeStruct((TOKENS, 256), BF),
        name="norm",
    )(attention, *sums, gain)


def shards(hidden_states, w_query, w_key, w_value, norm_gain):
    position = lax.axis_index("seq")
    core = lax.axis_index("head") % 2
    x, z = position // SIDE, position % SIDE
    w_mine = jnp.concatenate([w_query, w_key, w_value], axis=1)
    line = jnp.stack([w_mine] + [along_line(w_mine, True, s) for s in SHIFTS])
    pieces = [line] + [along_line(line, False, s) for s in SHIFTS]
    back = jnp.array((0,) + SHIFTS, jnp.int32)
    near_x = jnp.where(core == 0, (x - back[:, None]) % SIDE, (x - back[None, :]) % SIDE)
    near_z = jnp.where(core == 0, (z - back[None, :]) % SIDE, (z - back[:, None]) % SIDE)
    place = jnp.concatenate([(near_x * SIDE + near_z).reshape(16), (position % 2).reshape(1)])
    qkv, l1, l2, l3, l4, q5, q6, q7, send_a, send_b = project(place.astype(jnp.int32), hidden_states, pieces)
    got_a = flipped(send_a, 1)
    got_b = other_side(send_b)
    pair_6 = jnp.concatenate([send_a[256:320], got_a[256:320]], 0)
    pair_7 = jnp.concatenate([send_a[320:352], got_a[320:352]], 0)
    got_c = flipped(pair_6, 2)
    got_d = flipped(pair_7, 4)
    got_e = flipped(pair_7, 6)
    o1, e1, o2, e2 = pairs(l1, l2)
    edge = jnp.stack([position % 2, position == 0, position == 15]).astype(jnp.int32)
    attention, squares = fine(
        edge, qkv, l3, l4, q5, q6, q7, got_a, got_b, got_c, got_d, got_e, o1, e1, o2, e2
    )
    chip = squares + over_heads(squares, lambda i: i ^ 1)
    sums = [chip] + [over_heads(chip, lambda i, s=s: (i + 2 * s) % 8) for s in SHIFTS]
    return norm(attention, sums, norm_gain.reshape(1, 256))


def solution(mesh):
    in_specs = (P("seq", None), P("seq", "head"), P("seq", "head"), P("seq", "head"), P("head"))
    return jax.shard_map(
        shards, mesh=mesh, in_specs=in_specs, out_specs=P("seq", "head"), check_vma=False
    )
```

profile of v0, /device:TPU:0, one launch (start us, length us, event | category | flops | bytes accessed | tf_op | source)
XLA Modules:
  0.0 137.1 jit_solution(15600855883309261351)
XLA Ops:
  0.0 0.8 constant_dynamic-update-slice_fusion.2
  0.8 0.8 constant_dynamic-update-slice_fusion.1
  1.7 0.8 constant_dynamic-update-slice_fusion
  2.5 2.0 %collective-permute-start = (bf16[128,768]{1,0:T(8,128)(2,1)S(1)}, bf16[128,768]{1,0:T(8,128)(2,1)S(1)}, u32[]{:S(2)}, u32[]{:S(2)}) collective-permute-start(bf16[128,768]{1,0:T(8,128)(2,1)S(1)} %constant_dynamic-update-slice_fusion), channel_id=1, source_target_pairs={{0,8},{1,33},{2,10},{3,35},{4,12},{5,37},{6,14},{7,39},{8,16},{9,4... | collective-permute-start | bytes 589832 | tf_op jit(solution)/shard_map/ppermute | solution.py:39
  4.5 2.1 %collective-permute-start.1 = (bf16[128,768]{1,0:T(8,128)(2,1)S(1)}, bf16[128,768]{1,0:T(8,128)(2,1)S(1)}, u32[]{:S(2)}, u32[]{:S(2)}) collective-permute-start(bf16[128,768]{1,0:T(8,128)(2,1)S(1)} %constant_dynamic-update-slice_fusion), channel_id=1, source_target_pairs={{0,24},{1,97},{2,26},{3,99},{4,28},{5,101},{6,30},{7,103},{8,0},{9... | collective-permute-start | bytes 589832 | tf_op jit(solution)/shard_map/ppermute | solution.py:39
  6.7 1.9 %collective-permute-start.2 = (bf16[128,768]{1,0:T(8,128)(2,1)S(1)}, bf16[128,768]{1,0:T(8,128)(2,1)S(1)}, u32[]{:S(2)}, u32[]{:S(2)}) collective-permute-start(bf16[128,768]{1,0:T(8,128)(2,1)S(1)} %constant_dynamic-update-slice_fusion), channel_id=1, source_target_pairs={{0,16},{1,65},{2,18},{3,67},{4,20},{5,69},{6,22},{7,71},{8,24},{9,... | collective-permute-start | bytes 589832 | tf_op jit(solution)/shard_map/ppermute | solution.py:39
  8.5 1.8 %collective-permute-done = bf16[128,768]{1,0:T(8,128)(2,1)S(1)} collective-permute-done((bf16[128,768]{1,0:T(8,128)(2,1)S(1)}, bf16[128,768]{1,0:T(8,128)(2,1)S(1)}, u32[]{:S(2)}, u32[]{:S(2)}) %collective-permute-start) | collective-permute-done | bytes 196640 | tf_op jit(solution)/shard_map/ppermute | solution.py:39
  10.3 0.0 collective-permute-done.1
  10.3 3.6 %collective-permute-done.2 = bf16[128,768]{1,0:T(8,128)(2,1)S(1)} collective-permute-done((bf16[128,768]{1,0:T(8,128)(2,1)S(1)}, bf16[128,768]{1,0:T(8,128)(2,1)S(1)}, u32[]{:S(2)}, u32[]{:S(2)}) %collective-permute-start.2) | collective-permute-done | bytes 196640 | tf_op jit(solution)/shard_map/ppermute | solution.py:39
  13.9 0.1 pad_maximum_fusion.w0
  14.0 0.0 copy-start
  14.0 1.6 %collective-permute-start.3 = (bf16[4,128,768]{2,1,0:T(8,128)(2,1)S(1)}, bf16[4,128,768]{2,1,0:T(8,128)(2,1)S(1)}, u32[]{:S(2)}, u32[]{:S(2)}) collective-permute-start(bf16[4,128,768]{2,1,0:T(8,128)(2,1)S(1)} %pad_maximum_fusion.w0), channel_id=1, source_target_pairs={{0,32},{1,9},{2,34},{3,11},{4,36},{5,13},{6,38},{7,15},{8,40},{9,1... | collective-permute-start | bytes 2359304 | tf_op jit(solution)/shard_map/ppermute | solution.py:39
  15.5 1.7 %collective-permute-start.4 = (bf16[4,128,768]{2,1,0:T(8,128)(2,1)S(1)}, bf16[4,128,768]{2,1,0:T(8,128)(2,1)S(1)}, u32[]{:S(2)}, u32[]{:S(2)}) collective-permute-start(bf16[4,128,768]{2,1,0:T(8,128)(2,1)S(1)} %pad_maximum_fusion.w0), channel_id=1, source_target_pairs={{0,96},{1,25},{2,98},{3,27},{4,100},{5,29},{6,102},{7,31},{8,104},... | collective-permute-start | bytes 2359304 | tf_op jit(solution)/shard_map/ppermute | solution.py:39
  17.3 1.8 %collective-permute-start.5 = (bf16[4,128,768]{2,1,0:T(8,128)(2,1)S(1)}, bf16[4,128,768]{2,1,0:T(8,128)(2,1)S(1)}, u32[]{:S(2)}, u32[]{:S(2)}) collective-permute-start(bf16[4,128,768]{2,1,0:T(8,128)(2,1)S(1)} %pad_maximum_fusion.w0), channel_id=1, source_target_pairs={{0,64},{1,17},{2,66},{3,19},{4,68},{5,21},{6,70},{7,23},{8,72},{9,... | collective-permute-start | bytes 2359304 | tf_op jit(solution)/shard_map/ppermute | solution.py:39
  19.1 0.7 and_select_fusion.1
  19.8 0.1 select_add_fusion
  19.8 0.1 add.48
  19.9 0.6 pad_add_fusion.1.place
  20.6 6.7 %collective-permute-done.3.w1 = bf16[4,128,768]{2,1,0:T(8,128)(2,1)S(1)} collective-permute-done((bf16[4,128,768]{2,1,0:T(8,128)(2,1)S(1)}, bf16[4,128,768]{2,1,0:T(8,128)(2,1)S(1)}, u32[]{:S(2)}, u32[]{:S(2)}) %collective-permute-start.3) | collective-permute-done | bytes 786464 | tf_op jit(solution)/shard_map/ppermute | solution.py:39
  27.3 8.0 %collective-permute-done.4.w2 = bf16[4,128,768]{2,1,0:T(8,128)(2,1)S(1)} collective-permute-done((bf16[4,128,768]{2,1,0:T(8,128)(2,1)S(1)}, bf16[4,128,768]{2,1,0:T(8,128)(2,1)S(1)}, u32[]{:S(2)}, u32[]{:S(2)}) %collective-permute-start.4) | collective-permute-done | bytes 786464 | tf_op jit(solution)/shard_map/ppermute | solution.py:39
  35.3 1.4 %collective-permute-done.5.w3 = bf16[4,128,768]{2,1,0:T(8,128)(2,1)S(1)} collective-permute-done((bf16[4,128,768]{2,1,0:T(8,128)(2,1)S(1)}, bf16[4,128,768]{2,1,0:T(8,128)(2,1)S(1)}, u32[]{:S(2)}, u32[]{:S(2)}) %collective-permute-start.5) | collective-permute-done | bytes 786464 | tf_op jit(solution)/shard_map/ppermute | solution.py:39
  36.7 0.0 copy-done
  36.7 0.0 copy-done.10
  36.7 0.0 copy-done.11
  36.7 0.0 copy-start.12
  36.7 0.9 copy-done.12
  37.6 28.9 %project_and_pool.1 = (bf16[4096,768]{1,0:T(8,128)(2,1)}, bf16[2048,768]{1,0:T(8,128)(2,1)}, bf16[1024,768]{1,0:T(8,128)(2,1)}, bf16[512,768]{1,0:T(8,128)(2,1)}...) custom-call(s32[17]{0:T(128)} %pad_add_fusion.1.place, ...), custom_call_target="tpu_custom_call" | custom-call | flops 12884901888 | bytes 27262976 | tf_op jit(solution)/shard_map/project_and_pool/pallas_call | solution.py:173
  66.5 1.5 %collective-permute-start.6 = (bf16[352,512]{1,0:T(8,128)(2,1)}, bf16[352,512]{1,0:T(8,128)(2,1)S(1)}, u32[]{:S(2)}, u32[]{:S(2)}) collective-permute-start(bf16[352,512]{1,0:T(8,128)(2,1)} %get-tuple-element.27), channel_id=1, source_target_pairs={{0,8},{8,0},{16,24},{24,16},{32,40},{40,32},{48,56},{56,48},{64,72... | collective-permute-start | bytes 1081352 | tf_op jit(solution)/shard_map/ppermute | solution.py:43
  68.0 0.8 slice.14
  68.8 0.8 slice.12
  69.6 0.7 collective-permute-start.7
  70.3 4.9 %collective-permute-done.6.got_a = bf16[352,512]{1,0:T(8,128)(2,1)S(1)} collective-permute-done((bf16[352,512]{1,0:T(8,128)(2,1)}, bf16[352,512]{1,0:T(8,128)(2,1)S(1)}, u32[]{:S(2)}, u32[]{:S(2)}) %collective-permute-start.6) | collective-permute-done | bytes 360480 | tf_op jit(solution)/shard_map/ppermute | solution.py:43
  75.3 3.0 %collective-permute-start.10 = (bf16[64,512]{1,0:T(8,128)(2,1)S(1)}, bf16[64,512]{1,0:T(8,128)(2,1)S(1)}, u32[]{:S(2)}, u32[]{:S(2)}) collective-permute-start(bf16[64,512]{1,0:T(8,128)(2,1)S(1)} %pad_maximum_fusion.2), channel_id=1, source_target_pairs={{0,48},{8,56},{16,32},{24,40},{32,16},{40,24},{48,0},{56,8},{64,11... | collective-permute-start | bytes 196616 | tf_op jit(solution)/shard_map/ppermute | solution.py:43
  78.3 0.9 collective-permute-start.9
  79.3 1.2 collective-permute-start.8
  80.4 0.7 pad_add_fusion.edge
  81.1 13.9 %levels_1_2.1 = (bf16[2048,256]{1,0:T(8,128)(2,1)}, f32[2048,256]{1,0:T(8,128)}, bf16[1024,256]{1,0:T(8,128)(2,1)}, f32[1024,256]{1,0:T(8,128)}) custom-call(bf16[2048,768]{1,0:T(8,128)(2,1)} %get-tuple-element.29.l1, bf16[1024,768]{1,0:T(8,128)(2,1)} %get-tuple-element.30.l2), custom_call_target="tpu_custom_call" | custom-call | flops 402653184 | bytes 9437184 | tf_op jit(solution)/shard_map/levels_1_2/pallas_call | solution.py:250
  95.0 0.0 collective-permute-done.7.got_b
  95.0 0.0 copy-start.2
  95.0 0.0 collective-permute-done.10.got_e
  95.0 0.0 copy-start.4
  95.0 0.0 collective-permute-done.9.got_d
  95.1 0.0 copy-start.5
  95.1 0.0 collective-permute-done.8.got_c
  95.1 0.0 copy-start.3
  95.1 0.0 copy-done.1
  95.1 0.6 copy-done.2
  95.7 0.0 copy-done.4
  95.7 0.0 copy-done.5
  95.7 0.0 copy-done.3
  95.8 25.5 %merge_levels.1 = (f32[4096,256]{1,0:T(8,128)}, f32[32,128]{1,0:T(8,128)}) custom-call(s32[3]{0:T(128)} %pad_add_fusion.edge, bf16[4096,768]{1,0:T(8,128)(2,1)} %get-tuple-element.21.qkv, bf16[512,768]{1,0:T(8,128)(2,1)} %get-tuple-element.22.l3, bf16[256,768]{1,0:T(8,128)(2,1)} %get-tuple-element.23.l4, bf16[128,256]{1,0:T(8,128)(2,1)} %get-tuple-element.24.q5, ...), custom_call_target="tpu_custom_call" | custom-call | flops 2147483648 | bytes 18874368 | tf_op jit(solution)/shard_map/merge_levels/pallas_call | solution.py:390
  121.2 0.0 collective-permute-start.11
  121.3 1.4 %collective-permute-done.11 = f32[32,128]{1,0:T(8,128)S(1)} collective-permute-done((f32[32,128]{1,0:T(8,128)}, f32[32,128]{1,0:T(8,128)S(1)}, u32[]{:S(2)}, u32[]{:S(2)}) %collective-permute-start.11) | collective-permute-done | bytes 16416 | tf_op jit(solution)/shard_map/ppermute | solution.py:52
  122.6 0.7 add.49.s0
  123.4 1.6 %collective-permute-start.12 = (f32[32,128]{1,0:T(8,128)S(1)}, f32[32,128]{1,0:T(8,128)S(1)}, u32[]{:S(2)}, u32[]{:S(2)}) collective-permute-start(f32[32,128]{1,0:T(8,128)S(1)} %add.49.s0), channel_id=1, source_target_pairs={{0,2},{1,3},{2,4},{3,5},{4,6},{5,7},{6,0},{7,1},{8,10},{9,11},{10,... | collective-permute-start | bytes 49160 | tf_op jit(solution)/shard_map/ppermute | solution.py:52
  124.9 1.7 %collective-permute-start.13 = (f32[32,128]{1,0:T(8,128)S(1)}, f32[32,128]{1,0:T(8,128)S(1)}, u32[]{:S(2)}, u32[]{:S(2)}) collective-permute-start(f32[32,128]{1,0:T(8,128)S(1)} %add.49.s0), channel_id=1, source_target_pairs={{0,6},{1,7},{2,0},{3,1},{4,2},{5,3},{6,4},{7,5},{8,14},{9,15},{10,... | collective-permute-start | bytes 49160 | tf_op jit(solution)/shard_map/ppermute | solution.py:52
  126.6 2.0 %collective-permute-start.14 = (f32[32,128]{1,0:T(8,128)S(1)}, f32[32,128]{1,0:T(8,128)S(1)}, u32[]{:S(2)}, u32[]{:S(2)}) collective-permute-start(f32[32,128]{1,0:T(8,128)S(1)} %add.49.s0), channel_id=1, source_target_pairs={{0,4},{1,5},{2,6},{3,7},{4,0},{5,1},{6,2},{7,3},{8,12},{9,13},{10,... | collective-permute-start | bytes 49160 | tf_op jit(solution)/shard_map/ppermute | solution.py:52
  128.6 0.0 collective-permute-done.12.s1
  128.6 0.1 collective-permute-done.13.s2
  128.7 3.2 %collective-permute-done.14.s3 = f32[32,128]{1,0:T(8,128)S(1)} collective-permute-done((f32[32,128]{1,0:T(8,128)S(1)}, f32[32,128]{1,0:T(8,128)S(1)}, u32[]{:S(2)}, u32[]{:S(2)}) %collective-permute-start.14) | collective-permute-done | bytes 16416 | tf_op jit(solution)/shard_map/ppermute | solution.py:52
  131.8 0.0 copy-done.6
  131.9 0.0 copy-done.7
  131.9 0.6 copy-done.9
  132.4 4.7 %norm.1 = bf16[4096,256]{1,0:T(8,128)(2,1)} custom-call(f32[4096,256]{1,0:T(8,128)} %get-tuple-element.35.attention, f32[32,128]{1,0:T(8,128)} %copy-done.6, f32[32,128]{1,0:T(8,128)} %copy-done.7, f32[32,128]{1,0:T(8,128)} %copy-done.8, f32[32,128]{1,0:T(8,128)} %copy-done.9, f32[1,256]{1,0:T(1,128)} %bitcast.12), custom_call_target="tpu_custom_call" | custom-call | tf_op jit(solution)/shard_map/norm/pallas_call | solution.py:424
  (12 shorter events, 0.0 us)
Async XLA Ops:
  2.5 7.8 %collective-permute-start = (bf16[128,768]{1,0:T(8,128)(2,1)S(1)}, bf16[128,768]{1,0:T(8,128)(2,1)S(1)}, u32[]{:S(2)}, u32[]{:S(2)}) collective-permute-start(bf16[128,768]{1,0:T(8,128)(2,1)S(1)} %constant_dynamic-update-slice_fusion), channel_id=1, source_target_pairs={{0,8},{1,33},{2,10},{3,35},{4,12},{5,37},{6,14},{7,39},{8,16},{9,4... | collective-permute-start | bytes 589832 | tf_op jit(solution)/shard_map/ppermute | solution.py:39
  4.5 5.8 %collective-permute-start.1 = (bf16[128,768]{1,0:T(8,128)(2,1)S(1)}, bf16[128,768]{1,0:T(8,128)(2,1)S(1)}, u32[]{:S(2)}, u32[]{:S(2)}) collective-permute-start(bf16[128,768]{1,0:T(8,128)(2,1)S(1)} %constant_dynamic-update-slice_fusion), channel_id=1, source_target_pairs={{0,24},{1,97},{2,26},{3,99},{4,28},{5,101},{6,30},{7,103},{8,0},{9... | collective-permute-start | bytes 589832 | tf_op jit(solution)/shard_map/ppermute | solution.py:39
  6.7 7.2 %collective-permute-start.2 = (bf16[128,768]{1,0:T(8,128)(2,1)S(1)}, bf16[128,768]{1,0:T(8,128)(2,1)S(1)}, u32[]{:S(2)}, u32[]{:S(2)}) collective-permute-start(bf16[128,768]{1,0:T(8,128)(2,1)S(1)} %constant_dynamic-update-slice_fusion), channel_id=1, source_target_pairs={{0,16},{1,65},{2,18},{3,67},{4,20},{5,69},{6,22},{7,71},{8,24},{9,... | collective-permute-start | bytes 589832 | tf_op jit(solution)/shard_map/ppermute | solution.py:39
  14.0 22.7 %copy-start = (bf16[4,128,768]{2,1,0:T(8,128)(2,1)}, bf16[4,128,768]{2,1,0:T(8,128)(2,1)S(1)}, u32[]{:S(2)}) copy-start(bf16[4,128,768]{2,1,0:T(8,128)(2,1)S(1)} %pad_maximum_fusion.w0) | copy-start | bytes 2359300
  14.0 13.3 %collective-permute-start.3 = (bf16[4,128,768]{2,1,0:T(8,128)(2,1)S(1)}, bf16[4,128,768]{2,1,0:T(8,128)(2,1)S(1)}, u32[]{:S(2)}, u32[]{:S(2)}) collective-permute-start(bf16[4,128,768]{2,1,0:T(8,128)(2,1)S(1)} %pad_maximum_fusion.w0), channel_id=1, source_target_pairs={{0,32},{1,9},{2,34},{3,11},{4,36},{5,13},{6,38},{7,15},{8,40},{9,1... | collective-permute-start | bytes 2359304 | tf_op jit(solution)/shard_map/ppermute | solution.py:39
  15.5 19.7 %collective-permute-start.4 = (bf16[4,128,768]{2,1,0:T(8,128)(2,1)S(1)}, bf16[4,128,768]{2,1,0:T(8,128)(2,1)S(1)}, u32[]{:S(2)}, u32[]{:S(2)}) collective-permute-start(bf16[4,128,768]{2,1,0:T(8,128)(2,1)S(1)} %pad_maximum_fusion.w0), channel_id=1, source_target_pairs={{0,96},{1,25},{2,98},{3,27},{4,100},{5,29},{6,102},{7,31},{8,104},... | collective-permute-start | bytes 2359304 | tf_op jit(solution)/shard_map/ppermute | solution.py:39
  17.3 19.4 %collective-permute-start.5 = (bf16[4,128,768]{2,1,0:T(8,128)(2,1)S(1)}, bf16[4,128,768]{2,1,0:T(8,128)(2,1)S(1)}, u32[]{:S(2)}, u32[]{:S(2)}) collective-permute-start(bf16[4,128,768]{2,1,0:T(8,128)(2,1)S(1)} %pad_maximum_fusion.w0), channel_id=1, source_target_pairs={{0,64},{1,17},{2,66},{3,19},{4,68},{5,21},{6,70},{7,23},{8,72},{9,... | collective-permute-start | bytes 2359304 | tf_op jit(solution)/shard_map/ppermute | solution.py:39
  27.3 9.4 %copy-start.10 = (bf16[4,128,768]{2,1,0:T(8,128)(2,1)}, bf16[4,128,768]{2,1,0:T(8,128)(2,1)S(1)}, u32[]{:S(2)}) copy-start(bf16[4,128,768]{2,1,0:T(8,128)(2,1)S(1)} %collective-permute-done.3.w1) | copy-start | bytes 2359300
  35.3 1.4 %copy-start.11 = (bf16[4,128,768]{2,1,0:T(8,128)(2,1)}, bf16[4,128,768]{2,1,0:T(8,128)(2,1)S(1)}, u32[]{:S(2)}) copy-start(bf16[4,128,768]{2,1,0:T(8,128)(2,1)S(1)} %collective-permute-done.4.w2) | copy-start | bytes 2359300
  36.7 0.9 copy-start.12
  66.5 8.7 %collective-permute-start.6 = (bf16[352,512]{1,0:T(8,128)(2,1)}, bf16[352,512]{1,0:T(8,128)(2,1)S(1)}, u32[]{:S(2)}, u32[]{:S(2)}) collective-permute-start(bf16[352,512]{1,0:T(8,128)(2,1)} %get-tuple-element.27), channel_id=1, source_target_pairs={{0,8},{8,0},{16,24},{24,16},{32,40},{40,32},{48,56},{56,48},{64,72... | collective-permute-start | bytes 1081352 | tf_op jit(solution)/shard_map/ppermute | solution.py:43
  69.6 25.4 %collective-permute-start.7 = (bf16[128,512]{1,0:T(8,128)(2,1)}, bf16[128,512]{1,0:T(8,128)(2,1)S(1)}, u32[]{:S(2)}, u32[]{:S(2)}) collective-permute-start(bf16[128,512]{1,0:T(8,128)(2,1)} %get-tuple-element.28), channel_id=1, source_target_pairs={{8,16},{24,32},{40,48},{56,64},{72,80},{88,96},{104,112},{16,8},{3... | collective-permute-start | bytes 393224 | tf_op jit(solution)/shard_map/ppermute | solution.py:48
  75.2 19.8 %copy-start.1 = (bf16[352,512]{1,0:T(8,128)(2,1)}, bf16[352,512]{1,0:T(8,128)(2,1)S(1)}, u32[]{:S(2)}) copy-start(bf16[352,512]{1,0:T(8,128)(2,1)S(1)} %collective-permute-done.6.got_a) | copy-start | bytes 1081348
  75.3 19.8 %collective-permute-start.10 = (bf16[64,512]{1,0:T(8,128)(2,1)S(1)}, bf16[64,512]{1,0:T(8,128)(2,1)S(1)}, u32[]{:S(2)}, u32[]{:S(2)}) collective-permute-start(bf16[64,512]{1,0:T(8,128)(2,1)S(1)} %pad_maximum_fusion.2), channel_id=1, source_target_pairs={{0,48},{8,56},{16,32},{24,40},{32,16},{40,24},{48,0},{56,8},{64,11... | collective-permute-start | bytes 196616 | tf_op jit(solution)/shard_map/ppermute | solution.py:43
  78.3 16.8 %collective-permute-start.9 = (bf16[64,512]{1,0:T(8,128)(2,1)S(1)}, bf16[64,512]{1,0:T(8,128)(2,1)S(1)}, u32[]{:S(2)}, u32[]{:S(2)}) collective-permute-start(bf16[64,512]{1,0:T(8,128)(2,1)S(1)} %pad_maximum_fusion.2), channel_id=1, source_target_pairs={{0,32},{8,40},{16,48},{24,56},{32,0},{40,8},{48,16},{56,24},{64,96... | collective-permute-start | bytes 196616 | tf_op jit(solution)/shard_map/ppermute | solution.py:43
  79.3 15.8 %collective-permute-start.8 = (bf16[128,512]{1,0:T(8,128)(2,1)S(1)}, bf16[128,512]{1,0:T(8,128)(2,1)S(1)}, u32[]{:S(2)}, u32[]{:S(2)}) collective-permute-start(bf16[128,512]{1,0:T(8,128)(2,1)S(1)} %pad_maximum_fusion.1), channel_id=1, source_target_pairs={{0,16},{8,24},{16,0},{24,8},{32,48},{40,56},{48,32},{56,40},{64,80... | collective-permute-start | bytes 393224 | tf_op jit(solution)/shard_map/ppermute | solution.py:43
  95.0 0.7 copy-start.2
  95.0 0.7 copy-start.4
  95.1 0.7 copy-start.5
  95.1 0.7 copy-start.3
  121.2 1.4 %collective-permute-start.11 = (f32[32,128]{1,0:T(8,128)}, f32[32,128]{1,0:T(8,128)S(1)}, u32[]{:S(2)}, u32[]{:S(2)}) collective-permute-start(f32[32,128]{1,0:T(8,128)} %get-tuple-element.36), channel_id=1, source_target_pairs={{0,1},{1,0},{2,3},{3,2},{4,5},{5,4},{6,7},{7,6},{8,9},{9,8},{10,11... | collective-permute-start | bytes 49160 | tf_op jit(solution)/shard_map/ppermute | solution.py:52
  123.4 8.5 %copy-start.6 = (f32[32,128]{1,0:T(8,128)}, f32[32,128]{1,0:T(8,128)S(1)}, u32[]{:S(2)}) copy-start(f32[32,128]{1,0:T(8,128)S(1)} %add.49.s0) | copy-start | bytes 49156
  123.4 5.2 %collective-permute-start.12 = (f32[32,128]{1,0:T(8,128)S(1)}, f32[32,128]{1,0:T(8,128)S(1)}, u32[]{:S(2)}, u32[]{:S(2)}) collective-permute-start(f32[32,128]{1,0:T(8,128)S(1)} %add.49.s0), channel_id=1, source_target_pairs={{0,2},{1,3},{2,4},{3,5},{4,6},{5,7},{6,0},{7,1},{8,10},{9,11},{10,... | collective-permute-start | bytes 49160 | tf_op jit(solution)/shard_map/ppermute | solution.py:52
  124.9 3.7 %collective-permute-start.13 = (f32[32,128]{1,0:T(8,128)S(1)}, f32[32,128]{1,0:T(8,128)S(1)}, u32[]{:S(2)}, u32[]{:S(2)}) collective-permute-start(f32[32,128]{1,0:T(8,128)S(1)} %add.49.s0), channel_id=1, source_target_pairs={{0,6},{1,7},{2,0},{3,1},{4,2},{5,3},{6,4},{7,5},{8,14},{9,15},{10,... | collective-permute-start | bytes 49160 | tf_op jit(solution)/shard_map/ppermute | solution.py:52
  126.6 5.2 %collective-permute-start.14 = (f32[32,128]{1,0:T(8,128)S(1)}, f32[32,128]{1,0:T(8,128)S(1)}, u32[]{:S(2)}, u32[]{:S(2)}) collective-permute-start(f32[32,128]{1,0:T(8,128)S(1)} %add.49.s0), channel_id=1, source_target_pairs={{0,4},{1,5},{2,6},{3,7},{4,0},{5,1},{6,2},{7,3},{8,12},{9,13},{10,... | collective-permute-start | bytes 49160 | tf_op jit(solution)/shard_map/ppermute | solution.py:52
  128.6 3.3 %copy-start.7 = (f32[32,128]{1,0:T(8,128)}, f32[32,128]{1,0:T(8,128)S(1)}, u32[]{:S(2)}) copy-start(f32[32,128]{1,0:T(8,128)S(1)} %collective-permute-done.12.s1) | copy-start | bytes 49156
  128.7 3.2 %copy-start.8 = (f32[32,128]{1,0:T(8,128)}, f32[32,128]{1,0:T(8,128)S(1)}, u32[]{:S(2)}) copy-start(f32[32,128]{1,0:T(8,128)S(1)} %collective-permute-done.13.s2) | copy-start | bytes 49156
  131.8 0.6 copy-start.9
where the time goes:
time: 138 us; the launch traced here: 137 us
  Pallas kernels  73 us (53%)
  waiting for transfers between devices  31 us (22%)
  starting transfers between devices  23.6 us (17%)
  local copies, waits for them, and re-layouts  6.47 us (5%)
  other arithmetic  2.87 us (2%)
    pallas_call x1, Pallas kernels, project(): pl.pallas_call(project_kernel, grid_spec=pltpu.PrefetchScalarGridSpec(num...  28.9 us
    pallas_call x1, Pallas kernels, fine(): pl.pallas_call(fine_kernel, grid_spec=pltpu.PrefetchScalarGridSpec(num_sc...  25.5 us
    ppermute x6, waiting for transfers between devices, along_line(): return lax.ppermute(value, ('seq', 'head'), line_perm(first, shift))  21.5 us
    pallas_call x1, Pallas kernels, pairs(): pl.pallas_call(pairs_kernel, grid=(4,), in_specs=[tiles(512, 768), tiles(...  13.9 us
    ppermute x6, starting transfers between devices, along_line(): return lax.ppermute(value, ('seq', 'head'), line_perm(first, shift))  11.1 us
    ppermute x4, starting transfers between devices, flipped(): return lax.ppermute(value, 'seq', [(i, i ^ bits) for i in range(16)])  6.65 us
    ppermute x4, starting transfers between devices, over_heads(): return lax.ppermute(value, 'head', [(i, step(i)) for i in range(8)])  5.22 us
    ppermute x4, waiting for transfers between devices, flipped(): return lax.ppermute(value, 'seq', [(i, i ^ bits) for i in range(16)])  4.94 us
  transfers between devices with their start and end apart: 15, of which 9 were waited for; matrix products, arithmetic and copies ran while one was open for 3% of the time, Pallas kernels for 10%

commit v1 on v0

v1 whole, which is shorter than its diff:
```python
import jax
import jax.numpy as jnp
import numpy as np
from jax import lax
from jax.experimental import pallas as pl
from jax.experimental.pallas import tpu as pltpu
from jax.sharding import PartitionSpec as P

H = 16
DH = 128
B = 128
D = 2048
HEADS = 2
SIDE = 4
TOKENS = 4096
SCALE = float(DH**-0.5 * np.log2(np.e))
GONE = -1e30
SHIFTS = (1, 3, 2)
BF = jnp.bfloat16
F32 = jnp.float32
TM = 1024
CHUNK = 512
CHUNKS = TOKENS // CHUNK
RUNS = TOKENS // TM
GROUP = 8


def line_perm(first, shift):
    pairs = []
    for x in range(SIDE):
        for z in range(SIDE):
            for head in range(8):
                if (head % 2 == 0) == first:
                    target = x * SIDE + (z + shift) % SIDE
                else:
                    target = (x + shift) % SIDE * SIDE + z
                pairs.append(((x * SIDE + z) * 8 + head, target * 8 + head))
    return pairs


def along_line(value, first, shift):
    return lax.ppermute(value, ("seq", "head"), line_perm(first, shift))


def flipped(value, bits):
    return lax.ppermute(value, "seq", [(i, i ^ bits) for i in range(16)])


def other_side(value):
    pairs = [(i, i + 1) for i in range(1, 15, 2)] + [(i + 1, i) for i in range(1, 15, 2)]
    return lax.ppermute(value, "seq", pairs)


def over_heads(value, step):
    return lax.ppermute(value, "head", [(i, step(i)) for i in range(8)])


def dot(a, b):
    return lax.dot_general(a, b, (((1,), (0,)), ((), ())), preferred_element_type=F32)


def dot_t(a, b):
    return lax.dot_general(a, b, (((1,), (1,)), ((), ())), preferred_element_type=F32)


def iota(shape, dim):
    return lax.broadcasted_iota(jnp.int32, shape, dim)


def level_matches(rows, first, levels, row_dim):
    shape = (128, rows) if row_dim == 1 else (rows, rows)
    token, slot = iota(shape, 0), iota(shape, 1)
    found = jnp.zeros(shape, jnp.bool_)
    start = 0
    for level in levels:
        count = 128 >> (level - first + 1)
        found = found | ((slot - start) == (token >> (level - first + 1)))  & (slot >= start) & (
            slot < start + count
        )
        start += count
    return found


def pool_matrix(rows, tokens, levels, first=0):
    row, token = iota((rows, tokens), 0), iota((rows, tokens), 1)
    total = jnp.zeros((rows, tokens), F32)
    start = 0
    for level in levels:
        count = tokens >> (level - first)
        inside = (row >= start) & (row < start + count) & ((row - start) == (token >> (level - first)))
        total = jnp.where(inside, 2.0 ** (first - level), total)
        start += count
    return total.astype(BF)


def parts_of(source, target, sems, count):
    rows = source.shape[0] // count
    return [
        pltpu.make_async_copy(
            source.at[pl.ds(i * rows, rows)], target.at[pl.ds(i * rows, rows)], sems.at[i]
        )
        for i in range(count)
    ]


def part_of(source, target, sems, index, rows):
    at = pl.ds(pl.multiple_of(index * rows, rows), rows)
    return pltpu.make_async_copy(source.at[at], target.at[at], sems.at[index])


def start_all(copies):
    for copy in copies:
        copy.start()


def wait_all(copies):
    for copy in copies:
        copy.wait()


def moves(pairs, sems):
    return [pltpu.make_async_copy(a, b, sems.at[n]) for n, (a, b) in enumerate(pairs)]


def start_projection(place, hidden, pieces, h_all, w_all, h_sem, w_sem):
    for outer, piece in enumerate(pieces):
        for inner in range(SIDE):
            slot = outer * SIDE + inner
            at = pl.multiple_of(place[slot] * 128, 128)
            pltpu.make_async_copy(piece.at[inner], w_all.at[pl.ds(at, 128)], w_sem.at[slot]).start()
    for index in range(2):
        part_of(hidden, h_all, h_sem, index, CHUNK).start()


def wait_weights(pieces, w_all, w_sem):
    for slot in range(16):
        pltpu.make_async_copy(
            pieces[slot // SIDE].at[slot % SIDE], w_all.at[pl.ds(0, 128)], w_sem.at[slot]
        ).wait()


def next_rows(hidden, h_all, h_sem, index):
    part_of(hidden, h_all, h_sem, index, CHUNK).wait()

    @pl.when(index < CHUNKS - 2)
    def _():
        part_of(hidden, h_all, h_sem, index + 2, CHUNK).start()


def pool_block(p_fine, rows, block, l1, l2, l3):
    pooled = dot(p_fine, rows).astype(BF)
    l1[pl.ds(pl.multiple_of(block * 64, 64), 64), :] = pooled[:64]
    l2[pl.ds(pl.multiple_of(block * 32, 32), 32), :] = pooled[64:96]
    l3[pl.ds(pl.multiple_of(block * 16, 16), 16), :] = pooled[96:112]


def pool_runs(l3):
    p_coarse = pool_matrix(128, 128, (4, 5, 6, 7), 3)
    coarse = [dot(p_coarse, l3[run * 128 : run * 128 + 128, :]) for run in range(4)]
    return [
        jnp.concatenate([c[low:high] for c in coarse], 0).astype(BF)
        for low, high in ((0, 64), (64, 96), (96, 112), (112, 120))
    ]


def keys_kernel(
    place, hidden, w0, w1, w2, w3,
    full_out, l1_out, l2_out, l3_out, l4_out, a_out, b_out, six_out, seven_out,
    h_all, w_all, full, l1, l2, l3, l4, send_a, send_b, six, seven, h_sem, w_sem, out_sem, last_sem,
):
    pieces = (w0, w1, w2, w3)
    start_projection(place, hidden, pieces, h_all, w_all, h_sem, w_sem)
    p_fine = pool_matrix(112, 128, (1, 2, 3))
    wait_weights(pieces, w_all, w_sem)

    def sends(index):
        made = zip((full, l1, l2, l3), (full_out, l1_out, l2_out, l3_out), (1, 2, 4, 8))
        return [
            part_of(v, out, out_sem.at[n], index, CHUNK // ratio)
            for n, (v, out, ratio) in enumerate(made)
        ]

    @pl.loop(0, CHUNKS)
    def _(index):
        next_rows(hidden, h_all, h_sem, index)
        at = pl.ds(pl.multiple_of(index * CHUNK, CHUNK), CHUNK)
        rows = dot(h_all[at, :], w_all[...]).astype(BF)
        full[at, :] = rows
        for part in range(CHUNK // 128):
            pool_block(p_fine, rows[part * 128 : part * 128 + 128], index * (CHUNK // 128) + part, l1, l2, l3)
        start_all(sends(index))

    l4[...], five, six[...], seven[...] = pool_runs(l3)
    odd = place[16] == 1
    low, high = full[:128, :], full[TOKENS - 128 :, :]
    send_a[:128, :] = jnp.where(odd, low, high)
    send_b[...] = jnp.where(odd, high, low)
    send_a[128:, :] = five
    pairs = ((l4, l4_out), (send_a, a_out), (send_b, b_out), (six, six_out), (seven, seven_out))
    last = moves(pairs, last_sem)
    start_all(last)

    @pl.loop(0, CHUNKS)
    def _(index):
        wait_all(sends(index))

    wait_all(last)


def queries_kernel(
    place, hidden, w0, w1, w2, w3, kv1, kv2,
    full_out, o1_out, o2_out, virtual_out, q3_out, q4_out, q5_out, q6_out, q7_out,
    h_all, w_all, full, l1, l2, l3, q4, q5, q6, q7, kv1_all, kv2_all, o1, o2, virtual,
    h_sem, w_sem, kv_sem, out_sem, last_sem,
):
    pieces = (w0, w1, w2, w3)
    start_projection(place, hidden, pieces, h_all, w_all, h_sem, w_sem)
    p_fine = pool_matrix(112, 128, (1, 2, 3))
    wait_weights(pieces, w_all, w_sem)
    arriving = [parts_of(kv1, kv1_all, kv_sem.at[0], RUNS), parts_of(kv2, kv2_all, kv_sem.at[1], RUNS)]
    leaving = [
        parts_of(mine, out, out_sem.at[n], RUNS)
        for n, (mine, out) in enumerate(((full, full_out), (o1, o1_out), (o2, o2_out)))
    ]

    def attend_run(run):
        wait_all([group[run] for group in arriving])
        triples, places = [], []
        for head in range(HEADS):
            k, v = (slice(i * 256 + head * 128, i * 256 + head * 128 + 128) for i in range(2))
            for q_all, kv_all, out, count in ((l1, kv1_all, o1, 4), (l2, kv2_all, o2, 2)):
                for block in range(run * count, run * count + count):
                    mine = slice(block * 128, block * 128 + 128)
                    its = slice((block ^ 1) * 128, (block ^ 1) * 128 + 128)
                    triples.append((q_all[mine, k], kv_all[its, k], kv_all[its, v]))
                    places.append((out, mine, k))
        done = attend_all(triples)
        for (out, mine, k), (rows, _) in zip(places, done):
            out[mine, k] = rows
        for head in range(HEADS):
            ends = [level_row(total) for _, total in done[head * 6 : head * 6 + 6]]
            lanes = []
            for block in range(8):
                fine = ends[block // 2][:, block % 2 * 64 : block % 2 * 64 + 64]
                coarse = ends[4 + block // 4][:, block % 4 * 32 : block % 4 * 32 + 32]
                lanes.append(jnp.concatenate([fine, coarse, jnp.zeros((1, 32), F32)], 1))
            virtual[run * 8 : run * 8 + 8, head * 128 : head * 128 + 128] = jnp.concatenate(lanes, 0)

    for run in range(RUNS):
        for index in range(run * (TM // CHUNK), (run + 1) * (TM // CHUNK)):
            next_rows(hidden, h_all, h_sem, jnp.int32(index))
        start_all([group[run] for group in arriving])
        at = slice(run * TM, run * TM + TM)
        rows = (dot(h_all[at, :], w_all[...]) * SCALE).astype(BF)
        full[at, :] = rows
        leaving[0][run].start()
        for part in range(TM // 128):
            pool_block(p_fine, rows[part * 128 : part * 128 + 128], run * (TM // 128) + part, l1, l2, l3)
        if run:
            attend_run(run - 1)
            leaving[1][run - 1].start()
            leaving[2][run - 1].start()
    q4[...], q5[...], q6[...], q7[...] = pool_runs(l3)
    attend_run(RUNS - 1)
    leaving[1][RUNS - 1].start()
    leaving[2][RUNS - 1].start()
    pairs = ((virtual, virtual_out), (l3, q3_out), (q4, q4_out), (q5, q5_out), (q6, q6_out), (q7, q7_out))
    last = moves(pairs, last_sem)
    start_all(last)
    for group in leaving:
        wait_all(group)
    wait_all(last)


def project_keys(place, hidden, pieces):
    anywhere = pl.BlockSpec(memory_space=pl.ANY)
    levels = [(TOKENS >> level, 512) for level in range(5)]
    small = [(256, 512), (128, 512), (64, 512), (32, 512)]
    return pl.pallas_call(
        keys_kernel,
        in_specs=[pl.BlockSpec(memory_space=pltpu.SMEM)] + [anywhere] * 5,
        out_specs=[anywhere] * 9,
        out_shape=[jax.ShapeDtypeStruct(size, BF) for size in levels + small],
        scratch_shapes=[
            pltpu.VMEM((TOKENS, D), BF),
            pltpu.VMEM((D, 512), BF),
            *[pltpu.VMEM(size, BF) for size in levels + small],
            pltpu.SemaphoreType.DMA((CHUNKS,)),
            pltpu.SemaphoreType.DMA((16,)),
            pltpu.SemaphoreType.DMA((4, CHUNKS)),
            pltpu.SemaphoreType.DMA((5,)),
        ],
        compiler_params=pltpu.CompilerParams(vmem_limit_bytes=56 * 2**20),
        name="project_keys",
        cost_estimate=pl.CostEstimate(
            flops=2 * TOKENS * D * 512, bytes_accessed=26 * 2**20, transcendentals=0
        ),
    )(place, hidden, *pieces)


def project_queries(place, hidden, pieces, kv1, kv2):
    anywhere = pl.BlockSpec(memory_space=pl.ANY)
    shape = jax.ShapeDtypeStruct
    small = [shape((size, 256), BF) for size in (512, 256, 128, 64, 32)]
    buffer = lambda *size: pltpu.VMEM(size, BF)
    return pl.pallas_call(
        queries_kernel,
        in_specs=[pl.BlockSpec(memory_space=pltpu.SMEM)] + [anywhere] * 7,
        out_specs=[anywhere] * 9,
        out_shape=[shape((TOKENS, 256), BF), shape((2048, 256), BF), shape((1024, 256), BF)]
        + [shape((32, 256), F32)]
        + small,
        scratch_shapes=[
            buffer(TOKENS, D),
            buffer(D, 256),
            *[buffer(TOKENS >> level, 256) for level in range(4)],
            *[buffer(size, 256) for size in (256, 128, 64, 32)],
            buffer(2048, 512),
            buffer(1024, 512),
            buffer(2048, 256),
            buffer(1024, 256),
            pltpu.VMEM((32, 256), F32),
            pltpu.SemaphoreType.DMA((CHUNKS,)),
            pltpu.SemaphoreType.DMA((16,)),
            pltpu.SemaphoreType.DMA((2, RUNS)),
            pltpu.SemaphoreType.DMA((3, RUNS)),
            pltpu.SemaphoreType.DMA((6,)),
        ],
        compiler_params=pltpu.CompilerParams(vmem_limit_bytes=56 * 2**20),
        name="project_queries",
        cost_estimate=pl.CostEstimate(
            flops=2 * TOKENS * D * 256, bytes_accessed=26 * 2**20, transcendentals=2**20
        ),
    )(place, hidden, *pieces, kv1, kv2)


def with_ones(values):
    return jnp.concatenate([values, jnp.ones_like(values)], axis=1)


def quotient(rows, total):
    inverse = pl.reciprocal(total, approx=True)
    return rows * (inverse * (2.0 - total * inverse))


def attend_all(triples):
    scores = [dot_t(queries, key_rows) for queries, key_rows, _ in triples]
    highest = [jnp.max(s, axis=1, keepdims=True) for s in scores]
    weights = [jnp.exp2(s - h).astype(BF) for s, h in zip(scores, highest)]
    both = [dot(w, with_ones(values)) for w, (_, _, values) in zip(weights, triples)]
    return [
        (quotient(o[:, :DH], o[:, DH:]).astype(BF), h + jnp.log2(o[:, DH:])) for o, h in zip(both, highest)
    ]


def level_row(total):
    eye = iota((128, 128), 0) == iota((128, 128), 1)
    return jnp.sum(jnp.where(eye, total, 0.0), axis=0, keepdims=True)


def merged(parts, found):
    scores = [dot_t(queries, key_rows) for queries, key_rows, *_ in parts]
    scores = [s if p[5] is None else s + p[5] for s, p in zip(scores, parts)]
    coarse = [jnp.where(found, p[3], GONE) for p in parts]
    highest = [
        jnp.maximum(jnp.max(s, axis=1, keepdims=True), jnp.max(c, axis=1, keepdims=True))
        for s, c in zip(scores, coarse)
    ]
    weights = [
        jnp.concatenate([jnp.exp2(s - h).astype(BF), jnp.exp2(c - h).astype(BF)], 1)
        for s, c, h in zip(scores, coarse, highest)
    ]
    both = [
        dot(w, with_ones(jnp.concatenate([p[2], p[4]], 0))) for w, p in zip(weights, parts)
    ]
    return [(o[:, :DH], o[:, DH:], h) for o, h in zip(both, highest)]


def fine_kernel(
    edge, q3_in, kv3_in, q4_in, kv4_in, q5_in, q6_in, q7_in, got_a, got_b, got_d, got_s, got_c, got_e,
    virtual_in, q, kv, o1, o2, out, squares,
    q3, kv3, q4, kv4, q5, q6, q7, kv5, kv6, kv7, virtual,
    q_all, kv_all, o1_all, o2_all, o3, virtual_3, out_all, first_sem, in_sem, out_sem,
):
    odd = edge[0] == 1
    above, below = 0, 128 + TOKENS
    at_a = pl.ds(pl.multiple_of(jnp.where(odd, above, below), 128), 128)
    at_b = pl.ds(pl.multiple_of(jnp.where(odd, below, above), 128), 128)
    early = moves(
        (
            (q4_in, q4),
            (kv4_in, kv4),
            (q5_in, q5),
            (q6_in, q6),
            (q7_in, q7),
            (got_a.at[pl.ds(128, 128)], kv5),
            (got_c.at[pl.ds(0, 64)], kv6.at[pl.ds(0, 64)]),
            (got_e.at[pl.ds(0, 64)], kv6.at[pl.ds(64, 64)]),
            (got_d, kv7.at[pl.ds(0, 32)]),
            (got_s, kv7.at[pl.ds(32, 32)]),
            (got_c.at[pl.ds(64, 32)], kv7.at[pl.ds(64, 32)]),
            (got_e.at[pl.ds(64, 32)], kv7.at[pl.ds(96, 32)]),
            (q3_in, q3),
            (kv3_in, kv3),
            (virtual_in, virtual),
            (got_a.at[pl.ds(0, 128)], kv_all.at[at_a]),
            (got_b, kv_all.at[at_b]),
        ),
        first_sem,
    )
    inner = kv_all.at[pl.ds(128, TOKENS)]
    groups = ((q, q_all), (kv, inner), (o1, o1_all), (o2, o2_all))
    arriving = [parts_of(a, b, in_sem.at[n], RUNS) for n, (a, b) in enumerate(groups)]
    start_all(early)
    for part in range(2):
        start_all([group[part] for group in arriving])
    wait_all(early)

    found = level_matches(128, 4, (4, 5, 6, 7), 1)
    triples = []
    for head in range(HEADS):
        k, v = (slice(i * 256 + head * 128, i * 256 + head * 128 + 128) for i in range(2))
        for block in range(2):
            mine = slice(block * 128, block * 128 + 128)
            its = slice((block ^ 1) * 128, (block ^ 1) * 128 + 128)
            triples.append((q4[mine, k], kv4[its, k], kv4[its, v]))
        triples.append((q5[:, k], kv5[:, k], kv5[:, v]))
        triples.append((q6[:, k], kv6[:, k], kv6[:, v]))
        triples.append((q7[:, k], kv7[:, k], kv7[:, v]))
    done = attend_all(triples)
    parts = []
    for head in range(HEADS):
        k, v = (slice(i * 256 + head * 128, i * 256 + head * 128 + 128) for i in range(2))
        (oa, ea), (ob, eb), (o5, e5), (o6, e6), (o7, e7) = done[head * 5 : head * 5 + 5]
        for run in range(4):
            its = slice((run ^ 1) * 128, (run ^ 1) * 128 + 128)
            mine = slice(run * 128, run * 128 + 128)
            half = slice(run % 2 * 64, run % 2 * 64 + 64)
            values = jnp.concatenate(
                [
                    (oa, ob)[run // 2][half].astype(F32),
                    o5[run * 32 : run * 32 + 32].astype(F32),
                    o6[run * 16 : run * 16 + 16].astype(F32),
                    o7.astype(F32)[run * 8 : run * 8 + 8],
                    jnp.zeros((8, DH), F32),
                ],
                0,
            ).astype(BF)
            total = jnp.concatenate(
                [
                    (ea, eb)[run // 2][half],
                    e5[run * 32 : run * 32 + 32],
                    e6[run * 16 : run * 16 + 16],
                    e7[run * 8 : run * 8 + 8],
                    jnp.zeros((8, DH), F32),
                ],
                0,
            )
            parts.append((q3[mine, k], kv3[its, k], kv3[its, v], level_row(total), values, None))
    for index, (weighted, total, highest) in enumerate(merged(parts, found)):
        head, run = divmod(index, 4)
        c = slice(head * 128, head * 128 + 128)
        o3[run * 128 : run * 128 + 128, c] = quotient(weighted, total).astype(BF)
        ends = level_row(highest + jnp.log2(total))
        lanes = [
            jnp.concatenate(
                [jnp.zeros((1, 96), F32), ends[:, block * 16 : block * 16 + 16], jnp.zeros((1, 16), F32)], 1
            )
            for block in range(8)
        ]
        mine = slice(run * 8, run * 8 + 8)
        virtual_3[mine, c] = jnp.concatenate(lanes, 0) + virtual[mine, c]

    found = level_matches(128, 1, (1, 2, 3), 1)
    row = iota((8, 128), 0)
    arriving[1][0].wait()

    @pl.loop(0, RUNS)
    def _(step):
        part_of(q, q_all, in_sem.at[0], step, TM).wait()
        part_of(o1, o1_all, in_sem.at[2], step, TM // 2).wait()
        part_of(o2, o2_all, in_sem.at[3], step, TM // 4).wait()

        @pl.when(step < RUNS - 2)
        def _():
            part_of(q, q_all, in_sem.at[0], step + 2, TM).start()
            part_of(kv, inner, in_sem.at[1], step + 2, TM).start()
            part_of(o1, o1_all, in_sem.at[2], step + 2, TM // 2).start()
            part_of(o2, o2_all, in_sem.at[3], step + 2, TM // 4).start()

        @pl.when(step < RUNS - 1)
        def _():
            part_of(kv, inner, in_sem.at[1], step + 1, TM).wait()

        first = jnp.where((step == 0) & (edge[1] == 1), GONE, 0.0)
        last = jnp.where((step == 3) & (edge[2] == 1), GONE, 0.0)
        gathered = jnp.zeros((8, 128), F32)
        levels = virtual_3[pl.ds(pl.multiple_of(step * 8, 8), 8), :]
        for group in range(8 // GROUP):
            parts = []
            for block in range(group * GROUP, group * GROUP + GROUP):
                at = pl.multiple_of(step * TM + block * 128, 128)
                b = step * 8 + block
                at1 = pl.ds(pl.multiple_of(b * 64, 64), 64)
                at2 = pl.ds(pl.multiple_of(b * 32, 32), 32)
                at3 = pl.ds(pl.multiple_of(b * 16, 16), 16)
                bias = None
                if block == 0:
                    bias = jnp.where(iota((1, 384), 1) < 128, first, 0.0)
                if block == 7:
                    bias = jnp.where(iota((1, 384), 1) >= 256, last, 0.0)
                for head in range(HEADS):
                    c, gv = (slice(i * 256 + head * 128, i * 256 + head * 128 + 128) for i in range(2))
                    values = jnp.concatenate(
                        [o1_all[at1, c], o2_all[at2, c], o3[at3, c], jnp.zeros((16, DH), BF)], 0
                    )
                    parts.append(
                        (
                            q_all[pl.ds(at, 128), c],
                            kv_all[pl.ds(at, 384), c],
                            kv_all[pl.ds(at, 384), gv],
                            levels[block : block + 1, c],
                            values,
                            bias,
                        )
                    )
            done = merged(parts, found)
            for index, block in enumerate(range(group * GROUP, group * GROUP + GROUP)):
                sums = jnp.zeros((128, DH), F32)
                at = pl.ds(pl.multiple_of(step * TM + block * 128, 128), 128)
                for head in range(HEADS):
                    weighted, total, _ = done[index * HEADS + head]
                    attention = quotient(weighted, total)
                    out_all[at, head * 128 : head * 128 + 128] = attention.astype(BF)
                    sums = sums + attention * attention
                token_sums = dot_t(jnp.ones((8, DH), F32), sums)
                gathered = jnp.where(row == block, token_sums, gathered)
        squares[pl.ds(pl.multiple_of(step * 8, 8), 8), :] = gathered
        part_of(out_all, out, out_sem, step, TM).start()

    @pl.loop(0, 4)
    def _(step):
        part_of(out_all, out, out_sem, step, TM).wait()


def fine(edge, *arrays):
    anywhere = pl.BlockSpec(memory_space=pl.ANY)
    local = pl.BlockSpec(memory_space=pltpu.VMEM)
    shape = jax.ShapeDtypeStruct
    buffer = lambda *size: pltpu.VMEM(size, BF)
    return pl.pallas_call(
        fine_kernel,
        in_specs=[pl.BlockSpec(memory_space=pltpu.SMEM)] + [anywhere] * len(arrays),
        out_specs=[anywhere, local],
        scratch_shapes=[
            buffer(512, 256),
            buffer(512, 512),
            buffer(256, 256),
            buffer(256, 512),
            *[buffer(size, 256) for size in (128, 64, 32)],
            *[buffer(128, 512)] * 3,
            pltpu.VMEM((32, 256), F32),
            buffer(TOKENS, 256),
            buffer(TOKENS + 256, 512),
            buffer(TOKENS // 2, 256),
            buffer(TOKENS // 4, 256),
            buffer(512, 256),
            pltpu.VMEM((32, 256), F32),
            buffer(TOKENS, 256),
            pltpu.SemaphoreType.DMA((17,)),
            pltpu.SemaphoreType.DMA((4, RUNS)),
            pltpu.SemaphoreType.DMA((RUNS,)),
        ],
        out_shape=[shape((TOKENS, 256), BF), shape((32, 128), F32)],
        compiler_params=pltpu.CompilerParams(vmem_limit_bytes=56 * 2**20),
        name="merge_levels",
        cost_estimate=pl.CostEstimate(
            flops=4 * TOKENS * 512 * 256, bytes_accessed=18 * 2**20, transcendentals=TOKENS * 1024
        ),
    )(edge, *arrays)


def norm_kernel(attention, s0, s1, s2, s3, gain, out, rows, done, in_sem, out_sem):
    arriving = parts_of(attention, rows, in_sem, 4)
    leaving = parts_of(done, out, out_sem, 4)
    start_all(arriving)
    total = s0[...] + s1[...] + s2[...] + s3[...]
    factor = lax.rsqrt(total / D + 1e-6)
    eye = iota((128, 128), 0) == iota((128, 128), 1)
    for part in range(4):
        arriving[part].wait()
        for block in range(part * 8, part * 8 + 8):
            mine = slice(block * 128, block * 128 + 128)
            column = jnp.sum(jnp.where(eye, factor[block : block + 1], 0.0), axis=1, keepdims=True)
            done[mine, :] = (rows[mine, :].astype(F32) * column * gain[...]).astype(BF)
        leaving[part].start()
    wait_all(leaving)


def norm(attention, sums, gain):
    anywhere = pl.BlockSpec(memory_space=pl.ANY)
    local = pl.BlockSpec(memory_space=pltpu.VMEM)
    return pl.pallas_call(
        norm_kernel,
        in_specs=[anywhere] + [local] * 5,
        out_specs=anywhere,
        out_shape=jax.ShapeDtypeStruct((TOKENS, 256), BF),
        scratch_shapes=[
            pltpu.VMEM((TOKENS, 256), BF),
            pltpu.VMEM((TOKENS, 256), BF),
            pltpu.SemaphoreType.DMA((4,)),
            pltpu.SemaphoreType.DMA((4,)),
        ],
        compiler_params=pltpu.CompilerParams(vmem_limit_bytes=56 * 2**20),
        name="norm",
    )(attention, *sums, gain)


def join_kernel(a, b, c, out):
    out[:, :256] = a[...]
    out[:, 256:512] = b[...]
    out[:, 512:] = c[...]


def joined(*weights):
    local = pl.BlockSpec(memory_space=pltpu.VMEM)
    return pl.pallas_call(
        join_kernel,
        in_specs=[local] * 3,
        out_specs=local,
        out_shape=jax.ShapeDtypeStruct((128, 768), BF),
        name="join_weights",
    )(*weights)


def shards(hidden_states, w_query, w_key, w_value, norm_gain):
    position = lax.axis_index("seq")
    core = lax.axis_index("head") % 2
    x, z = position // SIDE, position % SIDE
    w_mine = joined(w_key, w_value, w_query)
    line = jnp.stack([w_mine] + [along_line(w_mine, True, s) for s in SHIFTS])
    line_kv, line_q = line[:, :, :512], line[:, :, 512:]
    pieces_kv = [line_kv] + [along_line(line_kv, False, s) for s in SHIFTS]
    pieces_q = [line_q] + [along_line(line_q, False, s) for s in SHIFTS]
    back = jnp.array((0,) + SHIFTS, jnp.int32)
    near_x = jnp.where(core == 0, (x - back[:, None]) % SIDE, (x - back[None, :]) % SIDE)
    near_z = jnp.where(core == 0, (z - back[None, :]) % SIDE, (z - back[:, None]) % SIDE)
    place = jnp.concatenate([(near_x * SIDE + near_z).reshape(16), (position % 2).reshape(1)])
    place = place.astype(jnp.int32)
    kv, kv1, kv2, kv3, kv4, send_a, send_b, send_6, send_7 = project_keys(place, hidden_states, pieces_kv)
    got_d = flipped(send_7, 4)
    got_a = flipped(send_a, 1)
    got_b = other_side(send_b)
    far = jnp.concatenate([send_6, got_d], 0)
    got_s = flipped(got_d, 1)
    got_c = flipped(far, 2)
    got_e = flipped(far, 3)
    q, o1, o2, virtual, q3, q4, q5, q6, q7 = project_queries(place, hidden_states, pieces_q, kv1, kv2)
    edge = jnp.stack([position % 2, position == 0, position == 15]).astype(jnp.int32)
    attention, squares = fine(
        edge, q3, kv3, q4, kv4, q5, q6, q7, got_a, got_b, got_d, got_s, got_c, got_e, virtual, q, kv, o1, o2
    )
    chip = squares + over_heads(squares, lambda i: i ^ 1)
    sums = [chip] + [over_heads(chip, lambda i, s=s: (i + 2 * s) % 8) for s in SHIFTS]
    return norm(attention, sums, norm_gain.reshape(1, 256))


def solution(mesh):
    in_specs = (P("seq", None), P("seq", "head"), P("seq", "head"), P("seq", "head"), P("head"))
    return jax.shard_map(
        shards, mesh=mesh, in_specs=in_specs, out_specs=P("seq", "head"), check_vma=False
    )
```

time: 138 us -> 107 us (0.78)
  Pallas kernels: 73 us -> 52 us
  waiting for transfers between devices: 31 us -> 16.1 us
  starting transfers between devices: 23.6 us -> 29.2 us
  local copies, waits for them, and re-layouts: 6.47 us -> 3.89 us
  other arithmetic: 2.87 us -> 4.44 us
    pallas_call x4 -> x5, Pallas kernels: 73 us -> 52 us  [the longest x1 18.3 us: project_queries(): pl.pallas_call(queries_kernel, in_specs=[pl.BlockSpec(memory_space=pltpu....]
    ppermute x6 -> x9, waiting for transfers between devices: 21.5 us -> 9.45 us  [along_line(): return lax.ppermute(value, ('seq', 'head'), line_perm(first, shift))]
    ppermute x6 -> x9, starting transfers between devices: 11.1 us -> 15.9 us  [along_line(): return lax.ppermute(value, ('seq', 'head'), line_perm(first, shift))]
    ppermute x4 -> x5, waiting for transfers between devices: 4.94 us -> 1.28 us  [flipped(): return lax.ppermute(value, 'seq', [(i, i ^ bits) for i in range(16)])]
    slice x4 -> x0, local copies, waits for them, and re-layouts: 1.65 us -> none  [the longest x2 0.85 us: shards(): pair_6 = jnp.concatenate([send_a[256:320], got_a[256:320]], 0)]
    ppermute x4 -> x5, starting transfers between devices: 6.65 us -> 7.32 us  [flipped(): return lax.ppermute(value, 'seq', [(i, i ^ bits) for i in range(16)])]
    unnamed x28 -> x37, local copies, waits for them, and re-layouts: 3.9 us -> 3.81 us
  transfers between devices with their start and end apart: 15 -> 19, of which waited for: 9 -> 9; matrix products, arithmetic and copies ran while one was open for 3% -> 3% of each run, Pallas kernels for 10% -> 32%
where the time goes in v1:
time: 107 us; the launch traced here: 106 us
  Pallas kernels  52 us (49%)
  starting transfers between devices  29.2 us (27%)
  waiting for transfers between devices  16.1 us (15%)
  other arithmetic  4.44 us (4%)
  local copies, waits for them, and re-layouts  3.89 us (4%)
    pallas_call x1, Pallas kernels, project_queries(): pl.pallas_call(queries_kernel, in_specs=[pl.BlockSpec(memory_space=pltpu....  18.3 us
    ppermute x9, starting transfers between devices, along_line(): return lax.ppermute(value, ('seq', 'head'), line_perm(first, shift))  15.9 us
    pallas_call x1, Pallas kernels, project_keys(): pl.pallas_call(keys_kernel, in_specs=[pl.BlockSpec(memory_space=pltpu.SME...  15.9 us
    pallas_call x1, Pallas kernels, fine(): pl.pallas_call(fine_kernel, in_specs=[pl.BlockSpec(memory_space=pltpu.SME...  12.6 us
    ppermute x9, waiting for transfers between devices, along_line(): return lax.ppermute(value, ('seq', 'head'), line_perm(first, shift))  9.45 us
    ppermute x5, starting transfers between devices, flipped(): return lax.ppermute(value, 'seq', [(i, i ^ bits) for i in range(16)])  7.32 us
    ppermute x4, waiting for transfers between devices, over_heads(): return lax.ppermute(value, 'head', [(i, step(i)) for i in range(8)])  5.34 us
    ppermute x4, starting transfers between devices, over_heads(): return lax.ppermute(value, 'head', [(i, step(i)) for i in range(8)])  5.31 us
  transfers between devices with their start and end apart: 19, of which 9 were waited for; matrix products, arithmetic and copies ran while one was open for 3% of the time, Pallas kernels for 32%

profile of v1, /device:TPU:0, one launch (start us, length us, event | category | flops | bytes accessed | tf_op | source)
XLA Modules:
  0.0 106.0 jit_solution(6262729884749001939)
XLA Ops:
  0.0 1.6 %join_weights.1 = bf16[128,768]{1,0:T(8,128)(2,1)} custom-call(bf16[128,256]{1,0:T(8,128)(2,1)} %a.1, bf16[128,256]{1,0:T(8,128)(2,1)} %b.1, bf16[128,256]{1,0:T(8,128)(2,1)} %c.1), custom_call_target="tpu_custom_call" | custom-call | tf_op jit(solution)/shard_map/join_weights/pallas_call | solution.py:627
  1.6 4.0 %collective-permute-start.2 = (bf16[128,768]{1,0:T(8,128)(2,1)}, bf16[128,768]{1,0:T(8,128)(2,1)S(1)}, u32[]{:S(2)}, u32[]{:S(2)}) collective-permute-start(bf16[128,768]{1,0:T(8,128)(2,1)} %join_weights.1), channel_id=1, source_target_pairs={{0,16},{1,65},{2,18},{3,67},{4,20},{5,69},{6,22},{7,71},{8,24},{9,... | collective-permute-start | bytes 589832 | tf_op jit(solution)/shard_map/ppermute | solution.py:42
  5.6 0.7 collective-permute-start.1
  6.3 1.3 %collective-permute-start = (bf16[128,768]{1,0:T(8,128)(2,1)}, bf16[128,768]{1,0:T(8,128)(2,1)S(1)}, u32[]{:S(2)}, u32[]{:S(2)}) collective-permute-start(bf16[128,768]{1,0:T(8,128)(2,1)} %join_weights.1), channel_id=1, source_target_pairs={{0,8},{1,33},{2,10},{3,35},{4,12},{5,37},{6,14},{7,39},{8,16},{9,4... | collective-permute-start | bytes 589832 | tf_op jit(solution)/shard_map/ppermute | solution.py:42
  7.6 0.7 and_select_fusion.1
  8.2 1.2 %collective-permute-done.2 = bf16[128,768]{1,0:T(8,128)(2,1)S(1)} collective-permute-done((bf16[128,768]{1,0:T(8,128)(2,1)}, bf16[128,768]{1,0:T(8,128)(2,1)S(1)}, u32[]{:S(2)}, u32[]{:S(2)}) %collective-permute-start.2) | collective-permute-done | bytes 196640 | tf_op jit(solution)/shard_map/ppermute | solution.py:42
  9.4 3.2 %collective-permute-done.1 = bf16[128,768]{1,0:T(8,128)(2,1)S(1)} collective-permute-done((bf16[128,768]{1,0:T(8,128)(2,1)}, bf16[128,768]{1,0:T(8,128)(2,1)S(1)}, u32[]{:S(2)}, u32[]{:S(2)}) %collective-permute-start.1) | collective-permute-done | bytes 196640 | tf_op jit(solution)/shard_map/ppermute | solution.py:42
  12.6 0.8 collective-permute-done
  13.4 0.9 pad_maximum_fusion.w0
  14.3 3.1 %collective-permute-start.8 = (bf16[4,128,512]{2,1,0:T(8,128)(2,1)S(1)}, bf16[4,128,512]{2,1,0:T(8,128)(2,1)S(1)}, u32[]{:S(2)}, u32[]{:S(2)}) collective-permute-start(bf16[4,128,512]{2,1,0:T(8,128)(2,1)S(1)} %pad_maximum_fusion.w0), channel_id=1, source_target_pairs={{0,64},{1,17},{2,66},{3,19},{4,68},{5,21},{6,70},{7,23},{8,72},{9,... | collective-permute-start | bytes 1572872 | tf_op jit(solution)/shard_map/ppermute | solution.py:42
  17.4 1.1 %collective-permute-start.7 = (bf16[4,128,512]{2,1,0:T(8,128)(2,1)S(1)}, bf16[4,128,512]{2,1,0:T(8,128)(2,1)S(1)}, u32[]{:S(2)}, u32[]{:S(2)}) collective-permute-start(bf16[4,128,512]{2,1,0:T(8,128)(2,1)S(1)} %pad_maximum_fusion.w0), channel_id=1, source_target_pairs={{0,96},{1,25},{2,98},{3,27},{4,100},{5,29},{6,102},{7,31},{8,104},... | collective-permute-start | bytes 1572872 | tf_op jit(solution)/shard_map/ppermute | solution.py:42
  18.6 0.9 collective-permute-start.6
  19.4 0.1 select_add_fusion
  19.5 0.1 add.48
  19.6 0.6 pad_add_fusion.1.place
  20.2 0.6 pad_add_fusion.edge
  20.8 0.9 pad_maximum_fusion.3.w0
  21.7 0.7 collective-permute-start.5
  22.4 2.6 %collective-permute-start.4 = (bf16[4,128,256]{2,1,0:T(8,128)(2,1)S(1)}, bf16[4,128,256]{2,1,0:T(8,128)(2,1)S(1)}, u32[]{:S(2)}, u32[]{:S(2)}) collective-permute-start(bf16[4,128,256]{2,1,0:T(8,128)(2,1)S(1)} %pad_maximum_fusion.3.w0), channel_id=1, source_target_pairs={{0,96},{1,25},{2,98},{3,27},{4,100},{5,29},{6,102},{7,31},{8,104},... | collective-permute-start | bytes 786440 | tf_op jit(solution)/shard_map/ppermute | solution.py:42
  25.0 0.2 collective-permute-done.8.w3
  25.2 1.5 %collective-permute-start.3 = (bf16[4,128,256]{2,1,0:T(8,128)(2,1)S(1)}, bf16[4,128,256]{2,1,0:T(8,128)(2,1)S(1)}, u32[]{:S(2)}, u32[]{:S(2)}) collective-permute-start(bf16[4,128,256]{2,1,0:T(8,128)(2,1)S(1)} %pad_maximum_fusion.3.w0), channel_id=1, source_target_pairs={{0,32},{1,9},{2,34},{3,11},{4,36},{5,13},{6,38},{7,15},{8,40},{9,1... | collective-permute-start | bytes 786440 | tf_op jit(solution)/shard_map/ppermute | solution.py:42
  26.7 4.1 %collective-permute-done.7.w2 = bf16[4,128,512]{2,1,0:T(8,128)(2,1)S(1)} collective-permute-done((bf16[4,128,512]{2,1,0:T(8,128)(2,1)S(1)}, bf16[4,128,512]{2,1,0:T(8,128)(2,1)S(1)}, u32[]{:S(2)}, u32[]{:S(2)}) %collective-permute-start.7) | collective-permute-done | bytes 524320 | tf_op jit(solution)/shard_map/ppermute | solution.py:42
  30.8 0.0 collective-permute-done.6.w1
  30.8 0.0 copy-done.1
  30.8 0.8 copy-done.16
  31.6 0.8 copy-done.17
  32.4 15.9 %project_keys.1 = (bf16[4096,512]{1,0:T(8,128)(2,1)}, bf16[2048,512]{1,0:T(8,128)(2,1)}, bf16[1024,512]{1,0:T(8,128)(2,1)}, bf16[512,512]{1,0:T(8,128)(2,1)}, bf...) custom-call(s32[17]{0:T(128)} %pad_add_fusion.1.place, ...), custom_call_target="tpu_custom_call" | custom-call | flops 8589934592 | bytes 27262976 | tf_op jit(solution)/shard_map/project_keys/pallas_call | solution.py:279
  48.3 1.4 %collective-permute-start.11 = (bf16[32,512]{1,0:T(8,128)(2,1)}, bf16[32,512]{1,0:T(8,128)(2,1)S(1)}, u32[]{:S(2)}, u32[]{:S(2)}) collective-permute-start(bf16[32,512]{1,0:T(8,128)(2,1)} %get-tuple-element.36), channel_id=1, source_target_pairs={{0,32},{8,40},{16,48},{24,56},{32,0},{40,8},{48,16},{56,24},{64,96... | collective-permute-start | bytes 98312 | tf_op jit(solution)/shard_map/ppermute | solution.py:46
  49.8 0.8 constant_dynamic-update-slice_fusion.1
  50.6 0.7 collective-permute-start.10
  51.3 1.3 %collective-permute-done.11.got_d = bf16[32,512]{1,0:T(8,128)(2,1)S(1)} collective-permute-done((bf16[32,512]{1,0:T(8,128)(2,1)}, bf16[32,512]{1,0:T(8,128)(2,1)S(1)}, u32[]{:S(2)}, u32[]{:S(2)}) %collective-permute-start.11) | collective-permute-done | bytes 32800 | tf_op jit(solution)/shard_map/ppermute | solution.py:46
  52.5 1.7 %collective-permute-start.9 = (bf16[256,512]{1,0:T(8,128)(2,1)}, bf16[256,512]{1,0:T(8,128)(2,1)S(1)}, u32[]{:S(2)}, u32[]{:S(2)}) collective-permute-start(bf16[256,512]{1,0:T(8,128)(2,1)} %get-tuple-element.34), channel_id=1, source_target_pairs={{0,8},{8,0},{16,24},{24,16},{32,40},{40,32},{48,56},{56,48},{64,72... | collective-permute-start | bytes 786440 | tf_op jit(solution)/shard_map/ppermute | solution.py:46
  54.3 0.0 collective-permute-done.5.w3
  54.3 1.8 %collective-permute-start.14 = (bf16[96,512]{1,0:T(8,128)(2,1)S(1)}, bf16[96,512]{1,0:T(8,128)(2,1)S(1)}, u32[]{:S(2)}, u32[]{:S(2)}) collective-permute-start(bf16[96,512]{1,0:T(8,128)(2,1)S(1)} %constant_dynamic-update-slice_fusion), channel_id=1, source_target_pairs={{0,24},{8,16},{16,8},{24,0},{32,56},{40,48},{48,40},{56,32},{64,88... | collective-permute-start | bytes 294920 | tf_op jit(solution)/shard_map/ppermute | solution.py:46
  56.1 0.0 collective-permute-done.4.w2
  56.1 1.5 %collective-permute-start.13 = (bf16[96,512]{1,0:T(8,128)(2,1)S(1)}, bf16[96,512]{1,0:T(8,128)(2,1)S(1)}, u32[]{:S(2)}, u32[]{:S(2)}) collective-permute-start(bf16[96,512]{1,0:T(8,128)(2,1)S(1)} %constant_dynamic-update-slice_fusion), channel_id=1, source_target_pairs={{0,16},{8,24},{16,0},{24,8},{32,48},{40,56},{48,32},{56,40},{64,80... | collective-permute-start | bytes 294920 | tf_op jit(solution)/shard_map/ppermute | solution.py:46
  57.6 0.0 collective-permute-done.3.w1
  57.6 0.8 collective-permute-start.12
  58.5 0.0 copy-done.2
  58.5 0.0 copy-done.4
  58.5 18.3 %project_queries.1 = (bf16[4096,256]{1,0:T(8,128)(2,1)}, bf16[2048,256]{1,0:T(8,128)(2,1)}, bf16[1024,256]{1,0:T(8,128)(2,1)}, f32[32,256]{1,0:T(8,128)}, bf16[5...) custom-call(s32[17]{0:T(128)} %pad_add_fusion.1.place, ...), custom_call_target="tpu_custom_call" | custom-call | flops 4294967296 | bytes 27262976 | tf_op jit(solution)/shard_map/project_queries/pallas_call | solution.py:306
  76.8 0.0 collective-permute-done.12.got_s
  76.8 0.0 collective-permute-done.14.got_e
  76.9 0.0 collective-permute-done.13.got_c
  76.9 0.0 collective-permute-done.10.got_b
  76.9 0.0 collective-permute-done.9.got_a
  76.9 0.0 copy-start.5
  76.9 0.5 copy-done.11
  77.5 0.0 copy-done.8
  77.5 0.1 copy-done.9
  77.5 0.0 copy-done.6
  77.6 0.1 copy-done.5
  77.7 12.6 %merge_levels.1 = (bf16[4096,256]{1,0:T(8,128)(2,1)}, f32[32,128]{1,0:T(8,128)}) custom-call(s32[3]{0:T(128)} %pad_add_fusion.edge, bf16[512,256]{1,0:T(8,128)(2,1)} %get-tuple-element.27.q3_in, bf16[512,512]{1,0:T(8,128)(2,1)} %get-tuple-element.28.kv3_in, bf16[256,256]{1,0:T(8,128)(2,1)} %get-tuple-element.29.q4_in, ...), custom_call_target="tpu_custom_call" | custom-call | flops 2147483648 | bytes 18874368 | tf_op jit(solution)/shard_map/merge_levels/pallas_call | solution.py:551
  90.3 0.1 collective-permute-start.15
  90.4 1.4 %collective-permute-done.15 = f32[32,128]{1,0:T(8,128)S(1)} collective-permute-done((f32[32,128]{1,0:T(8,128)}, f32[32,128]{1,0:T(8,128)S(1)}, u32[]{:S(2)}, u32[]{:S(2)}) %collective-permute-start.15) | collective-permute-done | bytes 16416 | tf_op jit(solution)/shard_map/ppermute | solution.py:55
  91.8 0.7 add.49.s0
  92.5 3.2 %collective-permute-start.18 = (f32[32,128]{1,0:T(8,128)S(1)}, f32[32,128]{1,0:T(8,128)S(1)}, u32[]{:S(2)}, u32[]{:S(2)}) collective-permute-start(f32[32,128]{1,0:T(8,128)S(1)} %add.49.s0), channel_id=1, source_target_pairs={{0,4},{1,5},{2,6},{3,7},{4,0},{5,1},{6,2},{7,3},{8,12},{9,13},{10,... | collective-permute-start | bytes 49160 | tf_op jit(solution)/shard_map/ppermute | solution.py:55
  95.7 1.0 collective-permute-start.17
  96.8 1.0 collective-permute-start.16
  97.7 0.0 collective-permute-done.18.s3
  97.8 1.7 %collective-permute-done.17.s2 = f32[32,128]{1,0:T(8,128)S(1)} collective-permute-done((f32[32,128]{1,0:T(8,128)S(1)}, f32[32,128]{1,0:T(8,128)S(1)}, u32[]{:S(2)}, u32[]{:S(2)}) %collective-permute-start.17) | collective-permute-done | bytes 16416 | tf_op jit(solution)/shard_map/ppermute | solution.py:55
  99.5 2.3 %collective-permute-done.16.s1 = f32[32,128]{1,0:T(8,128)S(1)} collective-permute-done((f32[32,128]{1,0:T(8,128)S(1)}, f32[32,128]{1,0:T(8,128)S(1)}, u32[]{:S(2)}, u32[]{:S(2)}) %collective-permute-start.16) | collective-permute-done | bytes 16416 | tf_op jit(solution)/shard_map/ppermute | solution.py:55
  101.7 0.6 copy-done.14
  102.3 3.5 %norm.1 = bf16[4096,256]{1,0:T(8,128)(2,1)} custom-call(bf16[4096,256]{1,0:T(8,128)(2,1)} %get-tuple-element.43.attention, f32[32,128]{1,0:T(8,128)} %copy-done.10, f32[32,128]{1,0:T(8,128)} %copy-done.14, f32[32,128]{1,0:T(8,128)} %copy-done.13, f32[32,128]{1,0:T(8,128)} %copy-done.12, f32[1,256]{1,0:T(1,128)} %bitcast.16), custom_call_target="tpu_custom_call" | custom-call | tf_op jit(solution)/shard_map/norm/pallas_call | solution.py:603
  (25 shorter events, 0.0 us)
Async XLA Ops:
  1.6 7.8 %collective-permute-start.2 = (bf16[128,768]{1,0:T(8,128)(2,1)}, bf16[128,768]{1,0:T(8,128)(2,1)S(1)}, u32[]{:S(2)}, u32[]{:S(2)}) collective-permute-start(bf16[128,768]{1,0:T(8,128)(2,1)} %join_weights.1), channel_id=1, source_target_pairs={{0,16},{1,65},{2,18},{3,67},{4,20},{5,69},{6,22},{7,71},{8,24},{9,... | collective-permute-start | bytes 589832 | tf_op jit(solution)/shard_map/ppermute | solution.py:42
  5.6 7.0 %collective-permute-start.1 = (bf16[128,768]{1,0:T(8,128)(2,1)}, bf16[128,768]{1,0:T(8,128)(2,1)S(1)}, u32[]{:S(2)}, u32[]{:S(2)}) collective-permute-start(bf16[128,768]{1,0:T(8,128)(2,1)} %join_weights.1), channel_id=1, source_target_pairs={{0,24},{1,97},{2,26},{3,99},{4,28},{5,101},{6,30},{7,103},{8,0},{9... | collective-permute-start | bytes 589832 | tf_op jit(solution)/shard_map/ppermute | solution.py:42
  6.3 7.1 %collective-permute-start = (bf16[128,768]{1,0:T(8,128)(2,1)}, bf16[128,768]{1,0:T(8,128)(2,1)S(1)}, u32[]{:S(2)}, u32[]{:S(2)}) collective-permute-start(bf16[128,768]{1,0:T(8,128)(2,1)} %join_weights.1), channel_id=1, source_target_pairs={{0,8},{1,33},{2,10},{3,35},{4,12},{5,37},{6,14},{7,39},{8,16},{9,4... | collective-permute-start | bytes 589832 | tf_op jit(solution)/shard_map/ppermute | solution.py:42
  14.3 16.5 %copy-start.1 = (bf16[4,128,512]{2,1,0:T(8,128)(2,1)}, bf16[4,128,512]{2,1,0:T(8,128)(2,1)S(1)}, u32[]{:S(2)}) copy-start(bf16[4,128,512]{2,1,0:T(8,128)(2,1)S(1)} %pad_maximum_fusion.w0) | copy-start | bytes 1572868
  14.3 10.9 %collective-permute-start.8 = (bf16[4,128,512]{2,1,0:T(8,128)(2,1)S(1)}, bf16[4,128,512]{2,1,0:T(8,128)(2,1)S(1)}, u32[]{:S(2)}, u32[]{:S(2)}) collective-permute-start(bf16[4,128,512]{2,1,0:T(8,128)(2,1)S(1)} %pad_maximum_fusion.w0), channel_id=1, source_target_pairs={{0,64},{1,17},{2,66},{3,19},{4,68},{5,21},{6,70},{7,23},{8,72},{9,... | collective-permute-start | bytes 1572872 | tf_op jit(solution)/shard_map/ppermute | solution.py:42
  17.4 13.4 %collective-permute-start.7 = (bf16[4,128,512]{2,1,0:T(8,128)(2,1)S(1)}, bf16[4,128,512]{2,1,0:T(8,128)(2,1)S(1)}, u32[]{:S(2)}, u32[]{:S(2)}) collective-permute-start(bf16[4,128,512]{2,1,0:T(8,128)(2,1)S(1)} %pad_maximum_fusion.w0), channel_id=1, source_target_pairs={{0,96},{1,25},{2,98},{3,27},{4,100},{5,29},{6,102},{7,31},{8,104},... | collective-permute-start | bytes 1572872 | tf_op jit(solution)/shard_map/ppermute | solution.py:42
  18.6 12.3 %collective-permute-start.6 = (bf16[4,128,512]{2,1,0:T(8,128)(2,1)S(1)}, bf16[4,128,512]{2,1,0:T(8,128)(2,1)S(1)}, u32[]{:S(2)}, u32[]{:S(2)}) collective-permute-start(bf16[4,128,512]{2,1,0:T(8,128)(2,1)S(1)} %pad_maximum_fusion.w0), channel_id=1, source_target_pairs={{0,32},{1,9},{2,34},{3,11},{4,36},{5,13},{6,38},{7,15},{8,40},{9,1... | collective-permute-start | bytes 1572872 | tf_op jit(solution)/shard_map/ppermute | solution.py:42
  21.6 26.7 %copy-start = (bf16[4,128,256]{2,1,0:T(8,128)(2,1)}, bf16[4,128,256]{2,1,0:T(8,128)(2,1)S(1)}, u32[]{:S(2)}) copy-start(bf16[4,128,256]{2,1,0:T(8,128)(2,1)S(1)} %pad_maximum_fusion.3.w0) | copy-start | bytes 786436
  21.7 32.6 %collective-permute-start.5 = (bf16[4,128,256]{2,1,0:T(8,128)(2,1)S(1)}, bf16[4,128,256]{2,1,0:T(8,128)(2,1)S(1)}, u32[]{:S(2)}, u32[]{:S(2)}) collective-permute-start(bf16[4,128,256]{2,1,0:T(8,128)(2,1)S(1)} %pad_maximum_fusion.3.w0), channel_id=1, source_target_pairs={{0,64},{1,17},{2,66},{3,19},{4,68},{5,21},{6,70},{7,23},{8,72},{9,... | collective-permute-start | bytes 786440 | tf_op jit(solution)/shard_map/ppermute | solution.py:42
  22.4 33.7 %collective-permute-start.4 = (bf16[4,128,256]{2,1,0:T(8,128)(2,1)S(1)}, bf16[4,128,256]{2,1,0:T(8,128)(2,1)S(1)}, u32[]{:S(2)}, u32[]{:S(2)}) collective-permute-start(bf16[4,128,256]{2,1,0:T(8,128)(2,1)S(1)} %pad_maximum_fusion.3.w0), channel_id=1, source_target_pairs={{0,96},{1,25},{2,98},{3,27},{4,100},{5,29},{6,102},{7,31},{8,104},... | collective-permute-start | bytes 786440 | tf_op jit(solution)/shard_map/ppermute | solution.py:42
  25.2 5.7 %copy-start.15 = (bf16[4,128,512]{2,1,0:T(8,128)(2,1)}, bf16[4,128,512]{2,1,0:T(8,128)(2,1)S(1)}, u32[]{:S(2)}) copy-start(bf16[4,128,512]{2,1,0:T(8,128)(2,1)S(1)} %collective-permute-done.8.w3) | copy-start | bytes 1572868
  25.2 32.5 %collective-permute-start.3 = (bf16[4,128,256]{2,1,0:T(8,128)(2,1)S(1)}, bf16[4,128,256]{2,1,0:T(8,128)(2,1)S(1)}, u32[]{:S(2)}, u32[]{:S(2)}) collective-permute-start(bf16[4,128,256]{2,1,0:T(8,128)(2,1)S(1)} %pad_maximum_fusion.3.w0), channel_id=1, source_target_pairs={{0,32},{1,9},{2,34},{3,11},{4,36},{5,13},{6,38},{7,15},{8,40},{9,1... | collective-permute-start | bytes 786440 | tf_op jit(solution)/shard_map/ppermute | solution.py:42
  30.8 0.8 copy-start.16
  31.6 0.8 copy-start.17
  48.3 4.2 %collective-permute-start.11 = (bf16[32,512]{1,0:T(8,128)(2,1)}, bf16[32,512]{1,0:T(8,128)(2,1)S(1)}, u32[]{:S(2)}, u32[]{:S(2)}) collective-permute-start(bf16[32,512]{1,0:T(8,128)(2,1)} %get-tuple-element.36), channel_id=1, source_target_pairs={{0,32},{8,40},{16,48},{24,56},{32,0},{40,8},{48,16},{56,24},{64,96... | collective-permute-start | bytes 98312 | tf_op jit(solution)/shard_map/ppermute | solution.py:46
  50.6 26.3 %collective-permute-start.10 = (bf16[128,512]{1,0:T(8,128)(2,1)}, bf16[128,512]{1,0:T(8,128)(2,1)S(1)}, u32[]{:S(2)}, u32[]{:S(2)}) collective-permute-start(bf16[128,512]{1,0:T(8,128)(2,1)} %get-tuple-element.35), channel_id=1, source_target_pairs={{8,16},{24,32},{40,48},{56,64},{72,80},{88,96},{104,112},{16,8},{3... | collective-permute-start | bytes 393224 | tf_op jit(solution)/shard_map/ppermute | solution.py:51
  52.5 24.3 %copy-start.7 = (bf16[32,512]{1,0:T(8,128)(2,1)}, bf16[32,512]{1,0:T(8,128)(2,1)S(1)}, u32[]{:S(2)}) copy-start(bf16[32,512]{1,0:T(8,128)(2,1)S(1)} %collective-permute-done.11.got_d) | copy-start | bytes 98308
  52.5 24.4 %collective-permute-start.9 = (bf16[256,512]{1,0:T(8,128)(2,1)}, bf16[256,512]{1,0:T(8,128)(2,1)S(1)}, u32[]{:S(2)}, u32[]{:S(2)}) collective-permute-start(bf16[256,512]{1,0:T(8,128)(2,1)} %get-tuple-element.34), channel_id=1, source_target_pairs={{0,8},{8,0},{16,24},{24,16},{32,40},{40,32},{48,56},{56,48},{64,72... | collective-permute-start | bytes 786440 | tf_op jit(solution)/shard_map/ppermute | solution.py:46
  54.3 4.2 %copy-start.2 = (bf16[4,128,256]{2,1,0:T(8,128)(2,1)}, bf16[4,128,256]{2,1,0:T(8,128)(2,1)S(1)}, u32[]{:S(2)}) copy-start(bf16[4,128,256]{2,1,0:T(8,128)(2,1)S(1)} %collective-permute-done.5.w3) | copy-start | bytes 786436
  54.3 22.6 %collective-permute-start.14 = (bf16[96,512]{1,0:T(8,128)(2,1)S(1)}, bf16[96,512]{1,0:T(8,128)(2,1)S(1)}, u32[]{:S(2)}, u32[]{:S(2)}) collective-permute-start(bf16[96,512]{1,0:T(8,128)(2,1)S(1)} %constant_dynamic-update-slice_fusion), channel_id=1, source_target_pairs={{0,24},{8,16},{16,8},{24,0},{32,56},{40,48},{48,40},{56,32},{64,88... | collective-permute-start | bytes 294920 | tf_op jit(solution)/shard_map/ppermute | solution.py:46
  56.1 2.4 %copy-start.3 = (bf16[4,128,256]{2,1,0:T(8,128)(2,1)}, bf16[4,128,256]{2,1,0:T(8,128)(2,1)S(1)}, u32[]{:S(2)}) copy-start(bf16[4,128,256]{2,1,0:T(8,128)(2,1)S(1)} %collective-permute-done.4.w2) | copy-start | bytes 786436
  56.1 20.8 %collective-permute-start.13 = (bf16[96,512]{1,0:T(8,128)(2,1)S(1)}, bf16[96,512]{1,0:T(8,128)(2,1)S(1)}, u32[]{:S(2)}, u32[]{:S(2)}) collective-permute-start(bf16[96,512]{1,0:T(8,128)(2,1)S(1)} %constant_dynamic-update-slice_fusion), channel_id=1, source_target_pairs={{0,16},{8,24},{16,0},{24,8},{32,48},{40,56},{48,32},{56,40},{64,80... | collective-permute-start | bytes 294920 | tf_op jit(solution)/shard_map/ppermute | solution.py:46
  57.6 0.8 copy-start.4
  57.6 19.2 %collective-permute-start.12 = (bf16[32,512]{1,0:T(8,128)(2,1)S(1)}, bf16[32,512]{1,0:T(8,128)(2,1)S(1)}, u32[]{:S(2)}, u32[]{:S(2)}) collective-permute-start(bf16[32,512]{1,0:T(8,128)(2,1)S(1)} %collective-permute-done.11.got_d), channel_id=1, source_target_pairs={{0,8},{8,0},{16,24},{24,16},{32,40},{40,32},{48,56},{56,48},{64,72... | collective-permute-start | bytes 98312 | tf_op jit(solution)/shard_map/ppermute | solution.py:46
  76.8 0.6 copy-start.11
  76.9 0.6 copy-start.8
  76.9 0.7 copy-start.9
  76.9 0.7 copy-start.6
  76.9 0.7 copy-start.5
  90.3 1.5 %collective-permute-start.15 = (f32[32,128]{1,0:T(8,128)}, f32[32,128]{1,0:T(8,128)S(1)}, u32[]{:S(2)}, u32[]{:S(2)}) collective-permute-start(f32[32,128]{1,0:T(8,128)} %get-tuple-element.44), channel_id=1, source_target_pairs={{0,1},{1,0},{2,3},{3,2},{4,5},{5,4},{6,7},{7,6},{8,9},{9,8},{10,11... | collective-permute-start | bytes 49160 | tf_op jit(solution)/shard_map/ppermute | solution.py:55
  92.5 9.2 %copy-start.10 = (f32[32,128]{1,0:T(8,128)}, f32[32,128]{1,0:T(8,128)S(1)}, u32[]{:S(2)}) copy-start(f32[32,128]{1,0:T(8,128)S(1)} %add.49.s0) | copy-start | bytes 49156
  92.5 5.2 %collective-permute-start.18 = (f32[32,128]{1,0:T(8,128)S(1)}, f32[32,128]{1,0:T(8,128)S(1)}, u32[]{:S(2)}, u32[]{:S(2)}) collective-permute-start(f32[32,128]{1,0:T(8,128)S(1)} %add.49.s0), channel_id=1, source_target_pairs={{0,4},{1,5},{2,6},{3,7},{4,0},{5,1},{6,2},{7,3},{8,12},{9,13},{10,... | collective-permute-start | bytes 49160 | tf_op jit(solution)/shard_map/ppermute | solution.py:55
  95.7 3.7 %collective-permute-start.17 = (f32[32,128]{1,0:T(8,128)S(1)}, f32[32,128]{1,0:T(8,128)S(1)}, u32[]{:S(2)}, u32[]{:S(2)}) collective-permute-start(f32[32,128]{1,0:T(8,128)S(1)} %add.49.s0), channel_id=1, source_target_pairs={{0,6},{1,7},{2,0},{3,1},{4,2},{5,3},{6,4},{7,5},{8,14},{9,15},{10,... | collective-permute-start | bytes 49160 | tf_op jit(solution)/shard_map/ppermute | solution.py:55
  96.8 4.9 %collective-permute-start.16 = (f32[32,128]{1,0:T(8,128)S(1)}, f32[32,128]{1,0:T(8,128)S(1)}, u32[]{:S(2)}, u32[]{:S(2)}) collective-permute-start(f32[32,128]{1,0:T(8,128)S(1)} %add.49.s0), channel_id=1, source_target_pairs={{0,2},{1,3},{2,4},{3,5},{4,6},{5,7},{6,0},{7,1},{8,10},{9,11},{10,... | collective-permute-start | bytes 49160 | tf_op jit(solution)/shard_map/ppermute | solution.py:55
  97.8 4.0 %copy-start.12 = (f32[32,128]{1,0:T(8,128)}, f32[32,128]{1,0:T(8,128)S(1)}, u32[]{:S(2)}) copy-start(f32[32,128]{1,0:T(8,128)S(1)} %collective-permute-done.18.s3) | copy-start | bytes 49156
  99.5 2.3 %copy-start.13 = (f32[32,128]{1,0:T(8,128)}, f32[32,128]{1,0:T(8,128)S(1)}, u32[]{:S(2)}) copy-start(f32[32,128]{1,0:T(8,128)S(1)} %collective-permute-done.17.s2) | copy-start | bytes 49156
  101.7 0.6 copy-start.14

commit v2 on v1

--- a/solution.py
+++ b/solution.py
@@ -22,6 +22,7 @@
 CHUNK = 512
 CHUNKS = TOKENS // CHUNK
 RUNS = TOKENS // TM
+VMEM_LIMIT = 32 * 2**20
 GROUP = 8
 
 
@@ -118,33 +119,19 @@
         copy.wait()
 
 
-def moves(pairs, sems):
-    return [pltpu.make_async_copy(a, b, sems.at[n]) for n, (a, b) in enumerate(pairs)]
-
-
-def start_projection(place, hidden, pieces, h_all, w_all, h_sem, w_sem):
-    for outer, piece in enumerate(pieces):
-        for inner in range(SIDE):
-            slot = outer * SIDE + inner
-            at = pl.multiple_of(place[slot] * 128, 128)
-            pltpu.make_async_copy(piece.at[inner], w_all.at[pl.ds(at, 128)], w_sem.at[slot]).start()
-    for index in range(2):
-        part_of(hidden, h_all, h_sem, index, CHUNK).start()
-
-
-def wait_weights(pieces, w_all, w_sem):
-    for slot in range(16):
-        pltpu.make_async_copy(
-            pieces[slot // SIDE].at[slot % SIDE], w_all.at[pl.ds(0, 128)], w_sem.at[slot]
-        ).wait()
-
-
 def next_rows(hidden, h_all, h_sem, index):
     part_of(hidden, h_all, h_sem, index, CHUNK).wait()
 
     @pl.when(index < CHUNKS - 2)
     def _():
         part_of(hidden, h_all, h_sem, index + 2, CHUNK).start()
+
+
+def place_weights(place, pieces, w_all):
+    for outer, piece in enumerate(pieces):
+        for inner in range(SIDE):
+            at = pl.multiple_of(place[outer * SIDE + inner] * 128, 128)
+            w_all[pl.ds(at, 128), :] = piece[inner]
 
 
 def pool_block(p_fine, rows, block, l1, l2, l3):
@@ -164,21 +151,12 @@
 
 
 def keys_kernel(
-    place, hidden, w0, w1, w2, w3,
-    full_out, l1_out, l2_out, l3_out, l4_out, a_out, b_out, six_out, seven_out,
-    h_all, w_all, full, l1, l2, l3, l4, send_a, send_b, six, seven, h_sem, w_sem, out_sem, last_sem,
+    place, hidden, w0, w1, w2, w3, full, l1, l2, l3, l4, send_a, send_b, six, seven, h_all, w_all, h_sem
 ):
-    pieces = (w0, w1, w2, w3)
-    start_projection(place, hidden, pieces, h_all, w_all, h_sem, w_sem)
+    for index in range(2):
+        part_of(hidden, h_all, h_sem, index, CHUNK).start()
+    place_weights(place, (w0, w1, w2, w3), w_all)
     p_fine = pool_matrix(112, 128, (1, 2, 3))
-    wait_weights(pieces, w_all, w_sem)
-
-    def sends(index):
-        made = zip((full, l1, l2, l3), (full_out, l1_out, l2_out, l3_out), (1, 2, 4, 8))
-        return [
-            part_of(v, out, out_sem.at[n], index, CHUNK // ratio)
-            for n, (v, out, ratio) in enumerate(made)
-        ]
 
     @pl.loop(0, CHUNKS)
     def _(index):
@@ -188,7 +166,6 @@
         full[at, :] = rows
         for part in range(CHUNK // 128):
             pool_block(p_fine, rows[part * 128 : part * 128 + 128], index * (CHUNK // 128) + part, l1, l2, l3)
-        start_all(sends(index))
 
     l4[...], five, six[...], seven[...] = pool_runs(l3)
     odd = place[16] == 1
@@ -196,39 +173,23 @@
     send_a[:128, :] = jnp.where(odd, low, high)
     send_b[...] = jnp.where(odd, high, low)
     send_a[128:, :] = five
-    pairs = ((l4, l4_out), (send_a, a_out), (send_b, b_out), (six, six_out), (seven, seven_out))
-    last = moves(pairs, last_sem)
-    start_all(last)
-
-    @pl.loop(0, CHUNKS)
-    def _(index):
-        wait_all(sends(index))
-
-    wait_all(last)
 
 
 def queries_kernel(
     place, hidden, w0, w1, w2, w3, kv1, kv2,
-    full_out, o1_out, o2_out, virtual_out, q3_out, q4_out, q5_out, q6_out, q7_out,
-    h_all, w_all, full, l1, l2, l3, q4, q5, q6, q7, kv1_all, kv2_all, o1, o2, virtual,
-    h_sem, w_sem, kv_sem, out_sem, last_sem,
+    full, o1, o2, virtual, l3, q4, q5, q6, q7,
+    h_all, w_all, l1, l2, h_sem,
 ):
-    pieces = (w0, w1, w2, w3)
-    start_projection(place, hidden, pieces, h_all, w_all, h_sem, w_sem)
+    for index in range(2):
+        part_of(hidden, h_all, h_sem, index, CHUNK).start()
+    place_weights(place, (w0, w1, w2, w3), w_all)
     p_fine = pool_matrix(112, 128, (1, 2, 3))
-    wait_weights(pieces, w_all, w_sem)
-    arriving = [parts_of(kv1, kv1_all, kv_sem.at[0], RUNS), parts_of(kv2, kv2_all, kv_sem.at[1], RUNS)]
-    leaving = [
-        parts_of(mine, out, out_sem.at[n], RUNS)
-        for n, (mine, out) in enumerate(((full, full_out), (o1, o1_out), (o2, o2_out)))
-    ]
 
     def attend_run(run):
-        wait_all([group[run] for group in arriving])
         triples, places = [], []
         for head in range(HEADS):
             k, v = (slice(i * 256 + head * 128, i * 256 + head * 128 + 128) for i in range(2))
-            for q_all, kv_all, out, count in ((l1, kv1_all, o1, 4), (l2, kv2_all, o2, 2)):
+            for q_all, kv_all, out, count in ((l1, kv1, o1, 4), (l2, kv2, o2, 2)):
                 for block in range(run * count, run * count + count):
                     mine = slice(block * 128, block * 128 + 128)
                     its = slice((block ^ 1) * 128, (block ^ 1) * 128 + 128)
@@ -249,48 +210,32 @@
     for run in range(RUNS):
         for index in range(run * (TM // CHUNK), (run + 1) * (TM // CHUNK)):
             next_rows(hidden, h_all, h_sem, jnp.int32(index))
-        start_all([group[run] for group in arriving])
         at = slice(run * TM, run * TM + TM)
-        rows = (dot(h_all[at, :], w_all[...]) * SCALE).astype(BF)
+        rows = dot(h_all[at, :], w_all[...]).astype(BF)
         full[at, :] = rows
-        leaving[0][run].start()
         for part in range(TM // 128):
             pool_block(p_fine, rows[part * 128 : part * 128 + 128], run * (TM // 128) + part, l1, l2, l3)
         if run:
             attend_run(run - 1)
-            leaving[1][run - 1].start()
-            leaving[2][run - 1].start()
     q4[...], q5[...], q6[...], q7[...] = pool_runs(l3)
     attend_run(RUNS - 1)
-    leaving[1][RUNS - 1].start()
-    leaving[2][RUNS - 1].start()
-    pairs = ((virtual, virtual_out), (l3, q3_out), (q4, q4_out), (q5, q5_out), (q6, q6_out), (q7, q7_out))
-    last = moves(pairs, last_sem)
-    start_all(last)
-    for group in leaving:
-        wait_all(group)
-    wait_all(last)
 
 
 def project_keys(place, hidden, pieces):
     anywhere = pl.BlockSpec(memory_space=pl.ANY)
-    levels = [(TOKENS >> level, 512) for level in range(5)]
-    small = [(256, 512), (128, 512), (64, 512), (32, 512)]
+    local = pl.BlockSpec(memory_space=pltpu.VMEM)
+    sizes = [TOKENS >> level for level in range(5)] + [256, 128, 64, 32]
     return pl.pallas_call(
         keys_kernel,
-        in_specs=[pl.BlockSpec(memory_space=pltpu.SMEM)] + [anywhere] * 5,
-        out_specs=[anywhere] * 9,
-        out_shape=[jax.ShapeDtypeStruct(size, BF) for size in levels + small],
+        in_specs=[pl.BlockSpec(memory_space=pltpu.SMEM), anywhere] + [local] * 4,
+        out_specs=[local] * 9,
+        out_shape=[jax.ShapeDtypeStruct((size, 512), BF) for size in sizes],
         scratch_shapes=[
             pltpu.VMEM((TOKENS, D), BF),
             pltpu.VMEM((D, 512), BF),
-            *[pltpu.VMEM(size, BF) for size in levels + small],
             pltpu.SemaphoreType.DMA((CHUNKS,)),
-            pltpu.SemaphoreType.DMA((16,)),
-            pltpu.SemaphoreType.DMA((4, CHUNKS)),
-            pltpu.SemaphoreType.DMA((5,)),
         ],
-        compiler_params=pltpu.CompilerParams(vmem_limit_bytes=56 * 2**20),
+        compiler_params=pltpu.CompilerParams(vmem_limit_bytes=VMEM_LIMIT),
         name="project_keys",
         cost_estimate=pl.CostEstimate(
             flops=2 * TOKENS * D * 512, bytes_accessed=26 * 2**20, transcendentals=0
@@ -300,33 +245,24 @@
 
 def project_queries(place, hidden, pieces, kv1, kv2):
     anywhere = pl.BlockSpec(memory_space=pl.ANY)
+    local = pl.BlockSpec(memory_space=pltpu.VMEM)
     shape = jax.ShapeDtypeStruct
     small = [shape((size, 256), BF) for size in (512, 256, 128, 64, 32)]
-    buffer = lambda *size: pltpu.VMEM(size, BF)
     return pl.pallas_call(
         queries_kernel,
-        in_specs=[pl.BlockSpec(memory_space=pltpu.SMEM)] + [anywhere] * 7,
-        out_specs=[anywhere] * 9,
+        in_specs=[pl.BlockSpec(memory_space=pltpu.SMEM), anywhere] + [local] * 6,
+        out_specs=[local] * 9,
         out_shape=[shape((TOKENS, 256), BF), shape((2048, 256), BF), shape((1024, 256), BF)]
         + [shape((32, 256), F32)]
         + small,
         scratch_shapes=[
-            buffer(TOKENS, D),
-            buffer(D, 256),
-            *[buffer(TOKENS >> level, 256) for level in range(4)],
-            *[buffer(size, 256) for size in (256, 128, 64, 32)],
-            buffer(2048, 512),
-            buffer(1024, 512),
-            buffer(2048, 256),
-            buffer(1024, 256),
-            pltpu.VMEM((32, 256), F32),
+            pltpu.VMEM((TOKENS, D), BF),
+            pltpu.VMEM((D, 256), BF),
+            pltpu.VMEM((2048, 256), BF),
+            pltpu.VMEM((1024, 256), BF),
             pltpu.SemaphoreType.DMA((CHUNKS,)),
-            pltpu.SemaphoreType.DMA((16,)),
-            pltpu.SemaphoreType.DMA((2, RUNS)),
-            pltpu.SemaphoreType.DMA((3, RUNS)),
-            pltpu.SemaphoreType.DMA((6,)),
         ],
-        compiler_params=pltpu.CompilerParams(vmem_limit_bytes=56 * 2**20),
+        compiler_params=pltpu.CompilerParams(vmem_limit_bytes=VMEM_LIMIT),
         name="project_queries",
         cost_estimate=pl.CostEstimate(
             flops=2 * TOKENS * D * 256, bytes_accessed=26 * 2**20, transcendentals=2**20
@@ -344,7 +280,7 @@
 
 
 def attend_all(triples):
-    scores = [dot_t(queries, key_rows) for queries, key_rows, _ in triples]
+    scores = [dot_t(queries, key_rows) * SCALE for queries, key_rows, _ in triples]
     highest = [jnp.max(s, axis=1, keepdims=True) for s in scores]
     weights = [jnp.exp2(s - h).astype(BF) for s, h in zip(scores, highest)]
     both = [dot(w, with_ones(values)) for w, (_, _, values) in zip(weights, triples)]
@@ -359,7 +295,7 @@
 
 
 def merged(parts, found):
-    scores = [dot_t(queries, key_rows) for queries, key_rows, *_ in parts]
+    scores = [dot_t(queries, key_rows) * SCALE for queries, key_rows, *_ in parts]
     scores = [s if p[5] is None else s + p[5] for s, p in zip(scores, parts)]
     coarse = [jnp.where(found, p[3], GONE) for p in parts]
     highest = [
@@ -377,45 +313,15 @@
 
 
 def fine_kernel(
-    edge, q3_in, kv3_in, q4_in, kv4_in, q5_in, q6_in, q7_in, got_a, got_b, got_d, got_s, got_c, got_e,
-    virtual_in, q, kv, o1, o2, out, squares,
-    q3, kv3, q4, kv4, q5, q6, q7, kv5, kv6, kv7, virtual,
-    q_all, kv_all, o1_all, o2_all, o3, virtual_3, out_all, first_sem, in_sem, out_sem,
+    edge, q3, kv3, q4, kv4, q5, q6, q7, got_a, got_b, got_d, got_s, got_c, got_e, virtual, q, kv, o1, o2,
+    out, squares, o3, virtual_3,
 ):
     odd = edge[0] == 1
-    above, below = 0, 128 + TOKENS
-    at_a = pl.ds(pl.multiple_of(jnp.where(odd, above, below), 128), 128)
-    at_b = pl.ds(pl.multiple_of(jnp.where(odd, below, above), 128), 128)
-    early = moves(
-        (
-            (q4_in, q4),
-            (kv4_in, kv4),
-            (q5_in, q5),
-            (q6_in, q6),
-            (q7_in, q7),
-            (got_a.at[pl.ds(128, 128)], kv5),
-            (got_c.at[pl.ds(0, 64)], kv6.at[pl.ds(0, 64)]),
-            (got_e.at[pl.ds(0, 64)], kv6.at[pl.ds(64, 64)]),
-            (got_d, kv7.at[pl.ds(0, 32)]),
-            (got_s, kv7.at[pl.ds(32, 32)]),
-            (got_c.at[pl.ds(64, 32)], kv7.at[pl.ds(64, 32)]),
-            (got_e.at[pl.ds(64, 32)], kv7.at[pl.ds(96, 32)]),
-            (q3_in, q3),
-            (kv3_in, kv3),
-            (virtual_in, virtual),
-            (got_a.at[pl.ds(0, 128)], kv_all.at[at_a]),
-            (got_b, kv_all.at[at_b]),
-        ),
-        first_sem,
-    )
-    inner = kv_all.at[pl.ds(128, TOKENS)]
-    groups = ((q, q_all), (kv, inner), (o1, o1_all), (o2, o2_all))
-    arriving = [parts_of(a, b, in_sem.at[n], RUNS) for n, (a, b) in enumerate(groups)]
-    start_all(early)
-    for part in range(2):
-        start_all([group[part] for group in arriving])
-    wait_all(early)
-
+    kv5 = got_a.at[pl.ds(128, 128)]
+    kv6 = jnp.concatenate([got_c[:64, :], got_e[:64, :]], 0)
+    kv7 = jnp.concatenate([got_d[...], got_s[...], got_c[64:, :], got_e[64:, :]], 0)
+    above = jnp.where(odd, got_a[:128, :], got_b[...])
+    below = jnp.where(odd, got_b[...], got_a[:128, :])
     found = level_matches(128, 4, (4, 5, 6, 7), 1)
     triples = []
     for head in range(HEADS):
@@ -473,25 +379,9 @@
 
     found = level_matches(128, 1, (1, 2, 3), 1)
     row = iota((8, 128), 0)
-    arriving[1][0].wait()
 
     @pl.loop(0, RUNS)
     def _(step):
-        part_of(q, q_all, in_sem.at[0], step, TM).wait()
-        part_of(o1, o1_all, in_sem.at[2], step, TM // 2).wait()
-        part_of(o2, o2_all, in_sem.at[3], step, TM // 4).wait()
-
-        @pl.when(step < RUNS - 2)
-        def _():
-            part_of(q, q_all, in_sem.at[0], step + 2, TM).start()
-            part_of(kv, inner, in_sem.at[1], step + 2, TM).start()
-            part_of(o1, o1_all, in_sem.at[2], step + 2, TM // 2).start()
-            part_of(o2, o2_all, in_sem.at[3], step + 2, TM // 4).start()
-
-        @pl.when(step < RUNS - 1)
-        def _():
-            part_of(kv, inner, in_sem.at[1], step + 1, TM).wait()
-
         first = jnp.where((step == 0) & (edge[1] == 1), GONE, 0.0)
         last = jnp.where((step == 3) & (edge[2] == 1), GONE, 0.0)
         gathered = jnp.zeros((8, 128), F32)
@@ -507,18 +397,33 @@
                 bias = None
                 if block == 0:
                     bias = jnp.where(iota((1, 384), 1) < 128, first, 0.0)
+                    before = pl.multiple_of(jnp.maximum(at - 128, 0), 128)
+                    window = jnp.concatenate(
+                        [jnp.where(step == 0, above, kv[pl.ds(before, 128), :]), kv[pl.ds(at, 256), :]], 0
+                    )
+                elif block == 7:
+                    after = pl.multiple_of(jnp.minimum(at + 128, TOKENS - 128), 128)
+                    window = jnp.concatenate(
+                        [
+                            kv[pl.ds(pl.multiple_of(at - 128, 128), 256), :],
+                            jnp.where(step == RUNS - 1, below, kv[pl.ds(after, 128), :]),
+                        ],
+                        0,
+                    )
+                else:
+                    window = kv.at[pl.ds(pl.multiple_of(at - 128, 128), 384)]
                 if block == 7:
                     bias = jnp.where(iota((1, 384), 1) >= 256, last, 0.0)
                 for head in range(HEADS):
                     c, gv = (slice(i * 256 + head * 128, i * 256 + head * 128 + 128) for i in range(2))
                     values = jnp.concatenate(
-                        [o1_all[at1, c], o2_all[at2, c], o3[at3, c], jnp.zeros((16, DH), BF)], 0
+                        [o1[at1, c], o2[at2, c], o3[at3, c], jnp.zeros((16, DH), BF)], 0
                     )
                     parts.append(
                         (
-                            q_all[pl.ds(at, 128), c],
-                            kv_all[pl.ds(at, 384), c],
-                            kv_all[pl.ds(at, 384), gv],
+                            q[pl.ds(at, 128), c],
+                            window[:, c],
+                            window[:, gv],
                             levels[block : block + 1, c],
                             values,
                             bias,
@@ -531,48 +436,23 @@
                 for head in range(HEADS):
                     weighted, total, _ = done[index * HEADS + head]
                     attention = quotient(weighted, total)
-                    out_all[at, head * 128 : head * 128 + 128] = attention.astype(BF)
+                    out[at, head * 128 : head * 128 + 128] = attention.astype(BF)
                     sums = sums + attention * attention
                 token_sums = dot_t(jnp.ones((8, DH), F32), sums)
                 gathered = jnp.where(row == block, token_sums, gathered)
         squares[pl.ds(pl.multiple_of(step * 8, 8), 8), :] = gathered
-        part_of(out_all, out, out_sem, step, TM).start()
-
-    @pl.loop(0, 4)
-    def _(step):
-        part_of(out_all, out, out_sem, step, TM).wait()
 
 
 def fine(edge, *arrays):
-    anywhere = pl.BlockSpec(memory_space=pl.ANY)
     local = pl.BlockSpec(memory_space=pltpu.VMEM)
     shape = jax.ShapeDtypeStruct
-    buffer = lambda *size: pltpu.VMEM(size, BF)
     return pl.pallas_call(
         fine_kernel,
-        in_specs=[pl.BlockSpec(memory_space=pltpu.SMEM)] + [anywhere] * len(arrays),
-        out_specs=[anywhere, local],
-        scratch_shapes=[
-            buffer(512, 256),
-            buffer(512, 512),
-            buffer(256, 256),
-            buffer(256, 512),
-            *[buffer(size, 256) for size in (128, 64, 32)],
-            *[buffer(128, 512)] * 3,
-            pltpu.VMEM((32, 256), F32),
-            buffer(TOKENS, 256),
-            buffer(TOKENS + 256, 512),
-            buffer(TOKENS // 2, 256),
-            buffer(TOKENS // 4, 256),
-            buffer(512, 256),
-            pltpu.VMEM((32, 256), F32),
-            buffer(TOKENS, 256),
-            pltpu.SemaphoreType.DMA((17,)),
-            pltpu.SemaphoreType.DMA((4, RUNS)),
-            pltpu.SemaphoreType.DMA((RUNS,)),
-        ],
+        in_specs=[pl.BlockSpec(memory_space=pltpu.SMEM)] + [local] * len(arrays),
+        out_specs=[local, local],
+        scratch_shapes=[pltpu.VMEM((512, 256), BF), pltpu.VMEM((32, 256), F32)],
         out_shape=[shape((TOKENS, 256), BF), shape((32, 128), F32)],
-        compiler_params=pltpu.CompilerParams(vmem_limit_bytes=56 * 2**20),
+        compiler_params=pltpu.CompilerParams(vmem_limit_bytes=VMEM_LIMIT),
         name="merge_levels",
         cost_estimate=pl.CostEstimate(
             flops=4 * TOKENS * 512 * 256, bytes_accessed=18 * 2**20, transcendentals=TOKENS * 1024
@@ -580,16 +460,13 @@
     )(edge, *arrays)
 
 
-def norm_kernel(attention, s0, s1, s2, s3, gain, out, rows, done, in_sem, out_sem):
-    arriving = parts_of(attention, rows, in_sem, 4)
-    leaving = parts_of(done, out, out_sem, 4)
-    start_all(arriving)
+def norm_kernel(rows, s0, s1, s2, s3, gain, out, done, out_sem):
+    leaving = parts_of(done, out, out_sem, 8)
     total = s0[...] + s1[...] + s2[...] + s3[...]
     factor = lax.rsqrt(total / D + 1e-6)
     eye = iota((128, 128), 0) == iota((128, 128), 1)
-    for part in range(4):
-        arriving[part].wait()
-        for block in range(part * 8, part * 8 + 8):
+    for part in range(8):
+        for block in range(part * 4, part * 4 + 4):
             mine = slice(block * 128, block * 128 + 128)
             column = jnp.sum(jnp.where(eye, factor[block : block + 1], 0.0), axis=1, keepdims=True)
             done[mine, :] = (rows[mine, :].astype(F32) * column * gain[...]).astype(BF)
@@ -598,20 +475,14 @@
 
 
 def norm(attention, sums, gain):
-    anywhere = pl.BlockSpec(memory_space=pl.ANY)
     local = pl.BlockSpec(memory_space=pltpu.VMEM)
     return pl.pallas_call(
         norm_kernel,
-        in_specs=[anywhere] + [local] * 5,
-        out_specs=anywhere,
+        in_specs=[local] * 6,
+        out_specs=pl.BlockSpec(memory_space=pl.ANY),
         out_shape=jax.ShapeDtypeStruct((TOKENS, 256), BF),
-        scratch_shapes=[
-            pltpu.VMEM((TOKENS, 256), BF),
-            pltpu.VMEM((TOKENS, 256), BF),
-            pltpu.SemaphoreType.DMA((4,)),
-            pltpu.SemaphoreType.DMA((4,)),
-        ],
-        compiler_params=pltpu.CompilerParams(vmem_limit_bytes=56 * 2**20),
+        scratch_shapes=[pltpu.VMEM((TOKENS, 256), BF), pltpu.SemaphoreType.DMA((8,))],
+        compiler_params=pltpu.CompilerParams(vmem_limit_bytes=16 * 2**20),
         name="norm",
     )(attention, *sums, gain)
 

time: 107 us -> 92.1 us (0.86)
  Pallas kernels: 52 us -> 42.5 us
  local copies, waits for them, and re-layouts: 3.89 us -> 0.1 us
  other arithmetic: 4.44 us -> 2.69 us
  waiting for transfers between devices: 16.1 us -> 17.5 us
    unnamed x37 -> x3, local copies, waits for them, and re-layouts: 3.81 us -> 0.01 us
    pallas_call x1, Pallas kernels: 12.6 us -> 9.71 us  [fine(): pl.pallas_call(fine_kernel, in_specs=[pl.BlockSpec(memory_space=pltpu.SME...]
    pallas_call x1, Pallas kernels: 18.3 us -> 15.9 us  [project_queries(): pl.pallas_call(queries_kernel, in_specs=[pl.BlockSpec(memory_space=pltpu....]
    pallas_call x1, Pallas kernels: 15.9 us -> 13.8 us  [project_keys(): pl.pallas_call(keys_kernel, in_specs=[pl.BlockSpec(memory_space=pltpu.SME...]
    pallas_call x1, Pallas kernels: 3.53 us -> 1.54 us  [norm(): pl.pallas_call(norm_kernel, in_specs=[local] * 6, out_specs=pl.BlockSpec(...]
  transfers between devices with their start and end apart: 19 -> 19, of which waited for: 9 -> 9; matrix products, arithmetic and copies ran while one was open for 3% -> 2% of each run, Pallas kernels for 32% -> 32%
where the time goes in v2:
time: 92.1 us; the launch traced here: 91.7 us
  Pallas kernels  42.5 us (46%)
  starting transfers between devices  28.6 us (31%)
  waiting for transfers between devices  17.5 us (19%)
  other arithmetic  2.69 us (3%)
    ppermute x9, starting transfers between devices, along_line(): return lax.ppermute(value, ('seq', 'head'), line_perm(first, shift))  15.9 us
    pallas_call x1, Pallas kernels, project_queries(): pl.pallas_call(queries_kernel, in_specs=[pl.BlockSpec(memory_space=pltpu....  15.9 us
    pallas_call x1, Pallas kernels, project_keys(): pl.pallas_call(keys_kernel, in_specs=[pl.BlockSpec(memory_space=pltpu.SME...  13.8 us
    ppermute x9, waiting for transfers between devices, along_line(): return lax.ppermute(value, ('seq', 'head'), line_perm(first, shift))  10.5 us
    pallas_call x1, Pallas kernels, fine(): pl.pallas_call(fine_kernel, in_specs=[pl.BlockSpec(memory_space=pltpu.SME...  9.71 us
    ppermute x5, starting transfers between devices, flipped(): return lax.ppermute(value, 'seq', [(i, i ^ bits) for i in range(16)])  6.74 us
    ppermute x4, starting transfers between devices, over_heads(): return lax.ppermute(value, 'head', [(i, step(i)) for i in range(8)])  5.24 us
    ppermute x4, waiting for transfers between devices, over_heads(): return lax.ppermute(value, 'head', [(i, step(i)) for i in range(8)])  5.17 us
  transfers between devices with their start and end apart: 19, of which 9 were waited for; matrix products, arithmetic and copies ran while one was open for 2% of the time, Pallas kernels for 32%

profile of v2, /device:TPU:0, one launch (start us, length us, event | category | flops | bytes accessed | tf_op | source)
XLA Modules:
  0.0 91.7 jit_solution(17878512078434518844)
XLA Ops:
  0.0 1.6 %join_weights.1 = bf16[128,768]{1,0:T(8,128)(2,1)} custom-call(bf16[128,256]{1,0:T(8,128)(2,1)} %a.1, bf16[128,256]{1,0:T(8,128)(2,1)} %b.1, bf16[128,256]{1,0:T(8,128)(2,1)} %c.1), custom_call_target="tpu_custom_call" | custom-call | tf_op jit(solution)/shard_map/join_weights/pallas_call | solution.py:498
  1.6 4.0 %collective-permute-start.2 = (bf16[128,768]{1,0:T(8,128)(2,1)}, bf16[128,768]{1,0:T(8,128)(2,1)S(1)}, u32[]{:S(2)}, u32[]{:S(2)}) collective-permute-start(bf16[128,768]{1,0:T(8,128)(2,1)} %join_weights.1), channel_id=1, source_target_pairs={{0,16},{1,65},{2,18},{3,67},{4,20},{5,69},{6,22},{7,71},{8,24},{9,... | collective-permute-start | bytes 589832 | tf_op jit(solution)/shard_map/ppermute | solution.py:43
  5.6 0.7 collective-permute-start.1
  6.3 1.3 %collective-permute-start = (bf16[128,768]{1,0:T(8,128)(2,1)}, bf16[128,768]{1,0:T(8,128)(2,1)S(1)}, u32[]{:S(2)}, u32[]{:S(2)}) collective-permute-start(bf16[128,768]{1,0:T(8,128)(2,1)} %join_weights.1), channel_id=1, source_target_pairs={{0,8},{1,33},{2,10},{3,35},{4,12},{5,37},{6,14},{7,39},{8,16},{9,4... | collective-permute-start | bytes 589832 | tf_op jit(solution)/shard_map/ppermute | solution.py:43
  7.6 0.7 and_select_fusion.1
  8.2 1.2 %collective-permute-done.2 = bf16[128,768]{1,0:T(8,128)(2,1)S(1)} collective-permute-done((bf16[128,768]{1,0:T(8,128)(2,1)}, bf16[128,768]{1,0:T(8,128)(2,1)S(1)}, u32[]{:S(2)}, u32[]{:S(2)}) %collective-permute-start.2) | collective-permute-done | bytes 196640 | tf_op jit(solution)/shard_map/ppermute | solution.py:43
  9.4 3.2 %collective-permute-done.1 = bf16[128,768]{1,0:T(8,128)(2,1)S(1)} collective-permute-done((bf16[128,768]{1,0:T(8,128)(2,1)}, bf16[128,768]{1,0:T(8,128)(2,1)S(1)}, u32[]{:S(2)}, u32[]{:S(2)}) %collective-permute-start.1) | collective-permute-done | bytes 196640 | tf_op jit(solution)/shard_map/ppermute | solution.py:43
  12.6 0.8 collective-permute-done
  13.4 0.9 %pad_maximum_fusion.w0 = bf16[4,128,512]{2,1,0:T(8,128)(2,1)S(1)} fusion(bf16[1,128,768]{2,1,0:T(8,128)(2,1)S(1)} %bitcast.11, bf16[1,128,768]{2,1,0:T(8,128)(2,1)S(1)} %bitcast.13, bf16[1,128,768]{2,1,0:T(8,128)(2,1)S(1)} %bitcast.15, bf16[1,128,768]{2,1,0:T(8,128)(2,1)} %bitcast.9), kind=kLoop, calls=%fused_computation | loop fusion | flops 2097152 | bytes 1310720 | tf_op jit(solution)/shard_map/stack | solution.py:512
  14.3 3.1 %collective-permute-start.8 = (bf16[4,128,512]{2,1,0:T(8,128)(2,1)S(1)}, bf16[4,128,512]{2,1,0:T(8,128)(2,1)S(1)}, u32[]{:S(2)}, u32[]{:S(2)}) collective-permute-start(bf16[4,128,512]{2,1,0:T(8,128)(2,1)S(1)} %pad_maximum_fusion.w0), channel_id=1, source_target_pairs={{0,64},{1,17},{2,66},{3,19},{4,68},{5,21},{6,70},{7,23},{8,72},{9,... | collective-permute-start | bytes 1572872 | tf_op jit(solution)/shard_map/ppermute | solution.py:43
  17.4 1.1 %collective-permute-start.7 = (bf16[4,128,512]{2,1,0:T(8,128)(2,1)S(1)}, bf16[4,128,512]{2,1,0:T(8,128)(2,1)S(1)}, u32[]{:S(2)}, u32[]{:S(2)}) collective-permute-start(bf16[4,128,512]{2,1,0:T(8,128)(2,1)S(1)} %pad_maximum_fusion.w0), channel_id=1, source_target_pairs={{0,96},{1,25},{2,98},{3,27},{4,100},{5,29},{6,102},{7,31},{8,104},... | collective-permute-start | bytes 1572872 | tf_op jit(solution)/shard_map/ppermute | solution.py:43
  18.6 0.9 collective-permute-start.6
  19.4 0.1 select_add_fusion
  19.5 0.1 add.48
  19.6 0.1 pad_add_fusion.1.place
  19.7 0.1 pad_add_fusion.edge
  19.7 0.9 pad_maximum_fusion.3.w0
  20.6 0.7 collective-permute-start.5
  21.3 2.6 %collective-permute-start.4 = (bf16[4,128,256]{2,1,0:T(8,128)(2,1)S(1)}, bf16[4,128,256]{2,1,0:T(8,128)(2,1)S(1)}, u32[]{:S(2)}, u32[]{:S(2)}) collective-permute-start(bf16[4,128,256]{2,1,0:T(8,128)(2,1)S(1)} %pad_maximum_fusion.3.w0), channel_id=1, source_target_pairs={{0,96},{1,25},{2,98},{3,27},{4,100},{5,29},{6,102},{7,31},{8,104},... | collective-permute-start | bytes 786440 | tf_op jit(solution)/shard_map/ppermute | solution.py:43
  24.0 1.2 %collective-permute-done.8.w3 = bf16[4,128,512]{2,1,0:T(8,128)(2,1)S(1)} collective-permute-done((bf16[4,128,512]{2,1,0:T(8,128)(2,1)S(1)}, bf16[4,128,512]{2,1,0:T(8,128)(2,1)S(1)}, u32[]{:S(2)}, u32[]{:S(2)}) %collective-permute-start.8) | collective-permute-done | bytes 524320 | tf_op jit(solution)/shard_map/ppermute | solution.py:43
  25.2 1.5 %collective-permute-start.3 = (bf16[4,128,256]{2,1,0:T(8,128)(2,1)S(1)}, bf16[4,128,256]{2,1,0:T(8,128)(2,1)S(1)}, u32[]{:S(2)}, u32[]{:S(2)}) collective-permute-start(bf16[4,128,256]{2,1,0:T(8,128)(2,1)S(1)} %pad_maximum_fusion.3.w0), channel_id=1, source_target_pairs={{0,32},{1,9},{2,34},{3,11},{4,36},{5,13},{6,38},{7,15},{8,40},{9,1... | collective-permute-start | bytes 786440 | tf_op jit(solution)/shard_map/ppermute | solution.py:43
  26.7 4.2 %collective-permute-done.7.w2 = bf16[4,128,512]{2,1,0:T(8,128)(2,1)S(1)} collective-permute-done((bf16[4,128,512]{2,1,0:T(8,128)(2,1)S(1)}, bf16[4,128,512]{2,1,0:T(8,128)(2,1)S(1)}, u32[]{:S(2)}, u32[]{:S(2)}) %collective-permute-start.7) | collective-permute-done | bytes 524320 | tf_op jit(solution)/shard_map/ppermute | solution.py:43
  30.8 0.0 collective-permute-done.6.w1
  30.8 13.8 %project_keys.1 = (bf16[4096,512]{1,0:T(8,128)(2,1)S(1)}, bf16[2048,512]{1,0:T(8,128)(2,1)S(1)}, bf16[1024,512]{1,0:T(8,128)(2,1)S(1)}, bf16[512,512]{1,0:T(8,12...) custom-call(s32[17]{0:T(128)S(1)} %pad_add_fusion.1.place, ...), custom_call_target="tpu_custom_call" | custom-call | flops 8589934592 | bytes 27262976 | tf_op jit(solution)/shard_map/project_keys/pallas_call | solution.py:228
  44.6 1.5 %collective-permute-start.11 = (bf16[32,512]{1,0:T(8,128)(2,1)S(1)}, bf16[32,512]{1,0:T(8,128)(2,1)S(1)}, u32[]{:S(2)}, u32[]{:S(2)}) collective-permute-start(bf16[32,512]{1,0:T(8,128)(2,1)S(1)} %get-tuple-element.36), channel_id=1, source_target_pairs={{0,32},{8,40},{16,48},{24,56},{32,0},{40,8},{48,16},{56,24},{64,96... | collective-permute-start | bytes 98312 | tf_op jit(solution)/shard_map/ppermute | solution.py:47
  46.1 0.7 collective-permute-start.10
  46.8 1.8 %collective-permute-done.11.got_d = bf16[32,512]{1,0:T(8,128)(2,1)S(1)} collective-permute-done((bf16[32,512]{1,0:T(8,128)(2,1)S(1)}, bf16[32,512]{1,0:T(8,128)(2,1)S(1)}, u32[]{:S(2)}, u32[]{:S(2)}) %collective-permute-start.11) | collective-permute-done | bytes 32800 | tf_op jit(solution)/shard_map/ppermute | solution.py:47
  48.6 1.1 %collective-permute-start.9 = (bf16[256,512]{1,0:T(8,128)(2,1)S(1)}, bf16[256,512]{1,0:T(8,128)(2,1)S(1)}, u32[]{:S(2)}, u32[]{:S(2)}) collective-permute-start(bf16[256,512]{1,0:T(8,128)(2,1)S(1)} %get-tuple-element.34), channel_id=1, source_target_pairs={{0,8},{8,0},{16,24},{24,16},{32,40},{40,32},{48,56},{56,48},{64,72... | collective-permute-start | bytes 786440 | tf_op jit(solution)/shard_map/ppermute | solution.py:47
  49.7 0.0 collective-permute-done.5.w3
  49.8 1.8 %collective-permute-start.14 = (bf16[96,512]{1,0:T(8,128)(2,1)S(1)}, bf16[96,512]{1,0:T(8,128)(2,1)S(1)}, u32[]{:S(2)}, u32[]{:S(2)}) collective-permute-start(bf16[96,512]{1,0:T(8,128)(2,1)S(1)} %constant_dynamic-update-slice_fusion), channel_id=1, source_target_pairs={{0,24},{8,16},{16,8},{24,0},{32,56},{40,48},{48,40},{56,32},{64,88... | collective-permute-start | bytes 294920 | tf_op jit(solution)/shard_map/ppermute | solution.py:47
  51.5 0.0 collective-permute-done.4.w2
  51.5 1.4 %collective-permute-start.13 = (bf16[96,512]{1,0:T(8,128)(2,1)S(1)}, bf16[96,512]{1,0:T(8,128)(2,1)S(1)}, u32[]{:S(2)}, u32[]{:S(2)}) collective-permute-start(bf16[96,512]{1,0:T(8,128)(2,1)S(1)} %constant_dynamic-update-slice_fusion), channel_id=1, source_target_pairs={{0,16},{8,24},{16,0},{24,8},{32,48},{40,56},{48,32},{56,40},{64,80... | collective-permute-start | bytes 294920 | tf_op jit(solution)/shard_map/ppermute | solution.py:47
  53.0 0.0 collective-permute-done.3.w1
  53.0 0.9 collective-permute-start.12
  53.9 15.9 %project_queries.1 = (bf16[4096,256]{1,0:T(8,128)(2,1)S(1)}, bf16[2048,256]{1,0:T(8,128)(2,1)S(1)}, bf16[1024,256]{1,0:T(8,128)(2,1)S(1)}, f32[32,256]{1,0:T(8,1...) custom-call(s32[17]{0:T(128)S(1)} %pad_add_fusion.1.place, ...), custom_call_target="tpu_custom_call" | custom-call | flops 4294967296 | bytes 27262976 | tf_op jit(solution)/shard_map/project_queries/pallas_call | solution.py:251
  69.7 0.0 collective-permute-done.12.got_s
  69.8 0.0 collective-permute-done.14.got_e
  69.8 0.0 collective-permute-done.13.got_c
  69.8 0.0 collective-permute-done.10.got_b
  69.8 0.0 collective-permute-done.9.got_a
  69.8 0.0 copy-start
  69.8 9.7 %merge_levels.1 = (bf16[4096,256]{1,0:T(8,128)(2,1)S(1)}, f32[32,128]{1,0:T(8,128)S(1)}) custom-call(s32[3]{0:T(128)S(1)} %pad_add_fusion.edge, bf16[512,256]{1,0:T(8,128)(2,1)S(1)} %get-tuple-element.27.q3, bf16[512,512]{1,0:T(8,128)(2,1)S(1)} %get-tuple-element.28.kv3, bf16[256,256]{1,0:T(8,128)(2,1)S(1)} %get-tuple-element.29.q4, ...), custom_call_target="tpu_custom_call" | custom-call | flops 2147483648 | bytes 18874368 | tf_op jit(solution)/shard_map/merge_levels/pallas_call | solution.py:449
  79.5 0.0 collective-permute-start.15
  79.5 1.2 %collective-permute-done.15 = f32[32,128]{1,0:T(8,128)S(1)} collective-permute-done((f32[32,128]{1,0:T(8,128)S(1)}, f32[32,128]{1,0:T(8,128)S(1)}, u32[]{:S(2)}, u32[]{:S(2)}) %collective-permute-start.15) | collective-permute-done | bytes 16416 | tf_op jit(solution)/shard_map/ppermute | solution.py:56
  80.7 3.2 %collective-permute-start.18 = (f32[32,128]{1,0:T(8,128)S(1)}, f32[32,128]{1,0:T(8,128)S(1)}, u32[]{:S(2)}, u32[]{:S(2)}) collective-permute-start(f32[32,128]{1,0:T(8,128)S(1)} %add.49.s0), channel_id=1, source_target_pairs={{0,4},{1,5},{2,6},{3,7},{4,0},{5,1},{6,2},{7,3},{8,12},{9,13},{10,... | collective-permute-start | bytes 49160 | tf_op jit(solution)/shard_map/ppermute | solution.py:56
  83.9 1.1 %collective-permute-start.17 = (f32[32,128]{1,0:T(8,128)S(1)}, f32[32,128]{1,0:T(8,128)S(1)}, u32[]{:S(2)}, u32[]{:S(2)}) collective-permute-start(f32[32,128]{1,0:T(8,128)S(1)} %add.49.s0), channel_id=1, source_target_pairs={{0,6},{1,7},{2,0},{3,1},{4,2},{5,3},{6,4},{7,5},{8,14},{9,15},{10,... | collective-permute-start | bytes 49160 | tf_op jit(solution)/shard_map/ppermute | solution.py:56
  85.0 1.0 %collective-permute-start.16 = (f32[32,128]{1,0:T(8,128)S(1)}, f32[32,128]{1,0:T(8,128)S(1)}, u32[]{:S(2)}, u32[]{:S(2)}) collective-permute-start(f32[32,128]{1,0:T(8,128)S(1)} %add.49.s0), channel_id=1, source_target_pairs={{0,2},{1,3},{2,4},{3,5},{4,6},{5,7},{6,0},{7,1},{8,10},{9,11},{10,... | collective-permute-start | bytes 49160 | tf_op jit(solution)/shard_map/ppermute | solution.py:56
  86.0 0.0 collective-permute-done.18.s3
  86.0 1.7 %collective-permute-done.17.s2 = f32[32,128]{1,0:T(8,128)S(1)} collective-permute-done((f32[32,128]{1,0:T(8,128)S(1)}, f32[32,128]{1,0:T(8,128)S(1)}, u32[]{:S(2)}, u32[]{:S(2)}) %collective-permute-start.17) | collective-permute-done | bytes 16416 | tf_op jit(solution)/shard_map/ppermute | solution.py:56
  87.7 2.3 %collective-permute-done.16.s1 = f32[32,128]{1,0:T(8,128)S(1)} collective-permute-done((f32[32,128]{1,0:T(8,128)S(1)}, f32[32,128]{1,0:T(8,128)S(1)}, u32[]{:S(2)}, u32[]{:S(2)}) %collective-permute-start.16) | collective-permute-done | bytes 16416 | tf_op jit(solution)/shard_map/ppermute | solution.py:56
  90.0 0.0 copy-done
  90.0 1.5 %norm.1 = bf16[4096,256]{1,0:T(8,128)(2,1)} custom-call(bf16[4096,256]{1,0:T(8,128)(2,1)S(1)} %get-tuple-element.43.rows, f32[32,128]{1,0:T(8,128)S(1)} %add.49.s0, f32[32,128]{1,0:T(8,128)S(1)} %collective-permute-done.16.s1, f32[32,128]{1,0:T(8,128)S(1)} %collective-permute-done.17.s2, f32[32,128]{1,0:T(8,128)S(1)} %collective-permute-done.18.s3, ...), custom_call_target="tpu_custom_call" | custom-call | tf_op jit(solution)/shard_map/norm/pallas_call | solution.py:479
  (3 shorter events, 0.0 us)
Async XLA Ops:
  1.6 7.8 %collective-permute-start.2 = (bf16[128,768]{1,0:T(8,128)(2,1)}, bf16[128,768]{1,0:T(8,128)(2,1)S(1)}, u32[]{:S(2)}, u32[]{:S(2)}) collective-permute-start(bf16[128,768]{1,0:T(8,128)(2,1)} %join_weights.1), channel_id=1, source_target_pairs={{0,16},{1,65},{2,18},{3,67},{4,20},{5,69},{6,22},{7,71},{8,24},{9,... | collective-permute-start | bytes 589832 | tf_op jit(solution)/shard_map/ppermute | solution.py:43
  5.6 7.0 %collective-permute-start.1 = (bf16[128,768]{1,0:T(8,128)(2,1)}, bf16[128,768]{1,0:T(8,128)(2,1)S(1)}, u32[]{:S(2)}, u32[]{:S(2)}) collective-permute-start(bf16[128,768]{1,0:T(8,128)(2,1)} %join_weights.1), channel_id=1, source_target_pairs={{0,24},{1,97},{2,26},{3,99},{4,28},{5,101},{6,30},{7,103},{8,0},{9... | collective-permute-start | bytes 589832 | tf_op jit(solution)/shard_map/ppermute | solution.py:43
  6.3 7.1 %collective-permute-start = (bf16[128,768]{1,0:T(8,128)(2,1)}, bf16[128,768]{1,0:T(8,128)(2,1)S(1)}, u32[]{:S(2)}, u32[]{:S(2)}) collective-permute-start(bf16[128,768]{1,0:T(8,128)(2,1)} %join_weights.1), channel_id=1, source_target_pairs={{0,8},{1,33},{2,10},{3,35},{4,12},{5,37},{6,14},{7,39},{8,16},{9,4... | collective-permute-start | bytes 589832 | tf_op jit(solution)/shard_map/ppermute | solution.py:43
  14.3 10.9 %collective-permute-start.8 = (bf16[4,128,512]{2,1,0:T(8,128)(2,1)S(1)}, bf16[4,128,512]{2,1,0:T(8,128)(2,1)S(1)}, u32[]{:S(2)}, u32[]{:S(2)}) collective-permute-start(bf16[4,128,512]{2,1,0:T(8,128)(2,1)S(1)} %pad_maximum_fusion.w0), channel_id=1, source_target_pairs={{0,64},{1,17},{2,66},{3,19},{4,68},{5,21},{6,70},{7,23},{8,72},{9,... | collective-permute-start | bytes 1572872 | tf_op jit(solution)/shard_map/ppermute | solution.py:43
  17.4 13.4 %collective-permute-start.7 = (bf16[4,128,512]{2,1,0:T(8,128)(2,1)S(1)}, bf16[4,128,512]{2,1,0:T(8,128)(2,1)S(1)}, u32[]{:S(2)}, u32[]{:S(2)}) collective-permute-start(bf16[4,128,512]{2,1,0:T(8,128)(2,1)S(1)} %pad_maximum_fusion.w0), channel_id=1, source_target_pairs={{0,96},{1,25},{2,98},{3,27},{4,100},{5,29},{6,102},{7,31},{8,104},... | collective-permute-start | bytes 1572872 | tf_op jit(solution)/shard_map/ppermute | solution.py:43
  18.6 12.3 %collective-permute-start.6 = (bf16[4,128,512]{2,1,0:T(8,128)(2,1)S(1)}, bf16[4,128,512]{2,1,0:T(8,128)(2,1)S(1)}, u32[]{:S(2)}, u32[]{:S(2)}) collective-permute-start(bf16[4,128,512]{2,1,0:T(8,128)(2,1)S(1)} %pad_maximum_fusion.w0), channel_id=1, source_target_pairs={{0,32},{1,9},{2,34},{3,11},{4,36},{5,13},{6,38},{7,15},{8,40},{9,1... | collective-permute-start | bytes 1572872 | tf_op jit(solution)/shard_map/ppermute | solution.py:43
  20.6 29.1 %collective-permute-start.5 = (bf16[4,128,256]{2,1,0:T(8,128)(2,1)S(1)}, bf16[4,128,256]{2,1,0:T(8,128)(2,1)S(1)}, u32[]{:S(2)}, u32[]{:S(2)}) collective-permute-start(bf16[4,128,256]{2,1,0:T(8,128)(2,1)S(1)} %pad_maximum_fusion.3.w0), channel_id=1, source_target_pairs={{0,64},{1,17},{2,66},{3,19},{4,68},{5,21},{6,70},{7,23},{8,72},{9,... | collective-permute-start | bytes 786440 | tf_op jit(solution)/shard_map/ppermute | solution.py:43
  21.3 30.2 %collective-permute-start.4 = (bf16[4,128,256]{2,1,0:T(8,128)(2,1)S(1)}, bf16[4,128,256]{2,1,0:T(8,128)(2,1)S(1)}, u32[]{:S(2)}, u32[]{:S(2)}) collective-permute-start(bf16[4,128,256]{2,1,0:T(8,128)(2,1)S(1)} %pad_maximum_fusion.3.w0), channel_id=1, source_target_pairs={{0,96},{1,25},{2,98},{3,27},{4,100},{5,29},{6,102},{7,31},{8,104},... | collective-permute-start | bytes 786440 | tf_op jit(solution)/shard_map/ppermute | solution.py:43
  25.2 27.8 %collective-permute-start.3 = (bf16[4,128,256]{2,1,0:T(8,128)(2,1)S(1)}, bf16[4,128,256]{2,1,0:T(8,128)(2,1)S(1)}, u32[]{:S(2)}, u32[]{:S(2)}) collective-permute-start(bf16[4,128,256]{2,1,0:T(8,128)(2,1)S(1)} %pad_maximum_fusion.3.w0), channel_id=1, source_target_pairs={{0,32},{1,9},{2,34},{3,11},{4,36},{5,13},{6,38},{7,15},{8,40},{9,1... | collective-permute-start | bytes 786440 | tf_op jit(solution)/shard_map/ppermute | solution.py:43
  44.6 4.0 %collective-permute-start.11 = (bf16[32,512]{1,0:T(8,128)(2,1)S(1)}, bf16[32,512]{1,0:T(8,128)(2,1)S(1)}, u32[]{:S(2)}, u32[]{:S(2)}) collective-permute-start(bf16[32,512]{1,0:T(8,128)(2,1)S(1)} %get-tuple-element.36), channel_id=1, source_target_pairs={{0,32},{8,40},{16,48},{24,56},{32,0},{40,8},{48,16},{56,24},{64,96... | collective-permute-start | bytes 98312 | tf_op jit(solution)/shard_map/ppermute | solution.py:47
  46.1 23.7 %collective-permute-start.10 = (bf16[128,512]{1,0:T(8,128)(2,1)S(1)}, bf16[128,512]{1,0:T(8,128)(2,1)S(1)}, u32[]{:S(2)}, u32[]{:S(2)}) collective-permute-start(bf16[128,512]{1,0:T(8,128)(2,1)S(1)} %get-tuple-element.35), channel_id=1, source_target_pairs={{8,16},{24,32},{40,48},{56,64},{72,80},{88,96},{104,112},{16,8},{3... | collective-permute-start | bytes 393224 | tf_op jit(solution)/shard_map/ppermute | solution.py:52
  48.6 21.2 %collective-permute-start.9 = (bf16[256,512]{1,0:T(8,128)(2,1)S(1)}, bf16[256,512]{1,0:T(8,128)(2,1)S(1)}, u32[]{:S(2)}, u32[]{:S(2)}) collective-permute-start(bf16[256,512]{1,0:T(8,128)(2,1)S(1)} %get-tuple-element.34), channel_id=1, source_target_pairs={{0,8},{8,0},{16,24},{24,16},{32,40},{40,32},{48,56},{56,48},{64,72... | collective-permute-start | bytes 786440 | tf_op jit(solution)/shard_map/ppermute | solution.py:47
  49.8 20.0 %collective-permute-start.14 = (bf16[96,512]{1,0:T(8,128)(2,1)S(1)}, bf16[96,512]{1,0:T(8,128)(2,1)S(1)}, u32[]{:S(2)}, u32[]{:S(2)}) collective-permute-start(bf16[96,512]{1,0:T(8,128)(2,1)S(1)} %constant_dynamic-update-slice_fusion), channel_id=1, source_target_pairs={{0,24},{8,16},{16,8},{24,0},{32,56},{40,48},{48,40},{56,32},{64,88... | collective-permute-start | bytes 294920 | tf_op jit(solution)/shard_map/ppermute | solution.py:47
  51.5 18.3 %collective-permute-start.13 = (bf16[96,512]{1,0:T(8,128)(2,1)S(1)}, bf16[96,512]{1,0:T(8,128)(2,1)S(1)}, u32[]{:S(2)}, u32[]{:S(2)}) collective-permute-start(bf16[96,512]{1,0:T(8,128)(2,1)S(1)} %constant_dynamic-update-slice_fusion), channel_id=1, source_target_pairs={{0,16},{8,24},{16,0},{24,8},{32,48},{40,56},{48,32},{56,40},{64,80... | collective-permute-start | bytes 294920 | tf_op jit(solution)/shard_map/ppermute | solution.py:47
  53.0 16.8 %collective-permute-start.12 = (bf16[32,512]{1,0:T(8,128)(2,1)S(1)}, bf16[32,512]{1,0:T(8,128)(2,1)S(1)}, u32[]{:S(2)}, u32[]{:S(2)}) collective-permute-start(bf16[32,512]{1,0:T(8,128)(2,1)S(1)} %collective-permute-done.11.got_d), channel_id=1, source_target_pairs={{0,8},{8,0},{16,24},{24,16},{32,40},{40,32},{48,56},{56,48},{64,72... | collective-permute-start | bytes 98312 | tf_op jit(solution)/shard_map/ppermute | solution.py:47
  69.8 20.2 %copy-start = (f32[256]{0:T(256)S(1)}, f32[256]{0:T(256)}, u32[]{:S(2)}) copy-start(f32[256]{0:T(256)} %param.10) | copy-start | bytes 3076
  79.5 1.2 %collective-permute-start.15 = (f32[32,128]{1,0:T(8,128)S(1)}, f32[32,128]{1,0:T(8,128)S(1)}, u32[]{:S(2)}, u32[]{:S(2)}) collective-permute-start(f32[32,128]{1,0:T(8,128)S(1)} %get-tuple-element.44), channel_id=1, source_target_pairs={{0,1},{1,0},{2,3},{3,2},{4,5},{5,4},{6,7},{7,6},{8,9},{9,8},{10,11... | collective-permute-start | bytes 49160 | tf_op jit(solution)/shard_map/ppermute | solution.py:56
  80.7 5.2 %collective-permute-start.18 = (f32[32,128]{1,0:T(8,128)S(1)}, f32[32,128]{1,0:T(8,128)S(1)}, u32[]{:S(2)}, u32[]{:S(2)}) collective-permute-start(f32[32,128]{1,0:T(8,128)S(1)} %add.49.s0), channel_id=1, source_target_pairs={{0,4},{1,5},{2,6},{3,7},{4,0},{5,1},{6,2},{7,3},{8,12},{9,13},{10,... | collective-permute-start | bytes 49160 | tf_op jit(solution)/shard_map/ppermute | solution.py:56
  83.9 3.7 %collective-permute-start.17 = (f32[32,128]{1,0:T(8,128)S(1)}, f32[32,128]{1,0:T(8,128)S(1)}, u32[]{:S(2)}, u32[]{:S(2)}) collective-permute-start(f32[32,128]{1,0:T(8,128)S(1)} %add.49.s0), channel_id=1, source_target_pairs={{0,6},{1,7},{2,0},{3,1},{4,2},{5,3},{6,4},{7,5},{8,14},{9,15},{10,... | collective-permute-start | bytes 49160 | tf_op jit(solution)/shard_map/ppermute | solution.py:56
  85.0 4.9 %collective-permute-start.16 = (f32[32,128]{1,0:T(8,128)S(1)}, f32[32,128]{1,0:T(8,128)S(1)}, u32[]{:S(2)}, u32[]{:S(2)}) collective-permute-start(f32[32,128]{1,0:T(8,128)S(1)} %add.49.s0), channel_id=1, source_target_pairs={{0,2},{1,3},{2,4},{3,5},{4,6},{5,7},{6,0},{7,1},{8,10},{9,11},{10,... | collective-permute-start | bytes 49160 | tf_op jit(solution)/shard_map/ppermute | solution.py:56

commit v3 on v2

--- a/solution.py
+++ b/solution.py
@@ -23,6 +23,8 @@
 CHUNKS = TOKENS // CHUNK
 RUNS = TOKENS // TM
 VMEM_LIMIT = 32 * 2**20
+EARLY_LIMIT = 32 * 2**20
+LATE_LIMIT = 32 * 2**20
 GROUP = 8
 
 
@@ -119,26 +121,31 @@
         copy.wait()
 
 
-def next_rows(hidden, h_all, h_sem, index):
-    part_of(hidden, h_all, h_sem, index, CHUNK).wait()
+def half_rows(place, base, hidden, ring, h_sem, index):
+    rows = pl.ds(pl.multiple_of(index * CHUNK, CHUNK), CHUNK)
+    slot = index % 3
+    return [
+        pltpu.make_async_copy(
+            hidden.at[rows, pl.ds(pl.multiple_of(place[base + block] * 128, 128), 128)],
+            ring.at[slot, :, pl.ds(block * 128, 128)],
+            h_sem.at[slot, block],
+        )
+        for block in range(ring.shape[2] // 128)
+    ]
+
+
+def next_half(place, base, hidden, ring, h_sem, index):
+    wait_all(half_rows(place, base, hidden, ring, h_sem, index))
 
     @pl.when(index < CHUNKS - 2)
     def _():
-        part_of(hidden, h_all, h_sem, index + 2, CHUNK).start()
-
-
-def place_weights(place, pieces, w_all):
-    for outer, piece in enumerate(pieces):
-        for inner in range(SIDE):
-            at = pl.multiple_of(place[outer * SIDE + inner] * 128, 128)
-            w_all[pl.ds(at, 128), :] = piece[inner]
-
-
-def pool_block(p_fine, rows, block, l1, l2, l3):
-    pooled = dot(p_fine, rows).astype(BF)
-    l1[pl.ds(pl.multiple_of(block * 64, 64), 64), :] = pooled[:64]
-    l2[pl.ds(pl.multiple_of(block * 32, 32), 32), :] = pooled[64:96]
-    l3[pl.ds(pl.multiple_of(block * 16, 16), 16), :] = pooled[96:112]
+        start_all(half_rows(place, base, hidden, ring, h_sem, index + 2))
+
+
+def join_half(pieces, w_half):
+    for n, piece in enumerate(pieces):
+        for i in range(SIDE):
+            w_half[(n * SIDE + i) * 128 : (n * SIDE + i + 1) * 128, :] = piece[i]
 
 
 def pool_runs(l3):
@@ -150,46 +157,132 @@
     ]
 
 
-def keys_kernel(
-    place, hidden, w0, w1, w2, w3, full, l1, l2, l3, l4, send_a, send_b, six, seven, h_all, w_all, h_sem
+def early_kernel(place, hidden, w0, w1, w2, sums, ring, w_half, h_sem):
+    for index in range(2):
+        start_all(half_rows(place, 0, hidden, ring, h_sem, index))
+    join_half((w0, w1, w2), w_half)
+
+    @pl.loop(0, CHUNKS)
+    def _(index):
+        next_half(place, 0, hidden, ring, h_sem, index)
+        at = pl.ds(pl.multiple_of(index * CHUNK, CHUNK), CHUNK)
+        sums[at, :] = dot(ring[index % 3], w_half[...]).astype(BF)
+
+
+def late_kernel(
+    place, hidden, w3, sums,
+    kv, kv1, kv2, kv3, kv4, q, q1, q2, q3, q4, q5, q6, q7, send_a, send_b, six, seven,
+    ring, w_half, l3, h_sem,
 ):
     for index in range(2):
-        part_of(hidden, h_all, h_sem, index, CHUNK).start()
-    place_weights(place, (w0, w1, w2, w3), w_all)
+        start_all(half_rows(place, 12, hidden, ring, h_sem, index))
+    join_half((w3,), w_half)
     p_fine = pool_matrix(112, 128, (1, 2, 3))
 
-    @pl.loop(0, CHUNKS)
+    def pool(index):
+        at = pl.ds(pl.multiple_of(index * CHUNK, CHUNK), CHUNK)
+        rows = jnp.concatenate([kv[at, :], q[at, :]], 1)
+        pooled = [
+            dot(p_fine, rows[part * 128 : part * 128 + 128]).astype(BF) for part in range(CHUNK // 128)
+        ]
+        for part, means in enumerate(pooled):
+            block = index * (CHUNK // 128) + part
+            at1 = pl.ds(pl.multiple_of(block * 64, 64), 64)
+            at2 = pl.ds(pl.multiple_of(block * 32, 32), 32)
+            at3 = pl.ds(pl.multiple_of(block * 16, 16), 16)
+            kv1[at1, :] = means[:64, :512]
+            q1[at1, :] = means[:64, 512:]
+            kv2[at2, :] = means[64:96, :512]
+            q2[at2, :] = means[64:96, 512:]
+            l3[at3, :] = means[96:112]
+
+    def project(index):
+        next_half(place, 12, hidden, ring, h_sem, index)
+        at = pl.ds(pl.multiple_of(index * CHUNK, CHUNK), CHUNK)
+        rows = (dot(ring[index % 3], w_half[...]) + sums[at, :].astype(F32)).astype(BF)
+        return at, rows
+
+    at, rows = project(jnp.int32(0))
+    kv[at, :] = rows[:, :512]
+    q[at, :] = rows[:, 512:]
+
+    @pl.loop(1, CHUNKS)
     def _(index):
-        next_rows(hidden, h_all, h_sem, index)
-        at = pl.ds(pl.multiple_of(index * CHUNK, CHUNK), CHUNK)
-        rows = dot(h_all[at, :], w_all[...]).astype(BF)
-        full[at, :] = rows
-        for part in range(CHUNK // 128):
-            pool_block(p_fine, rows[part * 128 : part * 128 + 128], index * (CHUNK // 128) + part, l1, l2, l3)
-
-    l4[...], five, six[...], seven[...] = pool_runs(l3)
+        at, rows = project(index)
+        pool(index - 1)
+        kv[at, :] = rows[:, :512]
+        q[at, :] = rows[:, 512:]
+
+    pool(CHUNKS - 1)
+    kv3[...] = l3[:, :512]
+    q3[...] = l3[:, 512:]
+    four, five, last, tail = pool_runs(l3)
+    kv4[...] = four[:, :512]
+    q4[...] = four[:, 512:]
+    q5[...] = five[:, 512:]
+    q6[...] = last[:, 512:]
+    q7[...] = tail[:, 512:]
+    six[...] = last[:, :512]
+    seven[...] = tail[:, :512]
     odd = place[16] == 1
-    low, high = full[:128, :], full[TOKENS - 128 :, :]
+    low, high = kv[:128, :], kv[TOKENS - 128 :, :]
     send_a[:128, :] = jnp.where(odd, low, high)
     send_b[...] = jnp.where(odd, high, low)
-    send_a[128:, :] = five
-
-
-def queries_kernel(
-    place, hidden, w0, w1, w2, w3, kv1, kv2,
-    full, o1, o2, virtual, l3, q4, q5, q6, q7,
-    h_all, w_all, l1, l2, h_sem,
-):
-    for index in range(2):
-        part_of(hidden, h_all, h_sem, index, CHUNK).start()
-    place_weights(place, (w0, w1, w2, w3), w_all)
-    p_fine = pool_matrix(112, 128, (1, 2, 3))
-
-    def attend_run(run):
+    send_a[128:, :] = five[:, :512]
+
+
+def project_early(place, hidden, pieces):
+    anywhere = pl.BlockSpec(memory_space=pl.ANY)
+    local = pl.BlockSpec(memory_space=pltpu.VMEM)
+    return pl.pallas_call(
+        early_kernel,
+        in_specs=[pl.BlockSpec(memory_space=pltpu.SMEM), anywhere] + [local] * 3,
+        out_specs=local,
+        out_shape=jax.ShapeDtypeStruct((TOKENS, 768), BF),
+        scratch_shapes=[
+            pltpu.VMEM((3, CHUNK, 1536), BF),
+            pltpu.VMEM((1536, 768), BF),
+            pltpu.SemaphoreType.DMA((3, 12)),
+        ],
+        compiler_params=pltpu.CompilerParams(vmem_limit_bytes=EARLY_LIMIT),
+        name="project_early",
+        cost_estimate=pl.CostEstimate(
+            flops=3 * TOKENS * 1024 * 768, bytes_accessed=12 * 2**20, transcendentals=0
+        ),
+    )(place, hidden, *pieces)
+
+
+def project_late(place, hidden, pieces, sums):
+    anywhere = pl.BlockSpec(memory_space=pl.ANY)
+    local = pl.BlockSpec(memory_space=pltpu.VMEM)
+    sizes = [(TOKENS >> level, 512) for level in range(5)]
+    sizes += [(TOKENS >> level, 256) for level in range(8)]
+    sizes += [(256, 512), (128, 512), (64, 512), (32, 512)]
+    return pl.pallas_call(
+        late_kernel,
+        in_specs=[pl.BlockSpec(memory_space=pltpu.SMEM), anywhere] + [local] * 2,
+        out_specs=[local] * len(sizes),
+        out_shape=[jax.ShapeDtypeStruct(size, BF) for size in sizes],
+        scratch_shapes=[
+            pltpu.VMEM((3, CHUNK, 512), BF),
+            pltpu.VMEM((512, 768), BF),
+            pltpu.VMEM((512, 768), BF),
+            pltpu.SemaphoreType.DMA((3, 4)),
+        ],
+        compiler_params=pltpu.CompilerParams(vmem_limit_bytes=LATE_LIMIT),
+        name="project_late",
+        cost_estimate=pl.CostEstimate(
+            flops=TOKENS * 1024 * 768, bytes_accessed=8 * 2**20, transcendentals=0
+        ),
+    )(place, hidden, *pieces, sums)
+
+
+def pairs_kernel(q1, kv1, q2, kv2, o1, o2, virtual):
+    for run in range(RUNS):
         triples, places = [], []
         for head in range(HEADS):
             k, v = (slice(i * 256 + head * 128, i * 256 + head * 128 + 128) for i in range(2))
-            for q_all, kv_all, out, count in ((l1, kv1, o1, 4), (l2, kv2, o2, 2)):
+            for q_all, kv_all, out, count in ((q1, kv1, o1, 4), (q2, kv2, o2, 2)):
                 for block in range(run * count, run * count + count):
                     mine = slice(block * 128, block * 128 + 128)
                     its = slice((block ^ 1) * 128, (block ^ 1) * 128 + 128)
@@ -207,67 +300,21 @@
                 lanes.append(jnp.concatenate([fine, coarse, jnp.zeros((1, 32), F32)], 1))
             virtual[run * 8 : run * 8 + 8, head * 128 : head * 128 + 128] = jnp.concatenate(lanes, 0)
 
-    for run in range(RUNS):
-        for index in range(run * (TM // CHUNK), (run + 1) * (TM // CHUNK)):
-            next_rows(hidden, h_all, h_sem, jnp.int32(index))
-        at = slice(run * TM, run * TM + TM)
-        rows = dot(h_all[at, :], w_all[...]).astype(BF)
-        full[at, :] = rows
-        for part in range(TM // 128):
-            pool_block(p_fine, rows[part * 128 : part * 128 + 128], run * (TM // 128) + part, l1, l2, l3)
-        if run:
-            attend_run(run - 1)
-    q4[...], q5[...], q6[...], q7[...] = pool_runs(l3)
-    attend_run(RUNS - 1)
-
-
-def project_keys(place, hidden, pieces):
-    anywhere = pl.BlockSpec(memory_space=pl.ANY)
-    local = pl.BlockSpec(memory_space=pltpu.VMEM)
-    sizes = [TOKENS >> level for level in range(5)] + [256, 128, 64, 32]
-    return pl.pallas_call(
-        keys_kernel,
-        in_specs=[pl.BlockSpec(memory_space=pltpu.SMEM), anywhere] + [local] * 4,
-        out_specs=[local] * 9,
-        out_shape=[jax.ShapeDtypeStruct((size, 512), BF) for size in sizes],
-        scratch_shapes=[
-            pltpu.VMEM((TOKENS, D), BF),
-            pltpu.VMEM((D, 512), BF),
-            pltpu.SemaphoreType.DMA((CHUNKS,)),
-        ],
-        compiler_params=pltpu.CompilerParams(vmem_limit_bytes=VMEM_LIMIT),
-        name="project_keys",
-        cost_estimate=pl.CostEstimate(
-            flops=2 * TOKENS * D * 512, bytes_accessed=26 * 2**20, transcendentals=0
-        ),
-    )(place, hidden, *pieces)
-
-
-def project_queries(place, hidden, pieces, kv1, kv2):
-    anywhere = pl.BlockSpec(memory_space=pl.ANY)
+
+def pairs(*arrays):
     local = pl.BlockSpec(memory_space=pltpu.VMEM)
     shape = jax.ShapeDtypeStruct
-    small = [shape((size, 256), BF) for size in (512, 256, 128, 64, 32)]
     return pl.pallas_call(
-        queries_kernel,
-        in_specs=[pl.BlockSpec(memory_space=pltpu.SMEM), anywhere] + [local] * 6,
-        out_specs=[local] * 9,
-        out_shape=[shape((TOKENS, 256), BF), shape((2048, 256), BF), shape((1024, 256), BF)]
-        + [shape((32, 256), F32)]
-        + small,
-        scratch_shapes=[
-            pltpu.VMEM((TOKENS, D), BF),
-            pltpu.VMEM((D, 256), BF),
-            pltpu.VMEM((2048, 256), BF),
-            pltpu.VMEM((1024, 256), BF),
-            pltpu.SemaphoreType.DMA((CHUNKS,)),
-        ],
+        pairs_kernel,
+        in_specs=[local] * 4,
+        out_specs=[local] * 3,
+        out_shape=[shape((2048, 256), BF), shape((1024, 256), BF), shape((32, 256), F32)],
         compiler_params=pltpu.CompilerParams(vmem_limit_bytes=VMEM_LIMIT),
-        name="project_queries",
+        name="levels_1_2",
         cost_estimate=pl.CostEstimate(
-            flops=2 * TOKENS * D * 256, bytes_accessed=26 * 2**20, transcendentals=2**20
+            flops=2 * 3072 * 128 * 512, bytes_accessed=9 * 2**20, transcendentals=3072 * 256
         ),
-    )(place, hidden, *pieces, kv1, kv2)
+    )(*arrays)
 
 
 def with_ones(values):
@@ -510,15 +557,18 @@
     x, z = position // SIDE, position % SIDE
     w_mine = joined(w_key, w_value, w_query)
     line = jnp.stack([w_mine] + [along_line(w_mine, True, s) for s in SHIFTS])
-    line_kv, line_q = line[:, :, :512], line[:, :, 512:]
-    pieces_kv = [line_kv] + [along_line(line_kv, False, s) for s in SHIFTS]
-    pieces_q = [line_q] + [along_line(line_q, False, s) for s in SHIFTS]
+    pieces = [line] + [along_line(line, False, s) for s in SHIFTS[:2]]
+    *pieces, line = lax.optimization_barrier((*pieces, line))
+    pieces = [*pieces, along_line(line, False, SHIFTS[2])]
     back = jnp.array((0,) + SHIFTS, jnp.int32)
     near_x = jnp.where(core == 0, (x - back[:, None]) % SIDE, (x - back[None, :]) % SIDE)
     near_z = jnp.where(core == 0, (z - back[None, :]) % SIDE, (z - back[:, None]) % SIDE)
     place = jnp.concatenate([(near_x * SIDE + near_z).reshape(16), (position % 2).reshape(1)])
     place = place.astype(jnp.int32)
-    kv, kv1, kv2, kv3, kv4, send_a, send_b, send_6, send_7 = project_keys(place, hidden_states, pieces_kv)
+    sums = project_early(place, hidden_states, pieces[:3])
+    kv, kv1, kv2, kv3, kv4, q, q1, q2, q3, q4, q5, q6, q7, send_a, send_b, send_6, send_7 = project_late(
+        place, hidden_states, pieces[3:], sums
+    )
     got_d = flipped(send_7, 4)
     got_a = flipped(send_a, 1)
     got_b = other_side(send_b)
@@ -526,7 +576,7 @@
     got_s = flipped(got_d, 1)
     got_c = flipped(far, 2)
     got_e = flipped(far, 3)
-    q, o1, o2, virtual, q3, q4, q5, q6, q7 = project_queries(place, hidden_states, pieces_q, kv1, kv2)
+    o1, o2, virtual = pairs(q1, kv1, q2, kv2)
     edge = jnp.stack([position % 2, position == 0, position == 15]).astype(jnp.int32)
     attention, squares = fine(
         edge, q3, kv3, q4, kv4, q5, q6, q7, got_a, got_b, got_d, got_s, got_c, got_e, virtual, q, kv, o1, o2

time: 92.1 us -> 88.1 us (0.957)
  waiting for transfers between devices: 17.5 us -> 26.2 us
  starting transfers between devices: 28.6 us -> 22.7 us
  Pallas kernels: 42.5 us -> 36.9 us
    ppermute x9 -> x6, waiting for transfers between devices: 10.5 us -> 18.1 us  [along_line(): return lax.ppermute(value, ('seq', 'head'), line_perm(first, shift))]
    ppermute x9 -> x6, starting transfers between devices: 15.9 us -> 8.82 us  [along_line(): return lax.ppermute(value, ('seq', 'head'), line_perm(first, shift))]
    pallas_call x2 -> x3, Pallas kernels: 29.7 us -> 24.8 us  [the longest x1 13.8 us: project_early(): pl.pallas_call(early_kernel, in_specs=[pl.BlockSpec(memory_space=pltpu.SM...]
    ppermute x5, starting transfers between devices: 6.74 us -> 8.01 us  [flipped(): return lax.ppermute(value, 'seq', [(i, i ^ bits) for i in range(16)])]
    ppermute x5, waiting for transfers between devices: 1.82 us -> 2.95 us  [flipped(): return lax.ppermute(value, 'seq', [(i, i ^ bits) for i in range(16)])]
  transfers between devices with their start and end apart: 19 -> 16, of which waited for: 9 -> 10; matrix products, arithmetic and copies ran while one was open for 2% -> 1% of each run, Pallas kernels for 32% -> 19%
where the time goes in v3:
time: 88.1 us; the launch traced here: 87.9 us
  Pallas kernels  36.9 us (42%)
  waiting for transfers between devices  26.2 us (30%)
  starting transfers between devices  22.7 us (26%)
  other arithmetic  1.92 us (2%)
    ppermute x6, waiting for transfers between devices, along_line(): return lax.ppermute(value, ('seq', 'head'), line_perm(first, shift))  18.1 us
    pallas_call x1, Pallas kernels, project_early(): pl.pallas_call(early_kernel, in_specs=[pl.BlockSpec(memory_space=pltpu.SM...  13.8 us
    pallas_call x1, Pallas kernels, fine(): pl.pallas_call(fine_kernel, in_specs=[pl.BlockSpec(memory_space=pltpu.SME...  8.97 us
    ppermute x6, starting transfers between devices, along_line(): return lax.ppermute(value, ('seq', 'head'), line_perm(first, shift))  8.82 us
    pallas_call x1, Pallas kernels, project_late(): pl.pallas_call(late_kernel, in_specs=[pl.BlockSpec(memory_space=pltpu.SME...  8.35 us
    ppermute x5, starting transfers between devices, flipped(): return lax.ppermute(value, 'seq', [(i, i ^ bits) for i in range(16)])  8.01 us
    ppermute x4, starting transfers between devices, over_heads(): return lax.ppermute(value, 'head', [(i, step(i)) for i in range(8)])  5.23 us
    ppermute x4, waiting for transfers between devices, over_heads(): return lax.ppermute(value, 'head', [(i, step(i)) for i in range(8)])  5.17 us
  transfers between devices with their start and end apart: 16, of which 10 were waited for; matrix products, arithmetic and copies ran while one was open for 1% of the time, Pallas kernels for 19%

profile of v3, /device:TPU:0, one launch (start us, length us, event | category | flops | bytes accessed | tf_op | source)
XLA Modules:
  0.0 87.9 jit_solution(9545922064828008472)
XLA Ops:
  0.0 1.6 %join_weights.1 = bf16[128,768]{1,0:T(8,128)(2,1)} custom-call(bf16[128,256]{1,0:T(8,128)(2,1)} %a.1, bf16[128,256]{1,0:T(8,128)(2,1)} %b.1, bf16[128,256]{1,0:T(8,128)(2,1)} %c.1), custom_call_target="tpu_custom_call" | custom-call | tf_op jit(solution)/shard_map/join_weights/pallas_call | solution.py:545
  1.6 4.0 %collective-permute-start.2 = (bf16[128,768]{1,0:T(8,128)(2,1)}, bf16[128,768]{1,0:T(8,128)(2,1)S(1)}, u32[]{:S(2)}, u32[]{:S(2)}) collective-permute-start(bf16[128,768]{1,0:T(8,128)(2,1)} %join_weights.1), channel_id=1, source_target_pairs={{0,16},{1,65},{2,18},{3,67},{4,20},{5,69},{6,22},{7,71},{8,24},{9,... | collective-permute-start | bytes 589832 | tf_op jit(solution)/shard_map/ppermute | solution.py:45
  5.6 0.7 collective-permute-start.1
  6.3 1.3 %collective-permute-start = (bf16[128,768]{1,0:T(8,128)(2,1)}, bf16[128,768]{1,0:T(8,128)(2,1)S(1)}, u32[]{:S(2)}, u32[]{:S(2)}) collective-permute-start(bf16[128,768]{1,0:T(8,128)(2,1)} %join_weights.1), channel_id=1, source_target_pairs={{0,8},{1,33},{2,10},{3,35},{4,12},{5,37},{6,14},{7,39},{8,16},{9,4... | collective-permute-start | bytes 589832 | tf_op jit(solution)/shard_map/ppermute | solution.py:45
  7.6 1.8 %collective-permute-done.2 = bf16[128,768]{1,0:T(8,128)(2,1)S(1)} collective-permute-done((bf16[128,768]{1,0:T(8,128)(2,1)}, bf16[128,768]{1,0:T(8,128)(2,1)S(1)}, u32[]{:S(2)}, u32[]{:S(2)}) %collective-permute-start.2) | collective-permute-done | bytes 196640 | tf_op jit(solution)/shard_map/ppermute | solution.py:45
  9.4 3.2 %collective-permute-done.1 = bf16[128,768]{1,0:T(8,128)(2,1)S(1)} collective-permute-done((bf16[128,768]{1,0:T(8,128)(2,1)}, bf16[128,768]{1,0:T(8,128)(2,1)S(1)}, u32[]{:S(2)}, u32[]{:S(2)}) %collective-permute-start.1) | collective-permute-done | bytes 196640 | tf_op jit(solution)/shard_map/ppermute | solution.py:45
  12.6 0.8 collective-permute-done
  13.4 1.0 %pad_maximum_fusion.w0 = bf16[4,128,768]{2,1,0:T(8,128)(2,1)S(1)} fusion(bf16[1,128,768]{2,1,0:T(8,128)(2,1)S(1)} %bitcast.10, bf16[1,128,768]{2,1,0:T(8,128)(2,1)S(1)} %bitcast.11, bf16[1,128,768]{2,1,0:T(8,128)(2,1)S(1)} %bitcast.12, bf16[1,128,768]{2,1,0:T(8,128)(2,1)} %bitcast.9), kind=kLoop, calls=%fused_computation | loop fusion | flops 1179648 | bytes 1572864 | tf_op jit(solution)/shard_map/stack | solution.py:559
  14.4 2.8 %collective-permute-start.4 = (bf16[4,128,768]{2,1,0:T(8,128)(2,1)S(1)}, bf16[4,128,768]{2,1,0:T(8,128)(2,1)S(1)}, u32[]{:S(2)}, u32[]{:S(2)}) collective-permute-start(bf16[4,128,768]{2,1,0:T(8,128)(2,1)S(1)} %pad_maximum_fusion.w0), channel_id=1, source_target_pairs={{0,96},{1,25},{2,98},{3,27},{4,100},{5,29},{6,102},{7,31},{8,104},... | collective-permute-start | bytes 2359304 | tf_op jit(solution)/shard_map/ppermute | solution.py:45
  17.2 0.0 collective-permute-start.3
  17.2 0.7 and_select_fusion.1
  17.9 0.1 select_add_fusion
  18.0 0.1 add.48
  18.0 0.1 pad_add_fusion.1.place
  18.1 8.6 %collective-permute-done.4.w2 = bf16[4,128,768]{2,1,0:T(8,128)(2,1)S(1)} collective-permute-done((bf16[4,128,768]{2,1,0:T(8,128)(2,1)S(1)}, bf16[4,128,768]{2,1,0:T(8,128)(2,1)S(1)}, u32[]{:S(2)}, u32[]{:S(2)}) %collective-permute-start.4) | collective-permute-done | bytes 786464 | tf_op jit(solution)/shard_map/ppermute | solution.py:45
  26.7 3.7 %collective-permute-done.3.w1 = bf16[4,128,768]{2,1,0:T(8,128)(2,1)S(1)} collective-permute-done((bf16[4,128,768]{2,1,0:T(8,128)(2,1)S(1)}, bf16[4,128,768]{2,1,0:T(8,128)(2,1)S(1)}, u32[]{:S(2)}, u32[]{:S(2)}) %collective-permute-start.3) | collective-permute-done | bytes 786464 | tf_op jit(solution)/shard_map/ppermute | solution.py:45
  30.4 0.0 collective-permute-start.5
  30.4 13.8 %project_early.1.sums = bf16[4096,768]{1,0:T(8,128)(2,1)S(1)} custom-call(s32[17]{0:T(128)S(1)} %pad_add_fusion.1.place, bf16[4096,2048]{1,0:T(8,128)(2,1)} %hidden.3, bf16[4,128,768]{2,1,0:T(8,128)(2,1)S(1)} %pad_maximum_fusion.w0, bf16[4,128,768]{2,1,0:T(8,128)(2,1)S(1)} %collective-permute-done.3.w1, bf16[4,128,768]{2,1,0:T(8,128)(2,1)S(1)} %collective-permute-done.4.w2), custom_call_target="tpu_custom_call" | custom-call | flops 9663676416 | bytes 12582912 | tf_op jit(solution)/shard_map/project_early/pallas_call | solution.py:237
  44.2 0.0 collective-permute-done.5.w3
  44.2 8.3 %project_late.1 = (bf16[4096,512]{1,0:T(8,128)(2,1)S(1)}, bf16[2048,512]{1,0:T(8,128)(2,1)S(1)}, bf16[1024,512]{1,0:T(8,128)(2,1)S(1)}, bf16[512,512]{1,0:T(8,12...) custom-call(s32[17]{0:T(128)S(1)} %pad_add_fusion.1.place, ...), custom_call_target="tpu_custom_call" | custom-call | flops 3221225472 | bytes 8388608 | tf_op jit(solution)/shard_map/project_late/pallas_call | solution.py:261
  52.6 0.9 %collective-permute-start.8 = (bf16[32,512]{1,0:T(8,128)(2,1)S(1)}, bf16[32,512]{1,0:T(8,128)(2,1)S(1)}, u32[]{:S(2)}, u32[]{:S(2)}) collective-permute-start(bf16[32,512]{1,0:T(8,128)(2,1)S(1)} %get-tuple-element.44), channel_id=1, source_target_pairs={{0,32},{8,40},{16,48},{24,56},{32,0},{40,8},{48,16},{56,24},{64,96... | collective-permute-start | bytes 98312 | tf_op jit(solution)/shard_map/ppermute | solution.py:49
  53.5 0.7 collective-permute-start.7
  54.2 3.0 %collective-permute-start.6 = (bf16[256,512]{1,0:T(8,128)(2,1)S(1)}, bf16[256,512]{1,0:T(8,128)(2,1)S(1)}, u32[]{:S(2)}, u32[]{:S(2)}) collective-permute-start(bf16[256,512]{1,0:T(8,128)(2,1)S(1)} %get-tuple-element.42), channel_id=1, source_target_pairs={{0,8},{8,0},{16,24},{24,16},{32,40},{40,32},{48,56},{56,48},{64,72... | collective-permute-start | bytes 786440 | tf_op jit(solution)/shard_map/ppermute | solution.py:49
  57.2 0.0 collective-permute-done.8.got_d
  57.2 2.3 %collective-permute-start.11 = (bf16[96,512]{1,0:T(8,128)(2,1)S(1)}, bf16[96,512]{1,0:T(8,128)(2,1)S(1)}, u32[]{:S(2)}, u32[]{:S(2)}) collective-permute-start(bf16[96,512]{1,0:T(8,128)(2,1)S(1)} %constant_dynamic-update-slice_fusion), channel_id=1, source_target_pairs={{0,24},{8,16},{16,8},{24,0},{32,56},{40,48},{48,40},{56,32},{64,88... | collective-permute-start | bytes 294920 | tf_op jit(solution)/shard_map/ppermute | solution.py:49
  59.5 1.4 %collective-permute-start.10 = (bf16[96,512]{1,0:T(8,128)(2,1)S(1)}, bf16[96,512]{1,0:T(8,128)(2,1)S(1)}, u32[]{:S(2)}, u32[]{:S(2)}) collective-permute-start(bf16[96,512]{1,0:T(8,128)(2,1)S(1)} %constant_dynamic-update-slice_fusion), channel_id=1, source_target_pairs={{0,16},{8,24},{16,0},{24,8},{32,48},{40,56},{48,32},{56,40},{64,80... | collective-permute-start | bytes 294920 | tf_op jit(solution)/shard_map/ppermute | solution.py:49
  60.9 0.1 pad_add_fusion.edge
  61.0 0.4 collective-permute-start.9
  61.4 2.7 %levels_1_2.1 = (bf16[2048,256]{1,0:T(8,128)(2,1)S(1)}, bf16[1024,256]{1,0:T(8,128)(2,1)S(1)}, f32[32,256]{1,0:T(8,128)S(1)}) custom-call(bf16[2048,256]{1,0:T(8,128)(2,1)S(1)} %get-tuple-element.46.q1, bf16[2048,512]{1,0:T(8,128)(2,1)S(1)} %get-tuple-element.47.kv1, bf16[1024,256]{1,0:T(8,128)(2,1)S(1)} %get-tuple-element.48.q2, ...), custom_call_target="tpu_custom_call" | custom-call | flops 402653184 | bytes 9437184 | tf_op jit(solution)/shard_map/levels_1_2/pallas_call | solution.py:307
  64.0 0.9 %collective-permute-done.9.got_s = bf16[32,512]{1,0:T(8,128)(2,1)S(1)} collective-permute-done((bf16[32,512]{1,0:T(8,128)(2,1)S(1)}, bf16[32,512]{1,0:T(8,128)(2,1)S(1)}, u32[]{:S(2)}, u32[]{:S(2)}) %collective-permute-start.9) | collective-permute-done | bytes 32800 | tf_op jit(solution)/shard_map/ppermute | solution.py:49
  65.0 0.0 collective-permute-done.11.got_e
  65.0 2.0 %collective-permute-done.10.got_c = bf16[96,512]{1,0:T(8,128)(2,1)S(1)} collective-permute-done((bf16[96,512]{1,0:T(8,128)(2,1)S(1)}, bf16[96,512]{1,0:T(8,128)(2,1)S(1)}, u32[]{:S(2)}, u32[]{:S(2)}) %collective-permute-start.10) | collective-permute-done | bytes 98336 | tf_op jit(solution)/shard_map/ppermute | solution.py:49
  67.0 0.0 collective-permute-done.7.got_b
  67.0 0.0 collective-permute-done.6.got_a
  67.0 0.0 copy-start
  67.0 9.0 %merge_levels.1 = (bf16[4096,256]{1,0:T(8,128)(2,1)S(1)}, f32[32,128]{1,0:T(8,128)S(1)}) custom-call(s32[3]{0:T(128)S(1)} %pad_add_fusion.edge, bf16[512,256]{1,0:T(8,128)(2,1)S(1)} %get-tuple-element.35.q3, bf16[512,512]{1,0:T(8,128)(2,1)S(1)} %get-tuple-element.36.kv3, bf16[256,256]{1,0:T(8,128)(2,1)S(1)} %get-tuple-element.37.q4, ...), custom_call_target="tpu_custom_call" | custom-call | flops 2147483648 | bytes 18874368 | tf_op jit(solution)/shard_map/merge_levels/pallas_call | solution.py:496
  76.0 0.0 collective-permute-start.12
  76.0 1.2 %collective-permute-done.12 = f32[32,128]{1,0:T(8,128)S(1)} collective-permute-done((f32[32,128]{1,0:T(8,128)S(1)}, f32[32,128]{1,0:T(8,128)S(1)}, u32[]{:S(2)}, u32[]{:S(2)}) %collective-permute-start.12) | collective-permute-done | bytes 16416 | tf_op jit(solution)/shard_map/ppermute | solution.py:58
  77.2 3.2 %collective-permute-start.15 = (f32[32,128]{1,0:T(8,128)S(1)}, f32[32,128]{1,0:T(8,128)S(1)}, u32[]{:S(2)}, u32[]{:S(2)}) collective-permute-start(f32[32,128]{1,0:T(8,128)S(1)} %add.49.s0), channel_id=1, source_target_pairs={{0,4},{1,5},{2,6},{3,7},{4,0},{5,1},{6,2},{7,3},{8,12},{9,13},{10,... | collective-permute-start | bytes 49160 | tf_op jit(solution)/shard_map/ppermute | solution.py:58
  80.4 1.1 %collective-permute-start.14 = (f32[32,128]{1,0:T(8,128)S(1)}, f32[32,128]{1,0:T(8,128)S(1)}, u32[]{:S(2)}, u32[]{:S(2)}) collective-permute-start(f32[32,128]{1,0:T(8,128)S(1)} %add.49.s0), channel_id=1, source_target_pairs={{0,6},{1,7},{2,0},{3,1},{4,2},{5,3},{6,4},{7,5},{8,14},{9,15},{10,... | collective-permute-start | bytes 49160 | tf_op jit(solution)/shard_map/ppermute | solution.py:58
  81.4 1.0 %collective-permute-start.13 = (f32[32,128]{1,0:T(8,128)S(1)}, f32[32,128]{1,0:T(8,128)S(1)}, u32[]{:S(2)}, u32[]{:S(2)}) collective-permute-start(f32[32,128]{1,0:T(8,128)S(1)} %add.49.s0), channel_id=1, source_target_pairs={{0,2},{1,3},{2,4},{3,5},{4,6},{5,7},{6,0},{7,1},{8,10},{9,11},{10,... | collective-permute-start | bytes 49160 | tf_op jit(solution)/shard_map/ppermute | solution.py:58
  82.4 0.0 collective-permute-done.15.s3
  82.4 1.7 %collective-permute-done.14.s2 = f32[32,128]{1,0:T(8,128)S(1)} collective-permute-done((f32[32,128]{1,0:T(8,128)S(1)}, f32[32,128]{1,0:T(8,128)S(1)}, u32[]{:S(2)}, u32[]{:S(2)}) %collective-permute-start.14) | collective-permute-done | bytes 16416 | tf_op jit(solution)/shard_map/ppermute | solution.py:58
  84.1 2.3 %collective-permute-done.13.s1 = f32[32,128]{1,0:T(8,128)S(1)} collective-permute-done((f32[32,128]{1,0:T(8,128)S(1)}, f32[32,128]{1,0:T(8,128)S(1)}, u32[]{:S(2)}, u32[]{:S(2)}) %collective-permute-start.13) | collective-permute-done | bytes 16416 | tf_op jit(solution)/shard_map/ppermute | solution.py:58
  86.4 0.0 copy-done
  86.4 1.5 %norm.1 = bf16[4096,256]{1,0:T(8,128)(2,1)} custom-call(bf16[4096,256]{1,0:T(8,128)(2,1)S(1)} %get-tuple-element.55.rows, f32[32,128]{1,0:T(8,128)S(1)} %add.49.s0, f32[32,128]{1,0:T(8,128)S(1)} %collective-permute-done.13.s1, f32[32,128]{1,0:T(8,128)S(1)} %collective-permute-done.14.s2, f32[32,128]{1,0:T(8,128)S(1)} %collective-permute-done.15.s3, ...), custom_call_target="tpu_custom_call" | custom-call | tf_op jit(solution)/shard_map/norm/pallas_call | solution.py:526
  (3 shorter events, 0.0 us)
Async XLA Ops:
  1.6 7.8 %collective-permute-start.2 = (bf16[128,768]{1,0:T(8,128)(2,1)}, bf16[128,768]{1,0:T(8,128)(2,1)S(1)}, u32[]{:S(2)}, u32[]{:S(2)}) collective-permute-start(bf16[128,768]{1,0:T(8,128)(2,1)} %join_weights.1), channel_id=1, source_target_pairs={{0,16},{1,65},{2,18},{3,67},{4,20},{5,69},{6,22},{7,71},{8,24},{9,... | collective-permute-start | bytes 589832 | tf_op jit(solution)/shard_map/ppermute | solution.py:45
  5.6 7.0 %collective-permute-start.1 = (bf16[128,768]{1,0:T(8,128)(2,1)}, bf16[128,768]{1,0:T(8,128)(2,1)S(1)}, u32[]{:S(2)}, u32[]{:S(2)}) collective-permute-start(bf16[128,768]{1,0:T(8,128)(2,1)} %join_weights.1), channel_id=1, source_target_pairs={{0,24},{1,97},{2,26},{3,99},{4,28},{5,101},{6,30},{7,103},{8,0},{9... | collective-permute-start | bytes 589832 | tf_op jit(solution)/shard_map/ppermute | solution.py:45
  6.3 7.1 %collective-permute-start = (bf16[128,768]{1,0:T(8,128)(2,1)}, bf16[128,768]{1,0:T(8,128)(2,1)S(1)}, u32[]{:S(2)}, u32[]{:S(2)}) collective-permute-start(bf16[128,768]{1,0:T(8,128)(2,1)} %join_weights.1), channel_id=1, source_target_pairs={{0,8},{1,33},{2,10},{3,35},{4,12},{5,37},{6,14},{7,39},{8,16},{9,4... | collective-permute-start | bytes 589832 | tf_op jit(solution)/shard_map/ppermute | solution.py:45
  14.4 12.3 %collective-permute-start.4 = (bf16[4,128,768]{2,1,0:T(8,128)(2,1)S(1)}, bf16[4,128,768]{2,1,0:T(8,128)(2,1)S(1)}, u32[]{:S(2)}, u32[]{:S(2)}) collective-permute-start(bf16[4,128,768]{2,1,0:T(8,128)(2,1)S(1)} %pad_maximum_fusion.w0), channel_id=1, source_target_pairs={{0,96},{1,25},{2,98},{3,27},{4,100},{5,29},{6,102},{7,31},{8,104},... | collective-permute-start | bytes 2359304 | tf_op jit(solution)/shard_map/ppermute | solution.py:45
  17.2 13.2 %collective-permute-start.3 = (bf16[4,128,768]{2,1,0:T(8,128)(2,1)S(1)}, bf16[4,128,768]{2,1,0:T(8,128)(2,1)S(1)}, u32[]{:S(2)}, u32[]{:S(2)}) collective-permute-start(bf16[4,128,768]{2,1,0:T(8,128)(2,1)S(1)} %pad_maximum_fusion.w0), channel_id=1, source_target_pairs={{0,32},{1,9},{2,34},{3,11},{4,36},{5,13},{6,38},{7,15},{8,40},{9,1... | collective-permute-start | bytes 2359304 | tf_op jit(solution)/shard_map/ppermute | solution.py:45
  30.4 13.8 %collective-permute-start.5 = (bf16[4,128,768]{2,1,0:T(8,128)(2,1)S(1)}, bf16[4,128,768]{2,1,0:T(8,128)(2,1)S(1)}, u32[]{:S(2)}, u32[]{:S(2)}) collective-permute-start(bf16[4,128,768]{2,1,0:T(8,128)(2,1)S(1)} %pad_maximum_fusion.w0), channel_id=1, source_target_pairs={{0,64},{1,17},{2,66},{3,19},{4,68},{5,21},{6,70},{7,23},{8,72},{9,... | collective-permute-start | bytes 2359304 | tf_op jit(solution)/shard_map/ppermute | solution.py:45
  52.6 4.6 %collective-permute-start.8 = (bf16[32,512]{1,0:T(8,128)(2,1)S(1)}, bf16[32,512]{1,0:T(8,128)(2,1)S(1)}, u32[]{:S(2)}, u32[]{:S(2)}) collective-permute-start(bf16[32,512]{1,0:T(8,128)(2,1)S(1)} %get-tuple-element.44), channel_id=1, source_target_pairs={{0,32},{8,40},{16,48},{24,56},{32,0},{40,8},{48,16},{56,24},{64,96... | collective-permute-start | bytes 98312 | tf_op jit(solution)/shard_map/ppermute | solution.py:49
  53.5 13.4 %collective-permute-start.7 = (bf16[128,512]{1,0:T(8,128)(2,1)S(1)}, bf16[128,512]{1,0:T(8,128)(2,1)S(1)}, u32[]{:S(2)}, u32[]{:S(2)}) collective-permute-start(bf16[128,512]{1,0:T(8,128)(2,1)S(1)} %get-tuple-element.43), channel_id=1, source_target_pairs={{8,16},{24,32},{40,48},{56,64},{72,80},{88,96},{104,112},{16,8},{3... | collective-permute-start | bytes 393224 | tf_op jit(solution)/shard_map/ppermute | solution.py:54
  54.2 12.8 %collective-permute-start.6 = (bf16[256,512]{1,0:T(8,128)(2,1)S(1)}, bf16[256,512]{1,0:T(8,128)(2,1)S(1)}, u32[]{:S(2)}, u32[]{:S(2)}) collective-permute-start(bf16[256,512]{1,0:T(8,128)(2,1)S(1)} %get-tuple-element.42), channel_id=1, source_target_pairs={{0,8},{8,0},{16,24},{24,16},{32,40},{40,32},{48,56},{56,48},{64,72... | collective-permute-start | bytes 786440 | tf_op jit(solution)/shard_map/ppermute | solution.py:49
  57.2 7.8 %collective-permute-start.11 = (bf16[96,512]{1,0:T(8,128)(2,1)S(1)}, bf16[96,512]{1,0:T(8,128)(2,1)S(1)}, u32[]{:S(2)}, u32[]{:S(2)}) collective-permute-start(bf16[96,512]{1,0:T(8,128)(2,1)S(1)} %constant_dynamic-update-slice_fusion), channel_id=1, source_target_pairs={{0,24},{8,16},{16,8},{24,0},{32,56},{40,48},{48,40},{56,32},{64,88... | collective-permute-start | bytes 294920 | tf_op jit(solution)/shard_map/ppermute | solution.py:49
  59.5 7.5 %collective-permute-start.10 = (bf16[96,512]{1,0:T(8,128)(2,1)S(1)}, bf16[96,512]{1,0:T(8,128)(2,1)S(1)}, u32[]{:S(2)}, u32[]{:S(2)}) collective-permute-start(bf16[96,512]{1,0:T(8,128)(2,1)S(1)} %constant_dynamic-update-slice_fusion), channel_id=1, source_target_pairs={{0,16},{8,24},{16,0},{24,8},{32,48},{40,56},{48,32},{56,40},{64,80... | collective-permute-start | bytes 294920 | tf_op jit(solution)/shard_map/ppermute | solution.py:49
  61.0 4.0 %collective-permute-start.9 = (bf16[32,512]{1,0:T(8,128)(2,1)S(1)}, bf16[32,512]{1,0:T(8,128)(2,1)S(1)}, u32[]{:S(2)}, u32[]{:S(2)}) collective-permute-start(bf16[32,512]{1,0:T(8,128)(2,1)S(1)} %collective-permute-done.8.got_d), channel_id=1, source_target_pairs={{0,8},{8,0},{16,24},{24,16},{32,40},{40,32},{48,56},{56,48},{64,72... | collective-permute-start | bytes 98312 | tf_op jit(solution)/shard_map/ppermute | solution.py:49
  67.0 19.4 %copy-start = (f32[256]{0:T(256)S(1)}, f32[256]{0:T(256)}, u32[]{:S(2)}) copy-start(f32[256]{0:T(256)} %param.10) | copy-start | bytes 3076
  76.0 1.2 %collective-permute-start.12 = (f32[32,128]{1,0:T(8,128)S(1)}, f32[32,128]{1,0:T(8,128)S(1)}, u32[]{:S(2)}, u32[]{:S(2)}) collective-permute-start(f32[32,128]{1,0:T(8,128)S(1)} %get-tuple-element.56), channel_id=1, source_target_pairs={{0,1},{1,0},{2,3},{3,2},{4,5},{5,4},{6,7},{7,6},{8,9},{9,8},{10,11... | collective-permute-start | bytes 49160 | tf_op jit(solution)/shard_map/ppermute | solution.py:58
  77.2 5.2 %collective-permute-start.15 = (f32[32,128]{1,0:T(8,128)S(1)}, f32[32,128]{1,0:T(8,128)S(1)}, u32[]{:S(2)}, u32[]{:S(2)}) collective-permute-start(f32[32,128]{1,0:T(8,128)S(1)} %add.49.s0), channel_id=1, source_target_pairs={{0,4},{1,5},{2,6},{3,7},{4,0},{5,1},{6,2},{7,3},{8,12},{9,13},{10,... | collective-permute-start | bytes 49160 | tf_op jit(solution)/shard_map/ppermute | solution.py:58
  80.4 3.7 %collective-permute-start.14 = (f32[32,128]{1,0:T(8,128)S(1)}, f32[32,128]{1,0:T(8,128)S(1)}, u32[]{:S(2)}, u32[]{:S(2)}) collective-permute-start(f32[32,128]{1,0:T(8,128)S(1)} %add.49.s0), channel_id=1, source_target_pairs={{0,6},{1,7},{2,0},{3,1},{4,2},{5,3},{6,4},{7,5},{8,14},{9,15},{10,... | collective-permute-start | bytes 49160 | tf_op jit(solution)/shard_map/ppermute | solution.py:58
  81.4 4.9 %collective-permute-start.13 = (f32[32,128]{1,0:T(8,128)S(1)}, f32[32,128]{1,0:T(8,128)S(1)}, u32[]{:S(2)}, u32[]{:S(2)}) collective-permute-start(f32[32,128]{1,0:T(8,128)S(1)} %add.49.s0), channel_id=1, source_target_pairs={{0,2},{1,3},{2,4},{3,5},{4,6},{5,7},{6,0},{7,1},{8,10},{9,11},{10,... | collective-permute-start | bytes 49160 | tf_op jit(solution)/shard_map/ppermute | solution.py:58

commit v4 on v3

--- a/solution.py
+++ b/solution.py
@@ -19,12 +19,12 @@
 BF = jnp.bfloat16
 F32 = jnp.float32
 TM = 1024
-CHUNK = 512
+CHUNK = 1024
 CHUNKS = TOKENS // CHUNK
 RUNS = TOKENS // TM
 VMEM_LIMIT = 32 * 2**20
-EARLY_LIMIT = 32 * 2**20
-LATE_LIMIT = 32 * 2**20
+EARLY_LIMIT = 28 * 2**20
+LATE_LIMIT = 20 * 2**20
 GROUP = 8
 
 
@@ -157,25 +157,38 @@
     ]
 
 
-def early_kernel(place, hidden, w0, w1, w2, sums, ring, w_half, h_sem):
+def early_kernel(place, hidden, w0, w1, w2, sums, rest, ring, w_half, h_sem, rest_sem):
     for index in range(2):
         start_all(half_rows(place, 0, hidden, ring, h_sem, index))
     join_half((w0, w1, w2), w_half)
+    columns = [
+        pltpu.make_async_copy(
+            hidden.at[:, pl.ds(pl.multiple_of(place[12 + block] * 128, 128), 128)],
+            rest.at[:, pl.ds(block * 128, 128)],
+            rest_sem.at[block],
+        )
+        for block in range(SIDE)
+    ]
 
     @pl.loop(0, CHUNKS)
     def _(index):
         next_half(place, 0, hidden, ring, h_sem, index)
+
+        @pl.when(index == CHUNKS - 2)
+        def _():
+            start_all(columns)
+
         at = pl.ds(pl.multiple_of(index * CHUNK, CHUNK), CHUNK)
         sums[at, :] = dot(ring[index % 3], w_half[...]).astype(BF)
 
+    wait_all(columns)
+
 
 def late_kernel(
-    place, hidden, w3, sums,
+    place, rest, w3, sums,
     kv, kv1, kv2, kv3, kv4, q, q1, q2, q3, q4, q5, q6, q7, send_a, send_b, six, seven,
-    ring, w_half, l3, h_sem,
+    w_half, l3,
 ):
-    for index in range(2):
-        start_all(half_rows(place, 12, hidden, ring, h_sem, index))
     join_half((w3,), w_half)
     p_fine = pool_matrix(112, 128, (1, 2, 3))
 
@@ -197,9 +210,8 @@
             l3[at3, :] = means[96:112]
 
     def project(index):
-        next_half(place, 12, hidden, ring, h_sem, index)
         at = pl.ds(pl.multiple_of(index * CHUNK, CHUNK), CHUNK)
-        rows = (dot(ring[index % 3], w_half[...]) + sums[at, :].astype(F32)).astype(BF)
+        rows = (dot(rest[at, :], w_half[...]) + sums[at, :].astype(F32)).astype(BF)
         return at, rows
 
     at, rows = project(jnp.int32(0))
@@ -237,12 +249,13 @@
     return pl.pallas_call(
         early_kernel,
         in_specs=[pl.BlockSpec(memory_space=pltpu.SMEM), anywhere] + [local] * 3,
-        out_specs=local,
-        out_shape=jax.ShapeDtypeStruct((TOKENS, 768), BF),
+        out_specs=[local, local],
+        out_shape=[jax.ShapeDtypeStruct((TOKENS, 768), BF), jax.ShapeDtypeStruct((TOKENS, 512), BF)],
         scratch_shapes=[
             pltpu.VMEM((3, CHUNK, 1536), BF),
             pltpu.VMEM((1536, 768), BF),
             pltpu.SemaphoreType.DMA((3, 12)),
+            pltpu.SemaphoreType.DMA((SIDE,)),
         ],
         compiler_params=pltpu.CompilerParams(vmem_limit_bytes=EARLY_LIMIT),
         name="project_early",
@@ -252,29 +265,26 @@
     )(place, hidden, *pieces)
 
 
-def project_late(place, hidden, pieces, sums):
-    anywhere = pl.BlockSpec(memory_space=pl.ANY)
+def project_late(place, rest, pieces, sums):
     local = pl.BlockSpec(memory_space=pltpu.VMEM)
     sizes = [(TOKENS >> level, 512) for level in range(5)]
     sizes += [(TOKENS >> level, 256) for level in range(8)]
     sizes += [(256, 512), (128, 512), (64, 512), (32, 512)]
     return pl.pallas_call(
         late_kernel,
-        in_specs=[pl.BlockSpec(memory_space=pltpu.SMEM), anywhere] + [local] * 2,
+        in_specs=[pl.BlockSpec(memory_space=pltpu.SMEM)] + [local] * 3,
         out_specs=[local] * len(sizes),
         out_shape=[jax.ShapeDtypeStruct(size, BF) for size in sizes],
         scratch_shapes=[
-            pltpu.VMEM((3, CHUNK, 512), BF),
             pltpu.VMEM((512, 768), BF),
             pltpu.VMEM((512, 768), BF),
-            pltpu.SemaphoreType.DMA((3, 4)),
         ],
         compiler_params=pltpu.CompilerParams(vmem_limit_bytes=LATE_LIMIT),
         name="project_late",
         cost_estimate=pl.CostEstimate(
             flops=TOKENS * 1024 * 768, bytes_accessed=8 * 2**20, transcendentals=0
         ),
-    )(place, hidden, *pieces, sums)
+    )(place, rest, *pieces, sums)
 
 
 def pairs_kernel(q1, kv1, q2, kv2, o1, o2, virtual):
@@ -565,9 +575,9 @@
     near_z = jnp.where(core == 0, (z - back[None, :]) % SIDE, (z - back[:, None]) % SIDE)
     place = jnp.concatenate([(near_x * SIDE + near_z).reshape(16), (position % 2).reshape(1)])
     place = place.astype(jnp.int32)
-    sums = project_early(place, hidden_states, pieces[:3])
+    sums, rest = project_early(place, hidden_states, pieces[:3])
     kv, kv1, kv2, kv3, kv4, q, q1, q2, q3, q4, q5, q6, q7, send_a, send_b, send_6, send_7 = project_late(
-        place, hidden_states, pieces[3:], sums
+        place, rest, pieces[3:], sums
     )
     got_d = flipped(send_7, 4)
     got_a = flipped(send_a, 1)

time: 88.1 us -> 85.9 us (0.975)
  Pallas kernels: 36.9 us -> 34.5 us
    pallas_call x1, Pallas kernels: 8.35 us -> 6.44 us  [project_late(): pl.pallas_call(late_kernel, in_specs=[pl.BlockSpec(memory_space=pltpu.SME...]
  transfers between devices with their start and end apart: 16 -> 16, of which waited for: 10 -> 11; matrix products, arithmetic and copies ran while one was open for 1% -> 1% of each run, Pallas kernels for 19% -> 19%
where the time goes in v4:
time: 85.9 us; the launch traced here: 85.7 us
  Pallas kernels  34.5 us (40%)
  waiting for transfers between devices  26.1 us (30%)
  starting transfers between devices  22.8 us (27%)
  other arithmetic  1.92 us (2%)
    ppermute x6, waiting for transfers between devices, along_line(): return lax.ppermute(value, ('seq', 'head'), line_perm(first, shift))  18.2 us
    pallas_call x1, Pallas kernels, project_early(): pl.pallas_call(early_kernel, in_specs=[pl.BlockSpec(memory_space=pltpu.SM...  13.3 us
    pallas_call x1, Pallas kernels, fine(): pl.pallas_call(fine_kernel, in_specs=[pl.BlockSpec(memory_space=pltpu.SME...  8.97 us
    ppermute x6, starting transfers between devices, along_line(): return lax.ppermute(value, ('seq', 'head'), line_perm(first, shift))  8.82 us
    ppermute x5, starting transfers between devices, flipped(): return lax.ppermute(value, 'seq', [(i, i ^ bits) for i in range(16)])  8.07 us
    pallas_call x1, Pallas kernels, project_late(): pl.pallas_call(late_kernel, in_specs=[pl.BlockSpec(memory_space=pltpu.SME...  6.44 us
    ppermute x4, starting transfers between devices, over_heads(): return lax.ppermute(value, 'head', [(i, step(i)) for i in range(8)])  5.24 us
    ppermute x4, waiting for transfers between devices, over_heads(): return lax.ppermute(value, 'head', [(i, step(i)) for i in range(8)])  5.15 us
  transfers between devices with their start and end apart: 16, of which 11 were waited for; matrix products, arithmetic and copies ran while one was open for 1% of the time, Pallas kernels for 19%

profile of v4, /device:TPU:0, one launch (start us, length us, event | category | flops | bytes accessed | tf_op | source)
XLA Modules:
  0.0 85.7 jit_solution(12297357161852066649)
XLA Ops:
  0.0 1.6 %join_weights.1 = bf16[128,768]{1,0:T(8,128)(2,1)} custom-call(bf16[128,256]{1,0:T(8,128)(2,1)} %a.1, bf16[128,256]{1,0:T(8,128)(2,1)} %b.1, bf16[128,256]{1,0:T(8,128)(2,1)} %c.1), custom_call_target="tpu_custom_call" | custom-call | tf_op jit(solution)/shard_map/join_weights/pallas_call | solution.py:555
  1.6 4.0 %collective-permute-start.2 = (bf16[128,768]{1,0:T(8,128)(2,1)}, bf16[128,768]{1,0:T(8,128)(2,1)S(1)}, u32[]{:S(2)}, u32[]{:S(2)}) collective-permute-start(bf16[128,768]{1,0:T(8,128)(2,1)} %join_weights.1), channel_id=1, source_target_pairs={{0,16},{1,65},{2,18},{3,67},{4,20},{5,69},{6,22},{7,71},{8,24},{9,... | collective-permute-start | bytes 589832 | tf_op jit(solution)/shard_map/ppermute | solution.py:45
  5.6 0.7 collective-permute-start.1
  6.3 1.3 %collective-permute-start = (bf16[128,768]{1,0:T(8,128)(2,1)}, bf16[128,768]{1,0:T(8,128)(2,1)S(1)}, u32[]{:S(2)}, u32[]{:S(2)}) collective-permute-start(bf16[128,768]{1,0:T(8,128)(2,1)} %join_weights.1), channel_id=1, source_target_pairs={{0,8},{1,33},{2,10},{3,35},{4,12},{5,37},{6,14},{7,39},{8,16},{9,4... | collective-permute-start | bytes 589832 | tf_op jit(solution)/shard_map/ppermute | solution.py:45
  7.6 1.8 %collective-permute-done.2 = bf16[128,768]{1,0:T(8,128)(2,1)S(1)} collective-permute-done((bf16[128,768]{1,0:T(8,128)(2,1)}, bf16[128,768]{1,0:T(8,128)(2,1)S(1)}, u32[]{:S(2)}, u32[]{:S(2)}) %collective-permute-start.2) | collective-permute-done | bytes 196640 | tf_op jit(solution)/shard_map/ppermute | solution.py:45
  9.4 3.2 %collective-permute-done.1 = bf16[128,768]{1,0:T(8,128)(2,1)S(1)} collective-permute-done((bf16[128,768]{1,0:T(8,128)(2,1)}, bf16[128,768]{1,0:T(8,128)(2,1)S(1)}, u32[]{:S(2)}, u32[]{:S(2)}) %collective-permute-start.1) | collective-permute-done | bytes 196640 | tf_op jit(solution)/shard_map/ppermute | solution.py:45
  12.6 0.8 collective-permute-done
  13.4 1.0 %pad_maximum_fusion.w0 = bf16[4,128,768]{2,1,0:T(8,128)(2,1)S(1)} fusion(bf16[1,128,768]{2,1,0:T(8,128)(2,1)S(1)} %bitcast.10, bf16[1,128,768]{2,1,0:T(8,128)(2,1)S(1)} %bitcast.11, bf16[1,128,768]{2,1,0:T(8,128)(2,1)S(1)} %bitcast.12, bf16[1,128,768]{2,1,0:T(8,128)(2,1)} %bitcast.9), kind=kLoop, calls=%fused_computation | loop fusion | flops 1179648 | bytes 1572864 | tf_op jit(solution)/shard_map/stack | solution.py:569
  14.4 2.8 %collective-permute-start.4 = (bf16[4,128,768]{2,1,0:T(8,128)(2,1)S(1)}, bf16[4,128,768]{2,1,0:T(8,128)(2,1)S(1)}, u32[]{:S(2)}, u32[]{:S(2)}) collective-permute-start(bf16[4,128,768]{2,1,0:T(8,128)(2,1)S(1)} %pad_maximum_fusion.w0), channel_id=1, source_target_pairs={{0,96},{1,25},{2,98},{3,27},{4,100},{5,29},{6,102},{7,31},{8,104},... | collective-permute-start | bytes 2359304 | tf_op jit(solution)/shard_map/ppermute | solution.py:45
  17.2 0.0 collective-permute-start.3
  17.2 0.7 and_select_fusion.1
  17.9 0.1 select_add_fusion
  18.0 0.1 add.48
  18.0 0.1 pad_add_fusion.1.place
  18.1 8.6 %collective-permute-done.4.w2 = bf16[4,128,768]{2,1,0:T(8,128)(2,1)S(1)} collective-permute-done((bf16[4,128,768]{2,1,0:T(8,128)(2,1)S(1)}, bf16[4,128,768]{2,1,0:T(8,128)(2,1)S(1)}, u32[]{:S(2)}, u32[]{:S(2)}) %collective-permute-start.4) | collective-permute-done | bytes 786464 | tf_op jit(solution)/shard_map/ppermute | solution.py:45
  26.7 3.7 %collective-permute-done.3.w1 = bf16[4,128,768]{2,1,0:T(8,128)(2,1)S(1)} collective-permute-done((bf16[4,128,768]{2,1,0:T(8,128)(2,1)S(1)}, bf16[4,128,768]{2,1,0:T(8,128)(2,1)S(1)}, u32[]{:S(2)}, u32[]{:S(2)}) %collective-permute-start.3) | collective-permute-done | bytes 786464 | tf_op jit(solution)/shard_map/ppermute | solution.py:45
  30.4 0.0 collective-permute-start.5
  30.4 13.3 %project_early.1 = (bf16[4096,768]{1,0:T(8,128)(2,1)S(1)}, bf16[4096,512]{1,0:T(8,128)(2,1)S(1)}) custom-call(s32[17]{0:T(128)S(1)} %pad_add_fusion.1.place, bf16[4096,2048]{1,0:T(8,128)(2,1)} %hidden.1, bf16[4,128,768]{2,1,0:T(8,128)(2,1)S(1)} %pad_maximum_fusion.w0, bf16[4,128,768]{2,1,0:T(8,128)(2,1)S(1)} %collective-permute-done.3.w1, ...), custom_call_target="tpu_custom_call" | custom-call | flops 9663676416 | bytes 12582912 | tf_op jit(solution)/shard_map/project_early/pallas_call | solution.py:249
  43.8 0.1 collective-permute-done.5.w3
  43.9 6.4 %project_late.1 = (bf16[4096,512]{1,0:T(8,128)(2,1)S(1)}, bf16[2048,512]{1,0:T(8,128)(2,1)S(1)}, bf16[1024,512]{1,0:T(8,128)(2,1)S(1)}, bf16[512,512]{1,0:T(8,12...) custom-call(s32[17]{0:T(128)S(1)} %pad_add_fusion.1.place, ...), custom_call_target="tpu_custom_call" | custom-call | flops 3221225472 | bytes 8388608 | tf_op jit(solution)/shard_map/project_late/pallas_call | solution.py:273
  50.4 0.8 collective-permute-start.8
  51.2 0.7 collective-permute-start.7
  51.8 3.0 %collective-permute-start.6 = (bf16[256,512]{1,0:T(8,128)(2,1)S(1)}, bf16[256,512]{1,0:T(8,128)(2,1)S(1)}, u32[]{:S(2)}, u32[]{:S(2)}) collective-permute-start(bf16[256,512]{1,0:T(8,128)(2,1)S(1)} %get-tuple-element.46), channel_id=1, source_target_pairs={{0,8},{8,0},{16,24},{24,16},{32,40},{40,32},{48,56},{56,48},{64,72... | collective-permute-start | bytes 786440 | tf_op jit(solution)/shard_map/ppermute | solution.py:49
  54.8 0.0 collective-permute-done.8.got_d
  54.8 2.4 %collective-permute-start.11 = (bf16[96,512]{1,0:T(8,128)(2,1)S(1)}, bf16[96,512]{1,0:T(8,128)(2,1)S(1)}, u32[]{:S(2)}, u32[]{:S(2)}) collective-permute-start(bf16[96,512]{1,0:T(8,128)(2,1)S(1)} %constant_dynamic-update-slice_fusion), channel_id=1, source_target_pairs={{0,24},{8,16},{16,8},{24,0},{32,56},{40,48},{48,40},{56,32},{64,88... | collective-permute-start | bytes 294920 | tf_op jit(solution)/shard_map/ppermute | solution.py:49
  57.2 1.4 %collective-permute-start.10 = (bf16[96,512]{1,0:T(8,128)(2,1)S(1)}, bf16[96,512]{1,0:T(8,128)(2,1)S(1)}, u32[]{:S(2)}, u32[]{:S(2)}) collective-permute-start(bf16[96,512]{1,0:T(8,128)(2,1)S(1)} %constant_dynamic-update-slice_fusion), channel_id=1, source_target_pairs={{0,16},{8,24},{16,0},{24,8},{32,48},{40,56},{48,32},{56,40},{64,80... | collective-permute-start | bytes 294920 | tf_op jit(solution)/shard_map/ppermute | solution.py:49
  58.7 0.1 pad_add_fusion.edge
  58.8 0.4 collective-permute-start.9
  59.2 2.6 %levels_1_2.1 = (bf16[2048,256]{1,0:T(8,128)(2,1)S(1)}, bf16[1024,256]{1,0:T(8,128)(2,1)S(1)}, f32[32,256]{1,0:T(8,128)S(1)}) custom-call(bf16[2048,256]{1,0:T(8,128)(2,1)S(1)} %get-tuple-element.50.q1, bf16[2048,512]{1,0:T(8,128)(2,1)S(1)} %get-tuple-element.51.kv1, bf16[1024,256]{1,0:T(8,128)(2,1)S(1)} %get-tuple-element.52.q2, ...), custom_call_target="tpu_custom_call" | custom-call | flops 402653184 | bytes 9437184 | tf_op jit(solution)/shard_map/levels_1_2/pallas_call | solution.py:317
  61.8 1.0 %collective-permute-done.9.got_s = bf16[32,512]{1,0:T(8,128)(2,1)S(1)} collective-permute-done((bf16[32,512]{1,0:T(8,128)(2,1)S(1)}, bf16[32,512]{1,0:T(8,128)(2,1)S(1)}, u32[]{:S(2)}, u32[]{:S(2)}) %collective-permute-start.9) | collective-permute-done | bytes 32800 | tf_op jit(solution)/shard_map/ppermute | solution.py:49
  62.9 0.0 collective-permute-done.11.got_e
  62.9 1.7 %collective-permute-done.10.got_c = bf16[96,512]{1,0:T(8,128)(2,1)S(1)} collective-permute-done((bf16[96,512]{1,0:T(8,128)(2,1)S(1)}, bf16[96,512]{1,0:T(8,128)(2,1)S(1)}, u32[]{:S(2)}, u32[]{:S(2)}) %collective-permute-start.10) | collective-permute-done | bytes 98336 | tf_op jit(solution)/shard_map/ppermute | solution.py:49
  64.6 0.0 collective-permute-done.7.got_b
  64.6 0.0 collective-permute-done.6.got_a
  64.6 0.0 copy-start
  64.6 9.0 %merge_levels.1 = (bf16[4096,256]{1,0:T(8,128)(2,1)S(1)}, f32[32,128]{1,0:T(8,128)S(1)}) custom-call(s32[3]{0:T(128)S(1)} %pad_add_fusion.edge, bf16[512,256]{1,0:T(8,128)(2,1)S(1)} %get-tuple-element.39.q3, bf16[512,512]{1,0:T(8,128)(2,1)S(1)} %get-tuple-element.40.kv3, bf16[256,256]{1,0:T(8,128)(2,1)S(1)} %get-tuple-element.41.q4, ...), custom_call_target="tpu_custom_call" | custom-call | flops 2147483648 | bytes 18874368 | tf_op jit(solution)/shard_map/merge_levels/pallas_call | solution.py:506
  73.6 0.0 collective-permute-start.12
  73.6 1.2 %collective-permute-done.12 = f32[32,128]{1,0:T(8,128)S(1)} collective-permute-done((f32[32,128]{1,0:T(8,128)S(1)}, f32[32,128]{1,0:T(8,128)S(1)}, u32[]{:S(2)}, u32[]{:S(2)}) %collective-permute-start.12) | collective-permute-done | bytes 16416 | tf_op jit(solution)/shard_map/ppermute | solution.py:58
  74.8 3.2 %collective-permute-start.15 = (f32[32,128]{1,0:T(8,128)S(1)}, f32[32,128]{1,0:T(8,128)S(1)}, u32[]{:S(2)}, u32[]{:S(2)}) collective-permute-start(f32[32,128]{1,0:T(8,128)S(1)} %add.49.s0), channel_id=1, source_target_pairs={{0,4},{1,5},{2,6},{3,7},{4,0},{5,1},{6,2},{7,3},{8,12},{9,13},{10,... | collective-permute-start | bytes 49160 | tf_op jit(solution)/shard_map/ppermute | solution.py:58
  78.0 1.0 %collective-permute-start.14 = (f32[32,128]{1,0:T(8,128)S(1)}, f32[32,128]{1,0:T(8,128)S(1)}, u32[]{:S(2)}, u32[]{:S(2)}) collective-permute-start(f32[32,128]{1,0:T(8,128)S(1)} %add.49.s0), channel_id=1, source_target_pairs={{0,6},{1,7},{2,0},{3,1},{4,2},{5,3},{6,4},{7,5},{8,14},{9,15},{10,... | collective-permute-start | bytes 49160 | tf_op jit(solution)/shard_map/ppermute | solution.py:58
  79.0 1.0 %collective-permute-start.13 = (f32[32,128]{1,0:T(8,128)S(1)}, f32[32,128]{1,0:T(8,128)S(1)}, u32[]{:S(2)}, u32[]{:S(2)}) collective-permute-start(f32[32,128]{1,0:T(8,128)S(1)} %add.49.s0), channel_id=1, source_target_pairs={{0,2},{1,3},{2,4},{3,5},{4,6},{5,7},{6,0},{7,1},{8,10},{9,11},{10,... | collective-permute-start | bytes 49160 | tf_op jit(solution)/shard_map/ppermute | solution.py:58
  80.0 0.0 collective-permute-done.15.s3
  80.0 1.7 %collective-permute-done.14.s2 = f32[32,128]{1,0:T(8,128)S(1)} collective-permute-done((f32[32,128]{1,0:T(8,128)S(1)}, f32[32,128]{1,0:T(8,128)S(1)}, u32[]{:S(2)}, u32[]{:S(2)}) %collective-permute-start.14) | collective-permute-done | bytes 16416 | tf_op jit(solution)/shard_map/ppermute | solution.py:58
  81.7 2.2 %collective-permute-done.13.s1 = f32[32,128]{1,0:T(8,128)S(1)} collective-permute-done((f32[32,128]{1,0:T(8,128)S(1)}, f32[32,128]{1,0:T(8,128)S(1)}, u32[]{:S(2)}, u32[]{:S(2)}) %collective-permute-start.13) | collective-permute-done | bytes 16416 | tf_op jit(solution)/shard_map/ppermute | solution.py:58
  84.0 0.0 copy-done
  84.0 1.5 %norm.1 = bf16[4096,256]{1,0:T(8,128)(2,1)} custom-call(bf16[4096,256]{1,0:T(8,128)(2,1)S(1)} %get-tuple-element.59.rows, f32[32,128]{1,0:T(8,128)S(1)} %add.49.s0, f32[32,128]{1,0:T(8,128)S(1)} %collective-permute-done.13.s1, f32[32,128]{1,0:T(8,128)S(1)} %collective-permute-done.14.s2, f32[32,128]{1,0:T(8,128)S(1)} %collective-permute-done.15.s3, ...), custom_call_target="tpu_custom_call" | custom-call | tf_op jit(solution)/shard_map/norm/pallas_call | solution.py:536
  (3 shorter events, 0.0 us)
Async XLA Ops:
  1.6 7.8 %collective-permute-start.2 = (bf16[128,768]{1,0:T(8,128)(2,1)}, bf16[128,768]{1,0:T(8,128)(2,1)S(1)}, u32[]{:S(2)}, u32[]{:S(2)}) collective-permute-start(bf16[128,768]{1,0:T(8,128)(2,1)} %join_weights.1), channel_id=1, source_target_pairs={{0,16},{1,65},{2,18},{3,67},{4,20},{5,69},{6,22},{7,71},{8,24},{9,... | collective-permute-start | bytes 589832 | tf_op jit(solution)/shard_map/ppermute | solution.py:45
  5.6 7.0 %collective-permute-start.1 = (bf16[128,768]{1,0:T(8,128)(2,1)}, bf16[128,768]{1,0:T(8,128)(2,1)S(1)}, u32[]{:S(2)}, u32[]{:S(2)}) collective-permute-start(bf16[128,768]{1,0:T(8,128)(2,1)} %join_weights.1), channel_id=1, source_target_pairs={{0,24},{1,97},{2,26},{3,99},{4,28},{5,101},{6,30},{7,103},{8,0},{9... | collective-permute-start | bytes 589832 | tf_op jit(solution)/shard_map/ppermute | solution.py:45
  6.3 7.1 %collective-permute-start = (bf16[128,768]{1,0:T(8,128)(2,1)}, bf16[128,768]{1,0:T(8,128)(2,1)S(1)}, u32[]{:S(2)}, u32[]{:S(2)}) collective-permute-start(bf16[128,768]{1,0:T(8,128)(2,1)} %join_weights.1), channel_id=1, source_target_pairs={{0,8},{1,33},{2,10},{3,35},{4,12},{5,37},{6,14},{7,39},{8,16},{9,4... | collective-permute-start | bytes 589832 | tf_op jit(solution)/shard_map/ppermute | solution.py:45
  14.4 12.3 %collective-permute-start.4 = (bf16[4,128,768]{2,1,0:T(8,128)(2,1)S(1)}, bf16[4,128,768]{2,1,0:T(8,128)(2,1)S(1)}, u32[]{:S(2)}, u32[]{:S(2)}) collective-permute-start(bf16[4,128,768]{2,1,0:T(8,128)(2,1)S(1)} %pad_maximum_fusion.w0), channel_id=1, source_target_pairs={{0,96},{1,25},{2,98},{3,27},{4,100},{5,29},{6,102},{7,31},{8,104},... | collective-permute-start | bytes 2359304 | tf_op jit(solution)/shard_map/ppermute | solution.py:45
  17.2 13.2 %collective-permute-start.3 = (bf16[4,128,768]{2,1,0:T(8,128)(2,1)S(1)}, bf16[4,128,768]{2,1,0:T(8,128)(2,1)S(1)}, u32[]{:S(2)}, u32[]{:S(2)}) collective-permute-start(bf16[4,128,768]{2,1,0:T(8,128)(2,1)S(1)} %pad_maximum_fusion.w0), channel_id=1, source_target_pairs={{0,32},{1,9},{2,34},{3,11},{4,36},{5,13},{6,38},{7,15},{8,40},{9,1... | collective-permute-start | bytes 2359304 | tf_op jit(solution)/shard_map/ppermute | solution.py:45
  30.4 13.5 %collective-permute-start.5 = (bf16[4,128,768]{2,1,0:T(8,128)(2,1)S(1)}, bf16[4,128,768]{2,1,0:T(8,128)(2,1)S(1)}, u32[]{:S(2)}, u32[]{:S(2)}) collective-permute-start(bf16[4,128,768]{2,1,0:T(8,128)(2,1)S(1)} %pad_maximum_fusion.w0), channel_id=1, source_target_pairs={{0,64},{1,17},{2,66},{3,19},{4,68},{5,21},{6,70},{7,23},{8,72},{9,... | collective-permute-start | bytes 2359304 | tf_op jit(solution)/shard_map/ppermute | solution.py:45
  50.4 4.5 %collective-permute-start.8 = (bf16[32,512]{1,0:T(8,128)(2,1)S(1)}, bf16[32,512]{1,0:T(8,128)(2,1)S(1)}, u32[]{:S(2)}, u32[]{:S(2)}) collective-permute-start(bf16[32,512]{1,0:T(8,128)(2,1)S(1)} %get-tuple-element.48), channel_id=1, source_target_pairs={{0,32},{8,40},{16,48},{24,56},{32,0},{40,8},{48,16},{56,24},{64,96... | collective-permute-start | bytes 98312 | tf_op jit(solution)/shard_map/ppermute | solution.py:49
  51.2 13.4 %collective-permute-start.7 = (bf16[128,512]{1,0:T(8,128)(2,1)S(1)}, bf16[128,512]{1,0:T(8,128)(2,1)S(1)}, u32[]{:S(2)}, u32[]{:S(2)}) collective-permute-start(bf16[128,512]{1,0:T(8,128)(2,1)S(1)} %get-tuple-element.47), channel_id=1, source_target_pairs={{8,16},{24,32},{40,48},{56,64},{72,80},{88,96},{104,112},{16,8},{3... | collective-permute-start | bytes 393224 | tf_op jit(solution)/shard_map/ppermute | solution.py:54
  51.8 12.8 %collective-permute-start.6 = (bf16[256,512]{1,0:T(8,128)(2,1)S(1)}, bf16[256,512]{1,0:T(8,128)(2,1)S(1)}, u32[]{:S(2)}, u32[]{:S(2)}) collective-permute-start(bf16[256,512]{1,0:T(8,128)(2,1)S(1)} %get-tuple-element.46), channel_id=1, source_target_pairs={{0,8},{8,0},{16,24},{24,16},{32,40},{40,32},{48,56},{56,48},{64,72... | collective-permute-start | bytes 786440 | tf_op jit(solution)/shard_map/ppermute | solution.py:49
  54.8 8.1 %collective-permute-start.11 = (bf16[96,512]{1,0:T(8,128)(2,1)S(1)}, bf16[96,512]{1,0:T(8,128)(2,1)S(1)}, u32[]{:S(2)}, u32[]{:S(2)}) collective-permute-start(bf16[96,512]{1,0:T(8,128)(2,1)S(1)} %constant_dynamic-update-slice_fusion), channel_id=1, source_target_pairs={{0,24},{8,16},{16,8},{24,0},{32,56},{40,48},{48,40},{56,32},{64,88... | collective-permute-start | bytes 294920 | tf_op jit(solution)/shard_map/ppermute | solution.py:49
  57.2 7.4 %collective-permute-start.10 = (bf16[96,512]{1,0:T(8,128)(2,1)S(1)}, bf16[96,512]{1,0:T(8,128)(2,1)S(1)}, u32[]{:S(2)}, u32[]{:S(2)}) collective-permute-start(bf16[96,512]{1,0:T(8,128)(2,1)S(1)} %constant_dynamic-update-slice_fusion), channel_id=1, source_target_pairs={{0,16},{8,24},{16,0},{24,8},{32,48},{40,56},{48,32},{56,40},{64,80... | collective-permute-start | bytes 294920 | tf_op jit(solution)/shard_map/ppermute | solution.py:49
  58.8 4.1 %collective-permute-start.9 = (bf16[32,512]{1,0:T(8,128)(2,1)S(1)}, bf16[32,512]{1,0:T(8,128)(2,1)S(1)}, u32[]{:S(2)}, u32[]{:S(2)}) collective-permute-start(bf16[32,512]{1,0:T(8,128)(2,1)S(1)} %collective-permute-done.8.got_d), channel_id=1, source_target_pairs={{0,8},{8,0},{16,24},{24,16},{32,40},{40,32},{48,56},{56,48},{64,72... | collective-permute-start | bytes 98312 | tf_op jit(solution)/shard_map/ppermute | solution.py:49
  64.6 19.4 %copy-start = (f32[256]{0:T(256)S(1)}, f32[256]{0:T(256)}, u32[]{:S(2)}) copy-start(f32[256]{0:T(256)} %param.10) | copy-start | bytes 3076
  73.6 1.2 %collective-permute-start.12 = (f32[32,128]{1,0:T(8,128)S(1)}, f32[32,128]{1,0:T(8,128)S(1)}, u32[]{:S(2)}, u32[]{:S(2)}) collective-permute-start(f32[32,128]{1,0:T(8,128)S(1)} %get-tuple-element.60), channel_id=1, source_target_pairs={{0,1},{1,0},{2,3},{3,2},{4,5},{5,4},{6,7},{7,6},{8,9},{9,8},{10,11... | collective-permute-start | bytes 49160 | tf_op jit(solution)/shard_map/ppermute | solution.py:58
  74.8 5.2 %collective-permute-start.15 = (f32[32,128]{1,0:T(8,128)S(1)}, f32[32,128]{1,0:T(8,128)S(1)}, u32[]{:S(2)}, u32[]{:S(2)}) collective-permute-start(f32[32,128]{1,0:T(8,128)S(1)} %add.49.s0), channel_id=1, source_target_pairs={{0,4},{1,5},{2,6},{3,7},{4,0},{5,1},{6,2},{7,3},{8,12},{9,13},{10,... | collective-permute-start | bytes 49160 | tf_op jit(solution)/shard_map/ppermute | solution.py:58
  78.0 3.7 %collective-permute-start.14 = (f32[32,128]{1,0:T(8,128)S(1)}, f32[32,128]{1,0:T(8,128)S(1)}, u32[]{:S(2)}, u32[]{:S(2)}) collective-permute-start(f32[32,128]{1,0:T(8,128)S(1)} %add.49.s0), channel_id=1, source_target_pairs={{0,6},{1,7},{2,0},{3,1},{4,2},{5,3},{6,4},{7,5},{8,14},{9,15},{10,... | collective-permute-start | bytes 49160 | tf_op jit(solution)/shard_map/ppermute | solution.py:58
  79.0 4.9 %collective-permute-start.13 = (f32[32,128]{1,0:T(8,128)S(1)}, f32[32,128]{1,0:T(8,128)S(1)}, u32[]{:S(2)}, u32[]{:S(2)}) collective-permute-start(f32[32,128]{1,0:T(8,128)S(1)} %add.49.s0), channel_id=1, source_target_pairs={{0,2},{1,3},{2,4},{3,5},{4,6},{5,7},{6,0},{7,1},{8,10},{9,11},{10,... | collective-permute-start | bytes 49160 | tf_op jit(solution)/shard_map/ppermute | solution.py:58

commit v5 on v4

--- a/solution.py
+++ b/solution.py
@@ -157,9 +157,36 @@
     ]
 
 
-def early_kernel(place, hidden, w0, w1, w2, sums, rest, ring, w_half, h_sem, rest_sem):
-    for index in range(2):
-        start_all(half_rows(place, 0, hidden, ring, h_sem, index))
+def fetch_kernel(place, hidden, ready, first, sems):
+    copies = [
+        pltpu.make_async_copy(
+            hidden.at[pl.ds(0, CHUNK), pl.ds(pl.multiple_of(place[block] * 128, 128), 128)],
+            first.at[:, pl.ds(block * 128, 128)],
+            sems.at[block],
+        )
+        for block in range(12)
+    ]
+    start_all(copies)
+    wait_all(copies)
+
+
+def fetch(place, hidden, ready):
+    anywhere = pl.BlockSpec(memory_space=pl.ANY)
+    return pl.pallas_call(
+        fetch_kernel,
+        in_specs=[pl.BlockSpec(memory_space=pltpu.SMEM), anywhere, anywhere],
+        out_specs=pl.BlockSpec(memory_space=pltpu.VMEM),
+        out_shape=jax.ShapeDtypeStruct((CHUNK, 1536), BF),
+        scratch_shapes=[pltpu.SemaphoreType.DMA((12,))],
+        compiler_params=pltpu.CompilerParams(vmem_limit_bytes=8 * 2**20),
+        name="fetch_first",
+        cost_estimate=pl.CostEstimate(flops=0, bytes_accessed=3 * 2**20, transcendentals=0),
+    )(place, hidden, ready)
+
+
+def early_kernel(place, hidden, first, w0, w1, w2, sums, rest, ring, w_half, h_sem, rest_sem):
+    for index in range(1, 3):
+        start_all(half_rows(place, 0, hidden, ring, h_sem, jnp.int32(index)))
     join_half((w0, w1, w2), w_half)
     columns = [
         pltpu.make_async_copy(
@@ -170,7 +197,9 @@
         for block in range(SIDE)
     ]
 
-    @pl.loop(0, CHUNKS)
+    sums[:CHUNK, :] = dot(first[...], w_half[...]).astype(BF)
+
+    @pl.loop(1, CHUNKS)
     def _(index):
         next_half(place, 0, hidden, ring, h_sem, index)
 
@@ -243,12 +272,12 @@
     send_a[128:, :] = five[:, :512]
 
 
-def project_early(place, hidden, pieces):
+def project_early(place, hidden, first, pieces):
     anywhere = pl.BlockSpec(memory_space=pl.ANY)
     local = pl.BlockSpec(memory_space=pltpu.VMEM)
     return pl.pallas_call(
         early_kernel,
-        in_specs=[pl.BlockSpec(memory_space=pltpu.SMEM), anywhere] + [local] * 3,
+        in_specs=[pl.BlockSpec(memory_space=pltpu.SMEM), anywhere] + [local] * 4,
         out_specs=[local, local],
         out_shape=[jax.ShapeDtypeStruct((TOKENS, 768), BF), jax.ShapeDtypeStruct((TOKENS, 512), BF)],
         scratch_shapes=[
@@ -262,7 +291,7 @@
         cost_estimate=pl.CostEstimate(
             flops=3 * TOKENS * 1024 * 768, bytes_accessed=12 * 2**20, transcendentals=0
         ),
-    )(place, hidden, *pieces)
+    )(place, hidden, first, *pieces)
 
 
 def project_late(place, rest, pieces, sums):
@@ -568,14 +597,15 @@
     w_mine = joined(w_key, w_value, w_query)
     line = jnp.stack([w_mine] + [along_line(w_mine, True, s) for s in SHIFTS])
     pieces = [line] + [along_line(line, False, s) for s in SHIFTS[:2]]
-    *pieces, line = lax.optimization_barrier((*pieces, line))
-    pieces = [*pieces, along_line(line, False, SHIFTS[2])]
     back = jnp.array((0,) + SHIFTS, jnp.int32)
     near_x = jnp.where(core == 0, (x - back[:, None]) % SIDE, (x - back[None, :]) % SIDE)
     near_z = jnp.where(core == 0, (z - back[None, :]) % SIDE, (z - back[:, None]) % SIDE)
     place = jnp.concatenate([(near_x * SIDE + near_z).reshape(16), (position % 2).reshape(1)])
     place = place.astype(jnp.int32)
-    sums, rest = project_early(place, hidden_states, pieces[:3])
+    first = fetch(place, hidden_states, line)
+    near, ready, first = lax.optimization_barrier((pieces[2], line, first))
+    pieces = [line, pieces[1], near, along_line(ready, False, SHIFTS[2])]
+    sums, rest = project_early(place, hidden_states, first, pieces[:3])
     kv, kv1, kv2, kv3, kv4, q, q1, q2, q3, q4, q5, q6, q7, send_a, send_b, send_6, send_7 = project_late(
         place, rest, pieces[3:], sums
     )

time: 85.9 us -> 85.5 us (level)
  waiting for transfers between devices: 26.1 us -> 15.9 us
  local copies, waits for them, and re-layouts: 0.1 us -> 5.87 us
  starting transfers between devices: 22.8 us -> 25.6 us
  Pallas kernels: 34.5 us -> 35.6 us
    ppermute x6, waiting for transfers between devices: 18.2 us -> 8.01 us  [along_line(): return lax.ppermute(value, ('seq', 'head'), line_perm(first, shift))]
    unnamed x3 -> x5, local copies, waits for them, and re-layouts: 0.01 us -> 5.78 us
    ppermute x6, starting transfers between devices: 8.82 us -> 11.6 us  [along_line(): return lax.ppermute(value, ('seq', 'head'), line_perm(first, shift))]
    pallas_call x0 -> x1, Pallas kernels: none -> 1.54 us  [fetch(): pl.pallas_call(fetch_kernel, in_specs=[pl.BlockSpec(memory_space=pltpu.SM...]
  transfers between devices with their start and end apart: 16 -> 16, of which waited for: 11 -> 10; matrix products, arithmetic and copies ran while one was open for 1% -> 1% of each run, Pallas kernels for 19% -> 20%
where the time goes in v5:
time: 85.5 us; the launch traced here: 85.3 us
  Pallas kernels  35.6 us (42%)
  starting transfers between devices  25.6 us (30%)
  waiting for transfers between devices  15.9 us (19%)
  local copies, waits for them, and re-layouts  5.87 us (7%)
  other arithmetic  1.92 us (2%)
    pallas_call x1, Pallas kernels, project_early(): pl.pallas_call(early_kernel, in_specs=[pl.BlockSpec(memory_space=pltpu.SM...  12.9 us
    ppermute x6, starting transfers between devices, along_line(): return lax.ppermute(value, ('seq', 'head'), line_perm(first, shift))  11.6 us
    pallas_call x1, Pallas kernels, fine(): pl.pallas_call(fine_kernel, in_specs=[pl.BlockSpec(memory_space=pltpu.SME...  8.97 us
    ppermute x5, starting transfers between devices, flipped(): return lax.ppermute(value, 'seq', [(i, i ^ bits) for i in range(16)])  8.19 us
    ppermute x6, waiting for transfers between devices, along_line(): return lax.ppermute(value, ('seq', 'head'), line_perm(first, shift))  8.01 us
    pallas_call x1, Pallas kernels, project_late(): pl.pallas_call(late_kernel, in_specs=[pl.BlockSpec(memory_space=pltpu.SME...  6.46 us
    unnamed x5, local copies, waits for them, and re-layouts  5.78 us
    ppermute x4, starting transfers between devices, over_heads(): return lax.ppermute(value, 'head', [(i, step(i)) for i in range(8)])  5.22 us
  transfers between devices with their start and end apart: 16, of which 10 were waited for; matrix products, arithmetic and copies ran while one was open for 1% of the time, Pallas kernels for 20%

profile of v5, /device:TPU:0, one launch (start us, length us, event | category | flops | bytes accessed | tf_op | source)
XLA Modules:
  0.0 85.3 jit_solution(8603536541244485768)
XLA Ops:
  0.0 1.6 %join_weights.1 = bf16[128,768]{1,0:T(8,128)(2,1)} custom-call(bf16[128,256]{1,0:T(8,128)(2,1)} %a.1, bf16[128,256]{1,0:T(8,128)(2,1)} %b.1, bf16[128,256]{1,0:T(8,128)(2,1)} %c.1), custom_call_target="tpu_custom_call" | custom-call | tf_op jit(solution)/shard_map/join_weights/pallas_call | solution.py:584
  1.6 4.0 %collective-permute-start.2 = (bf16[128,768]{1,0:T(8,128)(2,1)}, bf16[128,768]{1,0:T(8,128)(2,1)S(1)}, u32[]{:S(2)}, u32[]{:S(2)}) collective-permute-start(bf16[128,768]{1,0:T(8,128)(2,1)} %join_weights.1), channel_id=1, source_target_pairs={{0,16},{1,65},{2,18},{3,67},{4,20},{5,69},{6,22},{7,71},{8,24},{9,... | collective-permute-start | bytes 589832 | tf_op jit(solution)/shard_map/ppermute | solution.py:45
  5.6 0.7 collective-permute-start.1
  6.3 1.3 %collective-permute-start = (bf16[128,768]{1,0:T(8,128)(2,1)}, bf16[128,768]{1,0:T(8,128)(2,1)S(1)}, u32[]{:S(2)}, u32[]{:S(2)}) collective-permute-start(bf16[128,768]{1,0:T(8,128)(2,1)} %join_weights.1), channel_id=1, source_target_pairs={{0,8},{1,33},{2,10},{3,35},{4,12},{5,37},{6,14},{7,39},{8,16},{9,4... | collective-permute-start | bytes 589832 | tf_op jit(solution)/shard_map/ppermute | solution.py:45
  7.6 1.8 %collective-permute-done.2 = bf16[128,768]{1,0:T(8,128)(2,1)S(1)} collective-permute-done((bf16[128,768]{1,0:T(8,128)(2,1)}, bf16[128,768]{1,0:T(8,128)(2,1)S(1)}, u32[]{:S(2)}, u32[]{:S(2)}) %collective-permute-start.2) | collective-permute-done | bytes 196640 | tf_op jit(solution)/shard_map/ppermute | solution.py:45
  9.4 3.2 %collective-permute-done.1 = bf16[128,768]{1,0:T(8,128)(2,1)S(1)} collective-permute-done((bf16[128,768]{1,0:T(8,128)(2,1)}, bf16[128,768]{1,0:T(8,128)(2,1)S(1)}, u32[]{:S(2)}, u32[]{:S(2)}) %collective-permute-start.1) | collective-permute-done | bytes 196640 | tf_op jit(solution)/shard_map/ppermute | solution.py:45
  12.6 0.8 collective-permute-done
  13.4 1.0 %pad_maximum_fusion.ready.w0 = bf16[4,128,768]{2,1,0:T(8,128)(2,1)S(1)} fusion(bf16[1,128,768]{2,1,0:T(8,128)(2,1)S(1)} %bitcast.10, bf16[1,128,768]{2,1,0:T(8,128)(2,1)S(1)} %bitcast.11, bf16[1,128,768]{2,1,0:T(8,128)(2,1)S(1)} %bitcast.12, bf16[1,128,768]{2,1,0:T(8,128)(2,1)} %bitcast.9), kind=kLoop, calls=%fused_computation | loop fusion | flops 1179648 | bytes 1572864 | tf_op jit(solution)/shard_map/stack | solution.py:598
  14.4 2.8 %collective-permute-start.3 = (bf16[4,128,768]{2,1,0:T(8,128)(2,1)S(1)}, bf16[4,128,768]{2,1,0:T(8,128)(2,1)S(1)}, u32[]{:S(2)}, u32[]{:S(2)}) collective-permute-start(bf16[4,128,768]{2,1,0:T(8,128)(2,1)S(1)} %pad_maximum_fusion.ready.w0), channel_id=1, source_target_pairs={{0,96},{1,25},{2,98},{3,27},{4,100},{5,29},{6,102},{7,31},{8,104},... | collective-permute-start | bytes 2359304 | tf_op jit(solution)/shard_map/ppermute | solution.py:45
  17.2 0.0 collective-permute-start.4
  17.2 0.7 and_select_fusion.1
  17.9 0.1 select_add_fusion
  18.0 0.1 add.48
  18.0 0.1 pad_add_fusion.1.place
  18.1 0.0 copy-start
  18.1 5.8 %copy-done = bf16[4096,2048]{1,0:T(8,128)(2,1)S(1)} copy-done((bf16[4096,2048]{1,0:T(8,128)(2,1)S(1)}, bf16[4096,2048]{1,0:T(8,128)(2,1)}, u32[]{:S(2)}) %copy-start) | copy-done | bytes 16777240
  23.9 1.5 %fetch_first.1.first = bf16[1024,1536]{1,0:T(8,128)(2,1)S(1)} custom-call(s32[17]{0:T(128)S(1)} %pad_add_fusion.1.place, bf16[4096,2048]{1,0:T(8,128)(2,1)S(1)} %copy-done, bf16[4,128,768]{2,1,0:T(8,128)(2,1)S(1)} %pad_maximum_fusion.ready.w0), custom_call_target="tpu_custom_call" | custom-call | bytes 3145728 | tf_op jit(solution)/shard_map/fetch_first/pallas_call | solution.py:175
  25.4 1.3 %collective-permute-done.3.w2 = bf16[4,128,768]{2,1,0:T(8,128)(2,1)S(1)} collective-permute-done((bf16[4,128,768]{2,1,0:T(8,128)(2,1)S(1)}, bf16[4,128,768]{2,1,0:T(8,128)(2,1)S(1)}, u32[]{:S(2)}, u32[]{:S(2)}) %collective-permute-start.3) | collective-permute-done | bytes 786464 | tf_op jit(solution)/shard_map/ppermute | solution.py:45
  26.7 2.7 %collective-permute-start.5 = (bf16[4,128,768]{2,1,0:T(8,128)(2,1)S(1)}, bf16[4,128,768]{2,1,0:T(8,128)(2,1)S(1)}, u32[]{:S(2)}, u32[]{:S(2)}) collective-permute-start(bf16[4,128,768]{2,1,0:T(8,128)(2,1)S(1)} %pad_maximum_fusion.ready.w0), channel_id=1, source_target_pairs={{0,64},{1,17},{2,66},{3,19},{4,68},{5,21},{6,70},{7,23},{8,72},{9,... | collective-permute-start | bytes 2359304 | tf_op jit(solution)/shard_map/ppermute | solution.py:45
  29.5 0.9 %collective-permute-done.4.w1 = bf16[4,128,768]{2,1,0:T(8,128)(2,1)S(1)} collective-permute-done((bf16[4,128,768]{2,1,0:T(8,128)(2,1)S(1)}, bf16[4,128,768]{2,1,0:T(8,128)(2,1)S(1)}, u32[]{:S(2)}, u32[]{:S(2)}) %collective-permute-start.4) | collective-permute-done | bytes 786464 | tf_op jit(solution)/shard_map/ppermute | solution.py:45
  30.4 12.9 %project_early.1 = (bf16[4096,768]{1,0:T(8,128)(2,1)S(1)}, bf16[4096,512]{1,0:T(8,128)(2,1)S(1)}) custom-call(s32[17]{0:T(128)S(1)} %pad_add_fusion.1.place, bf16[4096,2048]{1,0:T(8,128)(2,1)} %hidden.3, bf16[1024,1536]{1,0:T(8,128)(2,1)S(1)} %fetch_first.1.first, bf16[4,128,768]{2,1,0:T(8,128)(2,1)S(1)} %pad_maximum_fusion.ready.w0, ...), custom_call_target="tpu_custom_call" | custom-call | flops 9663676416 | bytes 12582912 | tf_op jit(solution)/shard_map/project_early/pallas_call | solution.py:278
  43.3 0.0 collective-permute-done.5.w3
  43.3 6.5 %project_late.1 = (bf16[4096,512]{1,0:T(8,128)(2,1)S(1)}, bf16[2048,512]{1,0:T(8,128)(2,1)S(1)}, bf16[1024,512]{1,0:T(8,128)(2,1)S(1)}, bf16[512,512]{1,0:T(8,12...) custom-call(s32[17]{0:T(128)S(1)} %pad_add_fusion.1.place, ...), custom_call_target="tpu_custom_call" | custom-call | flops 3221225472 | bytes 8388608 | tf_op jit(solution)/shard_map/project_late/pallas_call | solution.py:302
  49.8 0.9 %collective-permute-start.8 = (bf16[32,512]{1,0:T(8,128)(2,1)S(1)}, bf16[32,512]{1,0:T(8,128)(2,1)S(1)}, u32[]{:S(2)}, u32[]{:S(2)}) collective-permute-start(bf16[32,512]{1,0:T(8,128)(2,1)S(1)} %get-tuple-element.46), channel_id=1, source_target_pairs={{0,32},{8,40},{16,48},{24,56},{32,0},{40,8},{48,16},{56,24},{64,96... | collective-permute-start | bytes 98312 | tf_op jit(solution)/shard_map/ppermute | solution.py:49
  50.7 0.7 collective-permute-start.7
  51.4 3.0 %collective-permute-start.6 = (bf16[256,512]{1,0:T(8,128)(2,1)S(1)}, bf16[256,512]{1,0:T(8,128)(2,1)S(1)}, u32[]{:S(2)}, u32[]{:S(2)}) collective-permute-start(bf16[256,512]{1,0:T(8,128)(2,1)S(1)} %get-tuple-element.44), channel_id=1, source_target_pairs={{0,8},{8,0},{16,24},{24,16},{32,40},{40,32},{48,56},{56,48},{64,72... | collective-permute-start | bytes 786440 | tf_op jit(solution)/shard_map/ppermute | solution.py:49
  54.4 0.0 collective-permute-done.8.got_d
  54.4 2.3 %collective-permute-start.11 = (bf16[96,512]{1,0:T(8,128)(2,1)S(1)}, bf16[96,512]{1,0:T(8,128)(2,1)S(1)}, u32[]{:S(2)}, u32[]{:S(2)}) collective-permute-start(bf16[96,512]{1,0:T(8,128)(2,1)S(1)} %constant_dynamic-update-slice_fusion), channel_id=1, source_target_pairs={{0,24},{8,16},{16,8},{24,0},{32,56},{40,48},{48,40},{56,32},{64,88... | collective-permute-start | bytes 294920 | tf_op jit(solution)/shard_map/ppermute | solution.py:49
  56.7 1.4 %collective-permute-start.10 = (bf16[96,512]{1,0:T(8,128)(2,1)S(1)}, bf16[96,512]{1,0:T(8,128)(2,1)S(1)}, u32[]{:S(2)}, u32[]{:S(2)}) collective-permute-start(bf16[96,512]{1,0:T(8,128)(2,1)S(1)} %constant_dynamic-update-slice_fusion), channel_id=1, source_target_pairs={{0,16},{8,24},{16,0},{24,8},{32,48},{40,56},{48,32},{56,40},{64,80... | collective-permute-start | bytes 294920 | tf_op jit(solution)/shard_map/ppermute | solution.py:49
  58.1 0.1 pad_add_fusion.edge
  58.2 0.5 collective-permute-start.9
  58.7 2.7 %levels_1_2.1 = (bf16[2048,256]{1,0:T(8,128)(2,1)S(1)}, bf16[1024,256]{1,0:T(8,128)(2,1)S(1)}, f32[32,256]{1,0:T(8,128)S(1)}) custom-call(bf16[2048,256]{1,0:T(8,128)(2,1)S(1)} %get-tuple-element.48.q1, bf16[2048,512]{1,0:T(8,128)(2,1)S(1)} %get-tuple-element.49.kv1, bf16[1024,256]{1,0:T(8,128)(2,1)S(1)} %get-tuple-element.50.q2, ...), custom_call_target="tpu_custom_call" | custom-call | flops 402653184 | bytes 9437184 | tf_op jit(solution)/shard_map/levels_1_2/pallas_call | solution.py:346
  61.4 0.9 %collective-permute-done.9.got_s = bf16[32,512]{1,0:T(8,128)(2,1)S(1)} collective-permute-done((bf16[32,512]{1,0:T(8,128)(2,1)S(1)}, bf16[32,512]{1,0:T(8,128)(2,1)S(1)}, u32[]{:S(2)}, u32[]{:S(2)}) %collective-permute-start.9) | collective-permute-done | bytes 32800 | tf_op jit(solution)/shard_map/ppermute | solution.py:49
  62.3 0.0 collective-permute-done.11.got_e
  62.3 1.9 %collective-permute-done.10.got_c = bf16[96,512]{1,0:T(8,128)(2,1)S(1)} collective-permute-done((bf16[96,512]{1,0:T(8,128)(2,1)S(1)}, bf16[96,512]{1,0:T(8,128)(2,1)S(1)}, u32[]{:S(2)}, u32[]{:S(2)}) %collective-permute-start.10) | collective-permute-done | bytes 98336 | tf_op jit(solution)/shard_map/ppermute | solution.py:49
  64.2 0.0 collective-permute-done.7.got_b
  64.2 0.0 collective-permute-done.6.got_a
  64.2 0.0 copy-start.1
  64.2 9.0 %merge_levels.1 = (bf16[4096,256]{1,0:T(8,128)(2,1)S(1)}, f32[32,128]{1,0:T(8,128)S(1)}) custom-call(s32[3]{0:T(128)S(1)} %pad_add_fusion.edge, bf16[512,256]{1,0:T(8,128)(2,1)S(1)} %get-tuple-element.37.q3, bf16[512,512]{1,0:T(8,128)(2,1)S(1)} %get-tuple-element.38.kv3, bf16[256,256]{1,0:T(8,128)(2,1)S(1)} %get-tuple-element.39.q4, ...), custom_call_target="tpu_custom_call" | custom-call | flops 2147483648 | bytes 18874368 | tf_op jit(solution)/shard_map/merge_levels/pallas_call | solution.py:535
  73.2 0.0 collective-permute-start.12
  73.2 1.2 %collective-permute-done.12 = f32[32,128]{1,0:T(8,128)S(1)} collective-permute-done((f32[32,128]{1,0:T(8,128)S(1)}, f32[32,128]{1,0:T(8,128)S(1)}, u32[]{:S(2)}, u32[]{:S(2)}) %collective-permute-start.12) | collective-permute-done | bytes 16416 | tf_op jit(solution)/shard_map/ppermute | solution.py:58
  74.4 3.2 %collective-permute-start.15 = (f32[32,128]{1,0:T(8,128)S(1)}, f32[32,128]{1,0:T(8,128)S(1)}, u32[]{:S(2)}, u32[]{:S(2)}) collective-permute-start(f32[32,128]{1,0:T(8,128)S(1)} %add.49.s0), channel_id=1, source_target_pairs={{0,4},{1,5},{2,6},{3,7},{4,0},{5,1},{6,2},{7,3},{8,12},{9,13},{10,... | collective-permute-start | bytes 49160 | tf_op jit(solution)/shard_map/ppermute | solution.py:58
  77.6 1.1 %collective-permute-start.14 = (f32[32,128]{1,0:T(8,128)S(1)}, f32[32,128]{1,0:T(8,128)S(1)}, u32[]{:S(2)}, u32[]{:S(2)}) collective-permute-start(f32[32,128]{1,0:T(8,128)S(1)} %add.49.s0), channel_id=1, source_target_pairs={{0,6},{1,7},{2,0},{3,1},{4,2},{5,3},{6,4},{7,5},{8,14},{9,15},{10,... | collective-permute-start | bytes 49160 | tf_op jit(solution)/shard_map/ppermute | solution.py:58
  78.6 1.0 %collective-permute-start.13 = (f32[32,128]{1,0:T(8,128)S(1)}, f32[32,128]{1,0:T(8,128)S(1)}, u32[]{:S(2)}, u32[]{:S(2)}) collective-permute-start(f32[32,128]{1,0:T(8,128)S(1)} %add.49.s0), channel_id=1, source_target_pairs={{0,2},{1,3},{2,4},{3,5},{4,6},{5,7},{6,0},{7,1},{8,10},{9,11},{10,... | collective-permute-start | bytes 49160 | tf_op jit(solution)/shard_map/ppermute | solution.py:58
  79.6 0.0 collective-permute-done.15.s3
  79.6 1.7 %collective-permute-done.14.s2 = f32[32,128]{1,0:T(8,128)S(1)} collective-permute-done((f32[32,128]{1,0:T(8,128)S(1)}, f32[32,128]{1,0:T(8,128)S(1)}, u32[]{:S(2)}, u32[]{:S(2)}) %collective-permute-start.14) | collective-permute-done | bytes 16416 | tf_op jit(solution)/shard_map/ppermute | solution.py:58
  81.3 2.3 %collective-permute-done.13.s1 = f32[32,128]{1,0:T(8,128)S(1)} collective-permute-done((f32[32,128]{1,0:T(8,128)S(1)}, f32[32,128]{1,0:T(8,128)S(1)}, u32[]{:S(2)}, u32[]{:S(2)}) %collective-permute-start.13) | collective-permute-done | bytes 16416 | tf_op jit(solution)/shard_map/ppermute | solution.py:58
  83.6 0.0 copy-done.1
  83.6 1.5 %norm.1 = bf16[4096,256]{1,0:T(8,128)(2,1)} custom-call(bf16[4096,256]{1,0:T(8,128)(2,1)S(1)} %get-tuple-element.57.rows, f32[32,128]{1,0:T(8,128)S(1)} %add.49.s0, f32[32,128]{1,0:T(8,128)S(1)} %collective-permute-done.13.s1, f32[32,128]{1,0:T(8,128)S(1)} %collective-permute-done.14.s2, f32[32,128]{1,0:T(8,128)S(1)} %collective-permute-done.15.s3, ...), custom_call_target="tpu_custom_call" | custom-call | tf_op jit(solution)/shard_map/norm/pallas_call | solution.py:565
  (3 shorter events, 0.0 us)
Async XLA Ops:
  1.6 7.8 %collective-permute-start.2 = (bf16[128,768]{1,0:T(8,128)(2,1)}, bf16[128,768]{1,0:T(8,128)(2,1)S(1)}, u32[]{:S(2)}, u32[]{:S(2)}) collective-permute-start(bf16[128,768]{1,0:T(8,128)(2,1)} %join_weights.1), channel_id=1, source_target_pairs={{0,16},{1,65},{2,18},{3,67},{4,20},{5,69},{6,22},{7,71},{8,24},{9,... | collective-permute-start | bytes 589832 | tf_op jit(solution)/shard_map/ppermute | solution.py:45
  5.6 7.0 %collective-permute-start.1 = (bf16[128,768]{1,0:T(8,128)(2,1)}, bf16[128,768]{1,0:T(8,128)(2,1)S(1)}, u32[]{:S(2)}, u32[]{:S(2)}) collective-permute-start(bf16[128,768]{1,0:T(8,128)(2,1)} %join_weights.1), channel_id=1, source_target_pairs={{0,24},{1,97},{2,26},{3,99},{4,28},{5,101},{6,30},{7,103},{8,0},{9... | collective-permute-start | bytes 589832 | tf_op jit(solution)/shard_map/ppermute | solution.py:45
  6.3 7.1 %collective-permute-start = (bf16[128,768]{1,0:T(8,128)(2,1)}, bf16[128,768]{1,0:T(8,128)(2,1)S(1)}, u32[]{:S(2)}, u32[]{:S(2)}) collective-permute-start(bf16[128,768]{1,0:T(8,128)(2,1)} %join_weights.1), channel_id=1, source_target_pairs={{0,8},{1,33},{2,10},{3,35},{4,12},{5,37},{6,14},{7,39},{8,16},{9,4... | collective-permute-start | bytes 589832 | tf_op jit(solution)/shard_map/ppermute | solution.py:45
  14.4 12.3 %collective-permute-start.3 = (bf16[4,128,768]{2,1,0:T(8,128)(2,1)S(1)}, bf16[4,128,768]{2,1,0:T(8,128)(2,1)S(1)}, u32[]{:S(2)}, u32[]{:S(2)}) collective-permute-start(bf16[4,128,768]{2,1,0:T(8,128)(2,1)S(1)} %pad_maximum_fusion.ready.w0), channel_id=1, source_target_pairs={{0,96},{1,25},{2,98},{3,27},{4,100},{5,29},{6,102},{7,31},{8,104},... | collective-permute-start | bytes 2359304 | tf_op jit(solution)/shard_map/ppermute | solution.py:45
  17.2 13.2 %collective-permute-start.4 = (bf16[4,128,768]{2,1,0:T(8,128)(2,1)S(1)}, bf16[4,128,768]{2,1,0:T(8,128)(2,1)S(1)}, u32[]{:S(2)}, u32[]{:S(2)}) collective-permute-start(bf16[4,128,768]{2,1,0:T(8,128)(2,1)S(1)} %pad_maximum_fusion.ready.w0), channel_id=1, source_target_pairs={{0,32},{1,9},{2,34},{3,11},{4,36},{5,13},{6,38},{7,15},{8,40},{9,1... | collective-permute-start | bytes 2359304 | tf_op jit(solution)/shard_map/ppermute | solution.py:45
  18.1 5.8 %copy-start = (bf16[4096,2048]{1,0:T(8,128)(2,1)S(1)}, bf16[4096,2048]{1,0:T(8,128)(2,1)}, u32[]{:S(2)}) copy-start(bf16[4096,2048]{1,0:T(8,128)(2,1)} %hidden.3) | copy-start | bytes 50331652
  26.7 16.6 %collective-permute-start.5 = (bf16[4,128,768]{2,1,0:T(8,128)(2,1)S(1)}, bf16[4,128,768]{2,1,0:T(8,128)(2,1)S(1)}, u32[]{:S(2)}, u32[]{:S(2)}) collective-permute-start(bf16[4,128,768]{2,1,0:T(8,128)(2,1)S(1)} %pad_maximum_fusion.ready.w0), channel_id=1, source_target_pairs={{0,64},{1,17},{2,66},{3,19},{4,68},{5,21},{6,70},{7,23},{8,72},{9,... | collective-permute-start | bytes 2359304 | tf_op jit(solution)/shard_map/ppermute | solution.py:45
  49.8 4.6 %collective-permute-start.8 = (bf16[32,512]{1,0:T(8,128)(2,1)S(1)}, bf16[32,512]{1,0:T(8,128)(2,1)S(1)}, u32[]{:S(2)}, u32[]{:S(2)}) collective-permute-start(bf16[32,512]{1,0:T(8,128)(2,1)S(1)} %get-tuple-element.46), channel_id=1, source_target_pairs={{0,32},{8,40},{16,48},{24,56},{32,0},{40,8},{48,16},{56,24},{64,96... | collective-permute-start | bytes 98312 | tf_op jit(solution)/shard_map/ppermute | solution.py:49
  50.7 13.4 %collective-permute-start.7 = (bf16[128,512]{1,0:T(8,128)(2,1)S(1)}, bf16[128,512]{1,0:T(8,128)(2,1)S(1)}, u32[]{:S(2)}, u32[]{:S(2)}) collective-permute-start(bf16[128,512]{1,0:T(8,128)(2,1)S(1)} %get-tuple-element.45), channel_id=1, source_target_pairs={{8,16},{24,32},{40,48},{56,64},{72,80},{88,96},{104,112},{16,8},{3... | collective-permute-start | bytes 393224 | tf_op jit(solution)/shard_map/ppermute | solution.py:54
  51.4 12.8 %collective-permute-start.6 = (bf16[256,512]{1,0:T(8,128)(2,1)S(1)}, bf16[256,512]{1,0:T(8,128)(2,1)S(1)}, u32[]{:S(2)}, u32[]{:S(2)}) collective-permute-start(bf16[256,512]{1,0:T(8,128)(2,1)S(1)} %get-tuple-element.44), channel_id=1, source_target_pairs={{0,8},{8,0},{16,24},{24,16},{32,40},{40,32},{48,56},{56,48},{64,72... | collective-permute-start | bytes 786440 | tf_op jit(solution)/shard_map/ppermute | solution.py:49
  54.4 7.9 %collective-permute-start.11 = (bf16[96,512]{1,0:T(8,128)(2,1)S(1)}, bf16[96,512]{1,0:T(8,128)(2,1)S(1)}, u32[]{:S(2)}, u32[]{:S(2)}) collective-permute-start(bf16[96,512]{1,0:T(8,128)(2,1)S(1)} %constant_dynamic-update-slice_fusion), channel_id=1, source_target_pairs={{0,24},{8,16},{16,8},{24,0},{32,56},{40,48},{48,40},{56,32},{64,88... | collective-permute-start | bytes 294920 | tf_op jit(solution)/shard_map/ppermute | solution.py:49
  56.7 7.5 %collective-permute-start.10 = (bf16[96,512]{1,0:T(8,128)(2,1)S(1)}, bf16[96,512]{1,0:T(8,128)(2,1)S(1)}, u32[]{:S(2)}, u32[]{:S(2)}) collective-permute-start(bf16[96,512]{1,0:T(8,128)(2,1)S(1)} %constant_dynamic-update-slice_fusion), channel_id=1, source_target_pairs={{0,16},{8,24},{16,0},{24,8},{32,48},{40,56},{48,32},{56,40},{64,80... | collective-permute-start | bytes 294920 | tf_op jit(solution)/shard_map/ppermute | solution.py:49
  58.2 4.1 %collective-permute-start.9 = (bf16[32,512]{1,0:T(8,128)(2,1)S(1)}, bf16[32,512]{1,0:T(8,128)(2,1)S(1)}, u32[]{:S(2)}, u32[]{:S(2)}) collective-permute-start(bf16[32,512]{1,0:T(8,128)(2,1)S(1)} %collective-permute-done.8.got_d), channel_id=1, source_target_pairs={{0,8},{8,0},{16,24},{24,16},{32,40},{40,32},{48,56},{56,48},{64,72... | collective-permute-start | bytes 98312 | tf_op jit(solution)/shard_map/ppermute | solution.py:49
  64.2 19.4 %copy-start.1 = (f32[256]{0:T(256)S(1)}, f32[256]{0:T(256)}, u32[]{:S(2)}) copy-start(f32[256]{0:T(256)} %param.10) | copy-start | bytes 3076
  73.2 1.2 %collective-permute-start.12 = (f32[32,128]{1,0:T(8,128)S(1)}, f32[32,128]{1,0:T(8,128)S(1)}, u32[]{:S(2)}, u32[]{:S(2)}) collective-permute-start(f32[32,128]{1,0:T(8,128)S(1)} %get-tuple-element.58), channel_id=1, source_target_pairs={{0,1},{1,0},{2,3},{3,2},{4,5},{5,4},{6,7},{7,6},{8,9},{9,8},{10,11... | collective-permute-start | bytes 49160 | tf_op jit(solution)/shard_map/ppermute | solution.py:58
  74.4 5.2 %collective-permute-start.15 = (f32[32,128]{1,0:T(8,128)S(1)}, f32[32,128]{1,0:T(8,128)S(1)}, u32[]{:S(2)}, u32[]{:S(2)}) collective-permute-start(f32[32,128]{1,0:T(8,128)S(1)} %add.49.s0), channel_id=1, source_target_pairs={{0,4},{1,5},{2,6},{3,7},{4,0},{5,1},{6,2},{7,3},{8,12},{9,13},{10,... | collective-permute-start | bytes 49160 | tf_op jit(solution)/shard_map/ppermute | solution.py:58
  77.6 3.7 %collective-permute-start.14 = (f32[32,128]{1,0:T(8,128)S(1)}, f32[32,128]{1,0:T(8,128)S(1)}, u32[]{:S(2)}, u32[]{:S(2)}) collective-permute-start(f32[32,128]{1,0:T(8,128)S(1)} %add.49.s0), channel_id=1, source_target_pairs={{0,6},{1,7},{2,0},{3,1},{4,2},{5,3},{6,4},{7,5},{8,14},{9,15},{10,... | collective-permute-start | bytes 49160 | tf_op jit(solution)/shard_map/ppermute | solution.py:58
  78.6 4.9 %collective-permute-start.13 = (f32[32,128]{1,0:T(8,128)S(1)}, f32[32,128]{1,0:T(8,128)S(1)}, u32[]{:S(2)}, u32[]{:S(2)}) collective-permute-start(f32[32,128]{1,0:T(8,128)S(1)} %add.49.s0), channel_id=1, source_target_pairs={{0,2},{1,3},{2,4},{3,5},{4,6},{5,7},{6,0},{7,1},{8,10},{9,11},{10,... | collective-permute-start | bytes 49160 | tf_op jit(solution)/shard_map/ppermute | solution.py:58
